TPU v7x, 32 devices: a whole 2x2x4 slice. The times are simulated.
32 devices in a mesh: row: 4 (over y, x), col: 8 (over z, core).
Axes of the slice: x: 2, y: 2, z: 4, core: 2. Of those that a mesh axis runs over, the one named last changes fastest.
Arguments:
- field: float32 [2, 1024, 4096], P(None, 'row', 'col'), may hold values from -4 to 4
- states: float32 [16, 64, 512], P('row', 'col'), may hold values from -1 to 1
- input_weight: bfloat16 [20736, 512], P('col'), may hold values from -0.0390625 to 0.0390625
- recurrent_weight: bfloat16 [512, 512], replicated, may hold values from -0.25 to 0.25
- bias: float32 [512], replicated, may hold values from -3 to 3
- output_weight: bfloat16 [512, 8192], P(None, 'col'), may hold values from -0.25 to 0.25
- model_gain: float32 [2, 64, 64], replicated, may hold values from 0.5 to 1.5
Outputs:
- prediction: float32 [2, 1024, 4096], P(None, 'row', 'col')
- fresh_states: float32 [16, 64, 512], P('row', 'col')
All inputs are finite; a program needn't handle non-finite values.
Results may differ from a plain program's by a relative error of at most 0.0033.
Values may be sent and summed in bfloat16 or wider, within the bound.
No kernel may reach another device: no remote copies, remote signals or barrier semaphores. Data moves between devices by JAX's collectives and lax.ppermute only.
A program may use at most 64 MiB of HBM per device.

v0:
```python
import jax
import jax.numpy as jnp
from jax import lax
from jax.sharding import PartitionSpec as P

CORE = 64
MARGIN = 4
NODES = 512
PATCH = 72


dispersion = 2.0
nonlinear = -0.7
time_step = 0.1


def extended(cells, sides, width):
    for axis, dim in sides:
        count = lax.axis_size(axis)
        head = lax.slice_in_dim(cells, 0, width, axis=dim)
        tail = lax.slice_in_dim(cells, cells.shape[dim] - width, cells.shape[dim], axis=dim)
        cells = jnp.concatenate(
            [
                lax.ppermute(tail, axis, [(i, (i + 1) % count) for i in range(count)]),
                cells,
                lax.ppermute(head, axis, [((i + 1) % count, i) for i in range(count)]),
            ],
            axis=dim,
        )
    return cells


def reaction(center, spread):
    real_part = center[0]
    imag_part = center[1]
    modulus = real_part * real_part + imag_part * imag_part
    first = (
        real_part
        + spread[0]
        - dispersion * spread[1]
        - modulus * (real_part - nonlinear * imag_part)
    )
    second = (
        imag_part
        + spread[1]
        + dispersion * spread[0]
        - modulus * (imag_part + nonlinear * real_part)
    )
    return jnp.stack([first, second])


def shrunk_tendency(padded):
    center = padded[:, 1:-1, 1:-1]
    spread = (
        padded[:, :-2, 1:-1]
        + padded[:, 2:, 1:-1]
        + padded[:, 1:-1, :-2]
        + padded[:, 1:-1, 2:]
        - 4.0 * center
    )
    return reaction(center, spread)


def section_slope(values):
    padded = extended(values, (("row", 1), ("col", 2)), 1)
    return shrunk_tendency(padded)


def local(field, states, input_weight, recurrent_weight, bias, output_weight, model_gain):
    height = field.shape[1]
    width = field.shape[2]
    slope_one = section_slope(field)
    slope_two = section_slope(field + 0.5 * time_step * slope_one)
    slope_three = section_slope(field + 0.5 * time_step * slope_two)
    slope_four = section_slope(field + time_step * slope_three)
    model = field + time_step / 6.0 * (slope_one + 2.0 * slope_two + 2.0 * slope_three + slope_four)
    both = extended(
        jnp.concatenate([field, model], 0).astype(jnp.bfloat16), (("row", 1), ("col", 2)), MARGIN
    ).astype(jnp.float32)
    block_rows = height // CORE
    block_cols = width // CORE
    count = block_rows * block_cols
    pieces = [
        both[
            :,
            row_index * CORE : row_index * CORE + PATCH,
            col_index * CORE : col_index * CORE + PATCH,
        ]
        for row_index in range(block_rows)
        for col_index in range(block_cols)
    ]
    inputs = jnp.stack(pieces).reshape(count, -1).astype(jnp.bfloat16)
    previous = states.reshape(count, NODES).astype(jnp.bfloat16)
    recur = jnp.dot(previous, recurrent_weight, preferred_element_type=jnp.float32)
    drive = jnp.dot(
        inputs,
        lax.all_gather(input_weight, "col", axis=0, tiled=True),
        preferred_element_type=jnp.float32,
    )
    fresh = jnp.tanh(drive + recur + bias)
    readin = fresh.astype(jnp.bfloat16)
    products = jnp.dot(
        lax.all_gather(readin, "col", axis=0, tiled=True),
        output_weight,
        preferred_element_type=jnp.float32,
    )
    readout = lax.all_to_all(products, "col", split_axis=0, concat_axis=1, tiled=True)
    placed = (
        readout.reshape(block_rows, block_cols, 2, CORE, CORE)
        .transpose(2, 0, 3, 1, 4)
        .reshape(2, height, width)
    )
    gained = (
        model.reshape(2, block_rows, CORE, block_cols, CORE) * model_gain[:, None, :, None, :]
    ).reshape(2, height, width)
    prediction = gained + placed
    return (prediction, fresh.reshape(block_rows, block_cols, NODES))


def solution(mesh):
    placed = (
        P(None, "row", "col"),
        P("row", "col", None),
        P("col", None),
        P(),
        P(),
        P(None, "col"),
        P(),
    )
    return jax.shard_map(
        local,
        mesh=mesh,
        in_specs=placed,
        out_specs=(P(None, "row", "col"), P("row", "col", None)),
        check_vma=False,
    )
```

profile of v0, /device:TPU:1, one launch (start us, length us, event | category | flops | bytes accessed | tf_op | source)
XLA Modules:
  0.0 298.6 jit_solution(4917274448269599713)
XLA Ops:
  13.5 3.0 %collective-permute-start.2 = (f32[2,258,1]{2,1,0:T(8,128)S(1)}, f32[2,258,1]{2,1,0:T(8,128)S(1)}, u32[]{:S(2)}, u32[]{:S(2)}) collective-permute-start(f32[2,258,1]{2,1,0:T(8,128)S(1)} %get-tuple-element.39), channel_id=1, source_target_pairs={{0,1},{1,2},{2,3},{3,4},{4,5},{5,6},{6,7},{7,0},{8,9},{9,10},{10,1... | collective-permute-start | bytes 6200 | tf_op jit(solution)/shard_map/ppermute | solution.py:24
  16.5 3.7 %collective-permute-done.2 = f32[2,258,1]{2,1,0:T(8,128)S(1)} collective-permute-done((f32[2,258,1]{2,1,0:T(8,128)S(1)}, f32[2,258,1]{2,1,0:T(8,128)S(1)}, u32[]{:S(2)}, u32[]{:S(2)}) %collective-permute-start.2) | collective-permute-done | bytes 2096 | tf_op jit(solution)/shard_map/ppermute | solution.py:24
  20.2 6.7 %collective-permute-done.3 = f32[2,258,1]{2,1,0:T(8,128)S(1)} collective-permute-done((f32[2,258,1]{2,1,0:T(8,128)S(1)}, f32[2,258,1]{2,1,0:T(8,128)S(1)}, u32[]{:S(2)}, u32[]{:S(2)}) %collective-permute-start.3) | collective-permute-done | bytes 2096 | tf_op jit(solution)/shard_map/ppermute | solution.py:26
  28.2 4.1 %collective-permute-start.4 = (f32[2,1,512]{2,1,0:T(1,128)S(1)}, f32[2,1,512]{2,1,0:T(1,128)S(1)}, u32[]{:S(2)}, u32[]{:S(2)}) collective-permute-start(f32[2,1,512]{2,1,0:T(1,128)S(1)} %get-tuple-element.62), channel_id=1, source_target_pairs={{0,8},{8,16},{16,24},{24,0},{1,9},{9,17},{17,25},{25,1},{2,10},{10... | collective-permute-start | bytes 12296 | tf_op jit(solution)/shard_map/ppermute | solution.py:24
  33.1 2.1 collective-permute-done.5
  35.9 11.9 %collective-permute-done.6 = f32[2,258,1]{2,1,0:T(8,128)S(1)} collective-permute-done((f32[2,258,1]{2,1,0:T(8,128)S(1)}, f32[2,258,1]{2,1,0:T(8,128)S(1)}, u32[]{:S(2)}, u32[]{:S(2)}) %collective-permute-start.6) | collective-permute-done | bytes 2096 | tf_op jit(solution)/shard_map/ppermute | solution.py:24
  47.8 9.5 %collective-permute-done.7 = f32[2,258,1]{2,1,0:T(8,128)S(1)} collective-permute-done((f32[2,258,1]{2,1,0:T(8,128)S(1)}, f32[2,258,1]{2,1,0:T(8,128)S(1)}, u32[]{:S(2)}, u32[]{:S(2)}) %collective-permute-start.7) | collective-permute-done | bytes 2096 | tf_op jit(solution)/shard_map/ppermute | solution.py:26
  63.1 11.3 %collective-permute-done.10 = f32[2,258,1]{2,1,0:T(8,128)S(1)} collective-permute-done((f32[2,258,1]{2,1,0:T(8,128)S(1)}, f32[2,258,1]{2,1,0:T(8,128)S(1)}, u32[]{:S(2)}, u32[]{:S(2)}) %collective-permute-start.10) | collective-permute-done | bytes 2096 | tf_op jit(solution)/shard_map/ppermute | solution.py:24
  74.4 15.7 %collective-permute-done.11 = f32[2,258,1]{2,1,0:T(8,128)S(1)} collective-permute-done((f32[2,258,1]{2,1,0:T(8,128)S(1)}, f32[2,258,1]{2,1,0:T(8,128)S(1)}, u32[]{:S(2)}, u32[]{:S(2)}) %collective-permute-start.11) | collective-permute-done | bytes 2096 | tf_op jit(solution)/shard_map/ppermute | solution.py:26
  91.4 2.4 collective-permute-start.13
  96.1 11.1 %collective-permute-done.14 = f32[2,258,1]{2,1,0:T(8,128)S(1)} collective-permute-done((f32[2,258,1]{2,1,0:T(8,128)S(1)}, f32[2,258,1]{2,1,0:T(8,128)S(1)}, u32[]{:S(2)}, u32[]{:S(2)}) %collective-permute-start.14) | collective-permute-done | bytes 2096 | tf_op jit(solution)/shard_map/ppermute | solution.py:24
  107.3 10.0 %collective-permute-done.15 = f32[2,258,1]{2,1,0:T(8,128)S(1)} collective-permute-done((f32[2,258,1]{2,1,0:T(8,128)S(1)}, f32[2,258,1]{2,1,0:T(8,128)S(1)}, u32[]{:S(2)}, u32[]{:S(2)}) %collective-permute-start.15) | collective-permute-done | bytes 2096 | tf_op jit(solution)/shard_map/ppermute | solution.py:26
  119.8 2.5 collective-permute-start.17
  139.2 16.7 %collective-permute-done.19 = bf16[4,264,4]{2,1,0:T(8,128)(2,1)S(1)} collective-permute-done((bf16[4,264,4]{2,1,0:T(8,128)(2,1)}, bf16[4,264,4]{2,1,0:T(8,128)(2,1)S(1)}, u32[]{:S(2)}, u32[]{:S(2)}) %collective-permute-start.19) | collective-permute-done | bytes 8480 | tf_op jit(solution)/shard_map/ppermute | solution.py:26
  164.3 9.3 %stack.155 = bf16[32,20736]{1,0:T(8,128)(2,1)S(1)} concatenate(bf16[1,20736]{1,0:T(2,128)(2,1)S(1)} %stack.123, bf16[1,20736]{1,0:T(2,128)(2,1)} %stack.124, bf16[1,20736]{1,0:T(2,128)(2,1)S(1)} %stack.125, bf16[1,20736]{1,0:T(2,128)(2,1)S(1)} %stack.126, bf16[1,20736]{1,0:T(2,128)(2,1)S(1)} %stack.127, bf16[1,20736]{1,0:T(2,128)(2,1)} %stack.128, bf16[1,20736]{1,0:T(2,128)(2,1)} %stack.129, ...), dimensions={0} | concatenate | bytes 2654208 | tf_op jit(solution)/shard_map/stack | solution.py:92
  173.6 49.1 %all-gather.2.cloned.1.call-done = bf16[20736,512]{1,0:T(8,128)(2,1)} async-done(((bf16[2592,512]{1,0:T(8,128)(2,1)}), bf16[20736,512]{1,0:T(8,128)(2,1)}) %all-gather.2.cloned.1.call-update) | async-done | bytes 21233680 | tf_op jit(solution)/shard_map/all_gather | solution.py:97
  222.7 9.6 %fusion.30 = (bf16[32,512]{1,0:T(8,128)(2,1)S(1)}, f32[32,512]{1,0:T(8,128)}) fusion(f32[512]{0:T(512)S(1)} %copy-done.7, f32[32,512]{1,0:T(8,128)S(1)} %fusion.20, bf16[32,20736]{1,0:T(8,128)(2,1)S(1)} %stack.155, bf16[20736,512]{1,0:T(8,128)(2,1)} %all-gather.2.cloned.1.call-done), kind=kOutput, calls=%fused_computation.140 | convolution fusion | flops 679526400 | bytes 22726656 | tf_op jit(solution)/shard_map/dot_general | solution.py:95
  232.3 14.3 %all_gather.7 = bf16[256,512]{1,0:T(8,128)(2,1)S(1)} all-gather(bf16[32,512]{1,0:T(8,128)(2,1)S(1)} %get-tuple-element.66), channel_id=1, replica_groups=mesh['row'=4,'col'=8] {'col'}, dimensions={0}, use_global_device_ids=true | all-gather | bytes 294912 | tf_op jit(solution)/shard_map/all_gather | solution.py:103
  248.0 3.7 %all-to-all-start = ((f32[8,32,1024]{2,1,0:T(8,128)}), f32[8,32,1024]{2,1,0:T(8,128)S(1)}, u32[]{:S(2)}, u32[]{:S(2)}) async-start(f32[8,32,1024]{2,1,0:T(8,128)} %bitcast.18), calls=%async_computation | async-start | bytes 2097152 | tf_op jit(solution)/shard_map/all_to_all | solution.py:107
  253.2 2.7 mul.228
  255.9 21.4 %all-to-all-done = f32[8,32,1024]{2,1,0:T(8,128)S(1)} async-done(((f32[8,32,1024]{2,1,0:T(8,128)}), f32[8,32,1024]{2,1,0:T(8,128)S(1)}, u32[]{:S(2)}, u32[]{:S(2)}) %all-to-all-start) | async-done | bytes 1048608 | tf_op jit(solution)/shard_map/all_to_all | solution.py:107
  282.1 4.1 %copy.13 = f32[2,4,64,8,64]{4,3,2,1,0:T(8,128)} copy(f32[2,4,64,8,64]{4,2,0,3,1:T(8,128)} %bitcast.16) | data formatting | bytes 2097152 | tf_op jit(solution)/shard_map/transpose | solution.py:110
  286.1 2.8 reshape.122
  288.9 2.9 multiply_add_fusion
  (109 shorter events, 53.7 us)
Async XLA Ops:
  7.2 239.4 %copy-start = (bf16[512,1024]{1,0:T(8,128)(2,1)S(1)}, bf16[512,1024]{1,0:T(8,128)(2,1)}, u32[]{:S(2)}) copy-start(bf16[512,1024]{1,0:T(8,128)(2,1)} %param.12) | copy-start | bytes 3145732
  7.2 215.5 %all-gather.2.cloned.1.call-start = ((), (), s32[]{:S(2)}) async-start(), calls=%async_computation.1 | async-start | bytes 23887872 | tf_op jit(solution)/shard_map/all_gather | solution.py:97
  8.5 4.0 %collective-permute-start = (f32[2,1,512]{2,1,0:T(1,128)S(1)}, f32[2,1,512]{2,1,0:T(1,128)S(1)}, u32[]{:S(2)}, u32[]{:S(2)}) collective-permute-start(f32[2,1,512]{2,1,0:T(1,128)S(1)} %get-tuple-element.64), channel_id=1, source_target_pairs={{0,8},{8,16},{16,24},{24,0},{1,9},{9,17},{17,25},{25,1},{2,10},{10... | collective-permute-start | bytes 12296 | tf_op jit(solution)/shard_map/ppermute | solution.py:24
  10.6 2.8 collective-permute-start.1
  13.5 6.7 %collective-permute-start.2 = (f32[2,258,1]{2,1,0:T(8,128)S(1)}, f32[2,258,1]{2,1,0:T(8,128)S(1)}, u32[]{:S(2)}, u32[]{:S(2)}) collective-permute-start(f32[2,258,1]{2,1,0:T(8,128)S(1)} %get-tuple-element.39), channel_id=1, source_target_pairs={{0,1},{1,2},{2,3},{3,4},{4,5},{5,6},{6,7},{7,0},{8,9},{9,10},{10,1... | collective-permute-start | bytes 6200 | tf_op jit(solution)/shard_map/ppermute | solution.py:24
  16.5 10.4 %collective-permute-start.3 = (f32[2,258,1]{2,1,0:T(8,128)S(1)}, f32[2,258,1]{2,1,0:T(8,128)S(1)}, u32[]{:S(2)}, u32[]{:S(2)}) collective-permute-start(f32[2,258,1]{2,1,0:T(8,128)S(1)} %get-tuple-element.40), channel_id=1, source_target_pairs={{1,0},{2,1},{3,2},{4,3},{5,4},{6,5},{7,6},{0,7},{9,8},{10,9},{11,1... | collective-permute-start | bytes 6200 | tf_op jit(solution)/shard_map/ppermute | solution.py:26
  28.2 4.9 %collective-permute-start.4 = (f32[2,1,512]{2,1,0:T(1,128)S(1)}, f32[2,1,512]{2,1,0:T(1,128)S(1)}, u32[]{:S(2)}, u32[]{:S(2)}) collective-permute-start(f32[2,1,512]{2,1,0:T(1,128)S(1)} %get-tuple-element.62), channel_id=1, source_target_pairs={{0,8},{8,16},{16,24},{24,0},{1,9},{9,17},{17,25},{25,1},{2,10},{10... | collective-permute-start | bytes 12296 | tf_op jit(solution)/shard_map/ppermute | solution.py:24
  32.3 2.9 collective-permute-start.5
  35.3 12.5 %collective-permute-start.6 = (f32[2,258,1]{2,1,0:T(8,128)S(1)}, f32[2,258,1]{2,1,0:T(8,128)S(1)}, u32[]{:S(2)}, u32[]{:S(2)}) collective-permute-start(f32[2,258,1]{2,1,0:T(8,128)S(1)} %get-tuple-element.37), channel_id=1, source_target_pairs={{0,1},{1,2},{2,3},{3,4},{4,5},{5,6},{6,7},{7,0},{8,9},{9,10},{10,1... | collective-permute-start | bytes 6200 | tf_op jit(solution)/shard_map/ppermute | solution.py:24
  35.9 21.4 %collective-permute-start.7 = (f32[2,258,1]{2,1,0:T(8,128)S(1)}, f32[2,258,1]{2,1,0:T(8,128)S(1)}, u32[]{:S(2)}, u32[]{:S(2)}) collective-permute-start(f32[2,258,1]{2,1,0:T(8,128)S(1)} %get-tuple-element.38), channel_id=1, source_target_pairs={{1,0},{2,1},{3,2},{4,3},{5,4},{6,5},{7,6},{0,7},{9,8},{10,9},{11,1... | collective-permute-start | bytes 6200 | tf_op jit(solution)/shard_map/ppermute | solution.py:26
  58.5 3.8 %collective-permute-start.8 = (f32[2,1,512]{2,1,0:T(1,128)S(1)}, f32[2,1,512]{2,1,0:T(1,128)S(1)}, u32[]{:S(2)}, u32[]{:S(2)}) collective-permute-start(f32[2,1,512]{2,1,0:T(1,128)S(1)} %get-tuple-element.60), channel_id=1, source_target_pairs={{0,8},{8,16},{16,24},{24,0},{1,9},{9,17},{17,25},{25,1},{2,10},{10... | collective-permute-start | bytes 12296 | tf_op jit(solution)/shard_map/ppermute | solution.py:24
  59.5 2.9 collective-permute-start.9
  62.5 11.9 %collective-permute-start.10 = (f32[2,258,1]{2,1,0:T(8,128)S(1)}, f32[2,258,1]{2,1,0:T(8,128)S(1)}, u32[]{:S(2)}, u32[]{:S(2)}) collective-permute-start(f32[2,258,1]{2,1,0:T(8,128)S(1)} %get-tuple-element.35), channel_id=1, source_target_pairs={{0,1},{1,2},{2,3},{3,4},{4,5},{5,6},{6,7},{7,0},{8,9},{9,10},{10,1... | collective-permute-start | bytes 6200 | tf_op jit(solution)/shard_map/ppermute | solution.py:24
  62.6 27.5 %collective-permute-start.11 = (f32[2,258,1]{2,1,0:T(8,128)S(1)}, f32[2,258,1]{2,1,0:T(8,128)S(1)}, u32[]{:S(2)}, u32[]{:S(2)}) collective-permute-start(f32[2,258,1]{2,1,0:T(8,128)S(1)} %get-tuple-element.36), channel_id=1, source_target_pairs={{1,0},{2,1},{3,2},{4,3},{5,4},{6,5},{7,6},{0,7},{9,8},{10,9},{11,1... | collective-permute-start | bytes 6200 | tf_op jit(solution)/shard_map/ppermute | solution.py:26
  91.4 3.8 %collective-permute-start.12 = (f32[2,1,512]{2,1,0:T(1,128)S(1)}, f32[2,1,512]{2,1,0:T(1,128)S(1)}, u32[]{:S(2)}, u32[]{:S(2)}) collective-permute-start(f32[2,1,512]{2,1,0:T(1,128)S(1)} %get-tuple-element.58), channel_id=1, source_target_pairs={{0,8},{8,16},{16,24},{24,0},{1,9},{9,17},{17,25},{25,1},{2,10},{10... | collective-permute-start | bytes 12296 | tf_op jit(solution)/shard_map/ppermute | solution.py:24
  91.4 3.8 %collective-permute-start.13 = (f32[2,1,512]{2,1,0:T(1,128)S(1)}, f32[2,1,512]{2,1,0:T(1,128)S(1)}, u32[]{:S(2)}, u32[]{:S(2)}) collective-permute-start(f32[2,1,512]{2,1,0:T(1,128)S(1)} %get-tuple-element.59), channel_id=1, source_target_pairs={{8,0},{16,8},{24,16},{0,24},{9,1},{17,9},{25,17},{1,25},{10,2},{18... | collective-permute-start | bytes 12296 | tf_op jit(solution)/shard_map/ppermute | solution.py:26
  95.4 11.9 %collective-permute-start.14 = (f32[2,258,1]{2,1,0:T(8,128)S(1)}, f32[2,258,1]{2,1,0:T(8,128)S(1)}, u32[]{:S(2)}, u32[]{:S(2)}) collective-permute-start(f32[2,258,1]{2,1,0:T(8,128)S(1)} %get-tuple-element.33), channel_id=1, source_target_pairs={{0,1},{1,2},{2,3},{3,4},{4,5},{5,6},{6,7},{7,0},{8,9},{9,10},{10,1... | collective-permute-start | bytes 6200 | tf_op jit(solution)/shard_map/ppermute | solution.py:24
  95.4 21.8 %collective-permute-start.15 = (f32[2,258,1]{2,1,0:T(8,128)S(1)}, f32[2,258,1]{2,1,0:T(8,128)S(1)}, u32[]{:S(2)}, u32[]{:S(2)}) collective-permute-start(f32[2,258,1]{2,1,0:T(8,128)S(1)} %get-tuple-element.34), channel_id=1, source_target_pairs={{1,0},{2,1},{3,2},{4,3},{5,4},{6,5},{7,6},{0,7},{9,8},{10,9},{11,1... | collective-permute-start | bytes 6200 | tf_op jit(solution)/shard_map/ppermute | solution.py:26
  119.8 7.9 %collective-permute-start.17 = (bf16[4,4,512]{2,1,0:T(4,128)(2,1)S(1)}, bf16[4,4,512]{2,1,0:T(4,128)(2,1)S(1)}, u32[]{:S(2)}, u32[]{:S(2)}) collective-permute-start(bf16[4,4,512]{2,1,0:T(4,128)(2,1)S(1)} %get-tuple-element.55), channel_id=1, source_target_pairs={{8,0},{16,8},{24,16},{0,24},{9,1},{17,9},{25,17},{1,25},{10,2},{18... | collective-permute-start | bytes 49160 | tf_op jit(solution)/shard_map/ppermute | solution.py:26
  127.7 5.2 %collective-permute-start.16 = (bf16[4,4,512]{2,1,0:T(4,128)(2,1)S(1)}, bf16[4,4,512]{2,1,0:T(4,128)(2,1)S(1)}, u32[]{:S(2)}, u32[]{:S(2)}) collective-permute-start(bf16[4,4,512]{2,1,0:T(4,128)(2,1)S(1)} %get-tuple-element.54), channel_id=1, source_target_pairs={{0,8},{8,16},{16,24},{24,0},{1,9},{9,17},{17,25},{25,1},{2,10},{10... | collective-permute-start | bytes 49160 | tf_op jit(solution)/shard_map/ppermute | solution.py:24
  133.9 21.9 %collective-permute-start.19 = (bf16[4,264,4]{2,1,0:T(8,128)(2,1)}, bf16[4,264,4]{2,1,0:T(8,128)(2,1)S(1)}, u32[]{:S(2)}, u32[]{:S(2)}) collective-permute-start(bf16[4,264,4]{2,1,0:T(8,128)(2,1)} %get-tuple-element.20), channel_id=1, source_target_pairs={{1,0},{2,1},{3,2},{4,3},{5,4},{6,5},{7,6},{0,7},{9,8},{10,9},{11,1... | collective-permute-start | bytes 25352 | tf_op jit(solution)/shard_map/ppermute | solution.py:26
  134.0 25.6 %collective-permute-start.18 = (bf16[4,264,4]{2,1,0:T(8,128)(2,1)}, bf16[4,264,4]{2,1,0:T(8,128)(2,1)S(1)}, u32[]{:S(2)}, u32[]{:S(2)}) collective-permute-start(bf16[4,264,4]{2,1,0:T(8,128)(2,1)} %get-tuple-element.21), channel_id=1, source_target_pairs={{0,1},{1,2},{2,3},{3,4},{4,5},{5,6},{6,7},{7,0},{8,9},{9,10},{10,1... | collective-permute-start | bytes 25352 | tf_op jit(solution)/shard_map/ppermute | solution.py:24
  164.1 58.6 %copy-start.7 = (f32[512]{0:T(512)S(1)}, f32[512]{0:T(512)}, u32[]{:S(2)}) copy-start(f32[512]{0:T(512)} %param.11) | copy-start | bytes 6148
  248.0 29.4 %all-to-all-start = ((f32[8,32,1024]{2,1,0:T(8,128)}), f32[8,32,1024]{2,1,0:T(8,128)S(1)}, u32[]{:S(2)}, u32[]{:S(2)}) async-start(f32[8,32,1024]{2,1,0:T(8,128)} %bitcast.18), calls=%async_computation | async-start | bytes 2097152 | tf_op jit(solution)/shard_map/all_to_all | solution.py:107
  (6 other events, 19.9 us)
Sparse Core Ops, SparseCore 0:
  9.7 212.9 all-gather.1
where the time goes:
time: 300 us; the launch traced here: 299 us
  waiting for transfers between devices  175 us (58%)
  local copies, waits for them, and re-layouts  46.7 us (16%)
  starting transfers between devices  24.9 us (8%)
  between operations  14.4 us (5%)
  blocking collectives  14.3 us (5%)
  other arithmetic  12.1 us (4%)
  matrix products  11.2 us (4%)
    ppermute x10, waiting for transfers between devices, extended(): lax.ppermute(head, axis, [((i + 1) % count, i) for i in range(count)])  61.4 us
    all_gather x1, waiting for transfers between devices, local(): lax.all_gather(input_weight, 'col', axis=0, tiled=True)  49.1 us
    ppermute x10, waiting for transfers between devices, extended(): lax.ppermute(tail, axis, [(i, (i + 1) % count) for i in range(count)])  42.4 us
    another operation x33, local copies, waits for them, and re-layouts, local(): inputs = jnp.stack(pieces).reshape(count, -1).astype(jnp.bfloat16)  30.3 us
    all_to_all x1, waiting for transfers between devices, local(): lax.all_to_all(products, 'col', split_axis=0, concat_axis=1, tiled=True)  21.4 us
    all_gather x1, blocking collectives, local(): lax.all_gather(readin, 'col', axis=0, tiled=True)  14.3 us
    ppermute x10, starting transfers between devices, extended(): lax.ppermute(tail, axis, [(i, (i + 1) % count) for i in range(count)])  12.6 us
    dot_general x1, matrix products, local(): jnp.dot(inputs, lax.all_gather(input_weight, 'col', axis=0, tiled=True),...  9.6 us
  transfers between devices with their start and end apart: 22, of which 17 were waited for; matrix products, arithmetic and copies ran while one was open for 15% of the time, Pallas kernels for 0%

commit v1 on v0

v1 whole, which is shorter than its diff:
```python
import functools

import jax
import jax.numpy as jnp
from jax import lax
from jax.experimental import pallas as pl
from jax.experimental.pallas import tpu as pltpu
from jax.sharding import PartitionSpec as P

CORE = 64
MARGIN = 4
NODES = 512
PATCH = 72
LANES = 128
STAGES = 4
GROUP = 8
REACH = MARGIN + STAGES
WINDOW = CORE + 2 * REACH

dispersion = 2.0
nonlinear = -0.7
time_step = 0.1

bf16 = jnp.bfloat16
f32 = jnp.float32
VMEM = pl.BlockSpec(memory_space=pltpu.VMEM)
SMEM = pl.BlockSpec(memory_space=pltpu.SMEM)


def call(kernel, outs, operands, scratch=(), megabytes=32, name=None):
    return pl.pallas_call(
        kernel,
        out_shape=tuple(jax.ShapeDtypeStruct(*out) for out in outs),
        in_specs=[SMEM] + [VMEM] * (len(operands) - 1),
        out_specs=tuple(VMEM for _ in outs),
        scratch_shapes=list(scratch),
        compiler_params=pltpu.CompilerParams(vmem_limit_bytes=megabytes * 2**20),
        name=name,
    )(*operands)


def tendency(real_part, imag_part):
    def spread(values):
        rows, cols = values.shape
        return (
            pltpu.roll(values, 1, 0)
            + pltpu.roll(values, rows - 1, 0)
            + pltpu.roll(values, 1, 1)
            + pltpu.roll(values, cols - 1, 1)
            - 4.0 * values
        )

    real_spread = spread(real_part)
    imag_spread = spread(imag_part)
    modulus = real_part * real_part + imag_part * imag_part
    first = (
        real_part
        + real_spread
        - dispersion * imag_spread
        - modulus * (real_part - nonlinear * imag_part)
    )
    second = (
        imag_part
        + imag_spread
        + dispersion * real_spread
        - modulus * (imag_part + nonlinear * real_part)
    )
    return first, second


def forecast(start):
    slope = tendency(*start)
    total = slope
    for ahead, weight in ((0.5, 2.0), (0.5, 2.0), (1.0, 1.0)):
        at = tuple(s + ahead * time_step * k for s, k in zip(start, slope))
        slope = tendency(*at)
        total = tuple(t + weight * k for t, k in zip(total, slope))
    return tuple(s + time_step / 6.0 * t for s, t in zip(start, total))


def aligned(value):
    return pl.multiple_of(value, GROUP)


def both_cores(half, own, other):
    low = jnp.where(half == 0, own, other)
    high = jnp.where(half == 0, other, own)
    return low, high


def tile_of(values, tile):
    return values[:, tile * LANES : (tile + 1) * LANES]


def write_lines(lines_ref, channel, tile, values):
    depth = lines_ref.shape[2]
    for part in range(PATCH // depth):
        at = MARGIN + part * depth
        lines_ref[channel * (PATCH // depth) + part, tile] = values[at : at + depth].astype(bf16)


def send_lines(place_ref, lines_ref, message_refs):
    pairs = len(message_refs)
    for ahead, message_ref in enumerate(message_refs):
        message_ref[...] = lines_ref[lax.rem(place_ref[1] + ahead, pairs)]


def inner_kernel(place_ref, field_ref, other_ref, *refs):
    message_refs, (model_ref, lines_ref) = refs[:-2], refs[-2:]
    half = place_ref[0]
    at = aligned((other_ref.shape[1] - WINDOW) * (1 - half))
    at_own = aligned(at + half * (field_ref.shape[1] - other_ref.shape[1]))
    start = []
    for channel in range(2):
        own = field_ref[channel, pl.ds(at_own, WINDOW), :]
        other = other_ref[channel, pl.ds(at, WINDOW), :]
        start.append(jnp.concatenate(both_cores(half, own, other), 1))
    model = forecast(start)
    tiles = start[0].shape[1] // LANES
    for channel, values in enumerate(tuple(start) + model):
        for tile in range(1, tiles - 1):
            write_lines(lines_ref, channel, tile - 1, tile_of(values, tile))
    for channel in range(2):
        model_ref[channel] = model[channel][REACH : REACH + CORE]
    send_lines(place_ref, lines_ref, message_refs)


def outer_kernel(place_ref, field_ref, other_ref, side_ref, ends_ref, inner_ref, gain_ref, *refs):
    message_refs, (same_ref, away_ref, lines_ref, window_ref) = refs[:-4], refs[-4:]
    half = place_ref[0]
    width = field_ref.shape[2]
    rows = other_ref.shape[1]
    tiles = 2 * width // LANES
    shift = half * (field_ref.shape[1] - rows)
    at = aligned((rows - WINDOW) * (1 - half))
    start = []
    for channel in range(2):
        own = field_ref[channel, pl.ds(aligned(at + shift), WINDOW), :]
        other = other_ref[channel, pl.ds(at, WINDOW), :]
        low, high = both_cores(half, own, other)
        side = side_ref[channel, pl.ds(at, WINDOW), :]
        start.append(jnp.concatenate([high[:, width - 2 * LANES :], side, low[:, : 2 * LANES]], 1))
    model = forecast(start)
    for channel, values in enumerate(tuple(start) + model):
        write_lines(lines_ref, channel, 0, tile_of(values, 3))
        write_lines(lines_ref, channel, 1, tile_of(values, 1))
    first = [values[REACH : REACH + CORE] for values in model]

    length = WINDOW - REACH
    at = aligned((rows - length) * half)
    start = []
    for channel in range(2):
        own = field_ref[channel, pl.ds(aligned(at + shift), length), :]
        other = other_ref[channel, pl.ds(at, length), :]
        side = side_ref[channel, pl.ds(at, length), :]
        cells = jnp.concatenate(both_cores(half, own, other) + (side,), 1)
        window_ref[channel, pl.ds(aligned(REACH * (1 - half)), length), :] = cells
        window_ref[channel, pl.ds(aligned(length * half), REACH), :] = ends_ref[channel]
        start.append(window_ref[channel])
    model = forecast(start)
    for channel, values in enumerate(tuple(start) + model):
        for tile in range(tiles):
            write_lines(lines_ref, channel, 2 + tile, tile_of(values, tile))
    send_lines(place_ref, lines_ref, message_refs)

    for channel in range(2):
        gain = gain_ref[channel]
        second = model[channel][REACH : REACH + CORE]
        for tile in range(tiles // 2):
            lanes = slice(tile * LANES, (tile + 1) * LANES)
            far = slice(width + tile * LANES, width + (tile + 1) * LANES)
            low = tile_of(first[channel], 3) if tile == 0 else inner_ref[channel, :, lanes]
            high = tile_of(first[channel], 1) if tile == tiles // 2 - 1 else inner_ref[channel, :, far]
            for row, (left, right) in enumerate(((low, high), (second[:, lanes], second[:, far]))):
                same_ref[channel, row, :, lanes] = gain * jnp.where(half == 0, left, right)
                away_ref[channel, row, :, lanes] = gain * jnp.where(half == 0, right, left)


def drive_kernel(pairs, place_ref, *refs):
    inner_refs, outer_refs, weight_refs = refs[:pairs], refs[pairs : 2 * pairs], refs[2 * pairs : 2 * pairs + 2]
    out_refs, (cells_ref, left_ref) = refs[2 * pairs + 2 : -2], refs[-2:]
    tiles, depth = outer_refs[0].shape[0] - 2, outer_refs[0].shape[1]
    total = pairs * tiles
    for pair in range(pairs):
        for row in range(2):
            for tile in range(tiles):
                if row == 1:
                    values = outer_refs[pair][2 + tile]
                elif tile == 0 or tile == tiles - 1:
                    values = outer_refs[pair][0 if tile == 0 else 1]
                else:
                    values = inner_refs[pair][tile - 1]
                at = (row * total + pair * tiles + tile) * depth
                cells_ref[at : at + depth, :] = values.astype(f32)
    lane = lax.broadcasted_iota(jnp.int32, (total, LANES), 1)
    half = place_ref[0]
    lines = depth // 2
    width = lines * PATCH
    sums = None
    for which in range(2):
        begin = lines * (half if which == 0 else 1 - half)
        for row in range(2):
            held = [None, None]
            for line in range(lines):
                own = cells_ref[pl.ds(row * total * depth + begin + line, total, stride=depth), :]
                before = pltpu.roll(own, 1, 0)
                after = pltpu.roll(own, total - 1, 0)
                even = jnp.where(lane >= LANES - MARGIN, before, own)
                odd = jnp.where(lane < MARGIN, after, own)
                first = line * PATCH
                offset = first % LANES
                lanes = slice(first - offset, first - offset + LANES)
                for parity, (values, shift) in enumerate(((even, MARGIN), (odd, MARGIN + CORE))):
                    at = (parity * 2 + row) * total
                    moved = pltpu.roll(values, (first + shift) % LANES, 1)
                    current = moved if offset == 0 else jnp.where(lane >= offset, moved, held[parity])
                    if offset + PATCH >= LANES or line == lines - 1:
                        left_ref[at : at + total, lanes] = current.astype(bf16)
                        if line == lines - 1 and offset + PATCH > LANES:
                            more = slice(lanes.stop, lanes.stop + LANES)
                            left_ref[at : at + total, more] = moved.astype(bf16)
                        current = moved
                    held[parity] = current
        term = jnp.dot(left_ref[:, :width], weight_refs[which][...], preferred_element_type=f32)
        sums = term if sums is None else sums + term
    for pair, out_ref in enumerate(out_refs):
        pieces = []
        for of in (pair, (pair + pairs // 2) % pairs):
            for row in range(2):
                for parity in range(2):
                    at = (parity * 2 + row) * total + of * tiles
                    pieces.append(sums[at : at + tiles])
        out_ref[...] = jnp.concatenate(pieces, 0).astype(bf16)


def halves(half, first, second):
    rows = first.shape[0]
    row = lax.broadcasted_iota(jnp.int32, first.shape, 0)
    low = jnp.where(row < rows // 2, first, pltpu.roll(second, rows // 2, 0))
    high = jnp.where(row < rows // 2, pltpu.roll(first, rows // 2, 0), second)
    return jnp.where(half == 0, low, high), jnp.where(half == 0, high, low)


def readout_kernel(pairs, slices, place_ref, *refs):
    parts, recur_ref, weights = refs[:pairs], refs[pairs], refs[pairs + 1 : pairs + 1 + slices]
    fresh_same, fresh_away, own_same, own_away, far_same, far_away = refs[pairs + 1 + slices :]
    half = place_ref[0]
    total = recur_ref[...]
    for part in parts:
        total = total + part[...].astype(f32)
    fresh = jnp.tanh(total)
    tiles = fresh.shape[0] // 8
    for row in range(2):
        at = row * 2 * tiles
        same, away = halves(half, fresh[at : at + tiles], fresh[at + tiles : at + 2 * tiles])
        fresh_same[row] = same
        fresh_away[row] = away
    readin = fresh.astype(bf16)
    lane = lax.broadcasted_iota(jnp.int32, (tiles, LANES), 1)
    for index, weight in enumerate(weights):
        products = jnp.dot(readin, weight[...], preferred_element_type=f32)
        lines = products.shape[1] // CORE
        begin = lax.bitwise_xor(place_ref[2], index) * lines
        for tile in range(products.shape[1] // LANES):
            values = tile_of(products, tile)
            for of, (same_ref, away_ref) in enumerate(((own_same, own_away), (far_same, far_away))):
                pair = []
                for row in range(2):
                    at = (of * 2 + row) * 2 * tiles
                    low, high = values[at : at + tiles], values[at + tiles : at + 2 * tiles]
                    pair.append(
                        (
                            jnp.where(lane < CORE, low, pltpu.roll(high, CORE, 1)),
                            jnp.where(lane < CORE, pltpu.roll(low, CORE, 1), high),
                        )
                    )
                for line in range(2):
                    same, away = halves(half, pair[0][line], pair[1][line])
                    same_ref[begin + 2 * tile + line] = same.astype(bf16)
                    away_ref[begin + 2 * tile + line] = away.astype(bf16)


def final_kernel(
    place_ref,
    own_same,
    own_away,
    far_same,
    far_away,
    gained_same,
    gained_away,
    fresh_same,
    fresh_away,
    out_ref,
    states_ref,
    cells_ref,
):
    half = place_ref[0]
    side = place_ref[3]
    tiles = out_ref.shape[2] // LANES
    block_rows = out_ref.shape[1] // CORE
    rows = 2 * tiles
    for away, (own, far, gained, fresh) in enumerate(
        ((own_same, far_same, gained_same, fresh_same), (own_away, far_away, gained_away, fresh_away))
    ):
        of = half if away == 0 else 1 - half
        places = (block_rows // 2 - 1 + of, (block_rows - 1) * of)
        for opposite, values in enumerate((own, far)):
            channel = side if opposite == 0 else 1 - side
            cells_ref[...] = values[...].astype(f32).reshape(CORE * rows, LANES)
            for row in range(2):
                for tile in range(tiles):
                    lanes = slice(tile * LANES, (tile + 1) * LANES)
                    placed = cells_ref[pl.ds(row * tiles + tile, CORE, stride=rows), :]
                    at = pl.multiple_of(places[row] * CORE, CORE)
                    out_ref[channel, pl.ds(at, CORE), lanes] = gained[channel, row, :, lanes] + placed
        for row in range(2):
            for column in range(2 * tiles):
                at = (column % 2) * tiles + column // 2
                states_ref[places[row], column : column + 1, :] = fresh[row, at : at + 1, :]


def local(field, states, input_weight, recurrent_weight, bias, output_weight, model_gain):
    height, width = field.shape[1:]
    sections = lax.axis_size("col")
    bands = lax.axis_size("row")
    pairs = sections // 2
    block_rows = height // CORE
    tiles = width // LANES
    depth = 4 * PATCH // pairs
    slices = sections // 2
    rows = height // 2 + REACH
    column = lax.axis_index("col")
    half = column % 2
    place = jnp.stack([half, column // 2, column % slices, column // slices])

    def across(values):
        return lax.ppermute(values, "col", [(i, i ^ 1) for i in range(sections)])

    def along(values, ahead):
        if ahead % pairs == 0:
            return values
        return lax.ppermute(values, "col", [(i, (i + 2 * ahead) % sections) for i in range(sections)])

    def own_rows(begin, count):
        return lax.dynamic_slice_in_dim(field, begin, count, 1)

    beyond = height - rows
    other = across(own_rows((1 - half) * beyond, rows))

    mine = own_rows(half * beyond, rows)
    first = half == 0
    left_edge = jnp.where(first, mine[:, :, :STAGES], other[:, :, :STAGES])
    right_edge = jnp.where(first, other[:, :, width - STAGES :], mine[:, :, width - STAGES :])
    after = along(left_edge, -1)
    before = along(right_edge, 1)

    inner = call(
        inner_kernel,
        [((2 * tiles - 2, depth, LANES), bf16)] * pairs + [((2, CORE, 2 * width), f32)],
        (place, field, other),
        [pltpu.VMEM((pairs, 2 * tiles - 2, depth, LANES), bf16)],
        name="inner_model",
    )
    inner_messages, inner_model = inner[:pairs], inner[pairs]
    inner_patches = [along(inner_messages[-ahead % pairs], -ahead) for ahead in range(pairs)]

    side = jnp.concatenate([after, jnp.zeros((2, rows, LANES - 2 * STAGES), f32), before], 2)
    edge = half * (rows - REACH)
    near = own_rows(half * (height - REACH), REACH)
    far = lax.dynamic_slice_in_dim(other, edge, REACH, 1)
    ends = jnp.concatenate(
        [jnp.where(first, near, far), jnp.where(first, far, near), lax.dynamic_slice_in_dim(side, edge, REACH, 1)], 2
    )
    pattern = []
    for band in range(bands):
        for item in range(0, sections, 2):
            pattern.append((band * sections + item, (band - 1) % bands * sections + item + 1))
            pattern.append((band * sections + item + 1, (band + 1) % bands * sections + item))
    ends = lax.ppermute(ends, ("row", "col"), pattern)

    outer = call(
        outer_kernel,
        [((2 * tiles + 2, depth, LANES), bf16)] * pairs + [((2, 2, CORE, width), f32)] * 2,
        (place, field, other, side, ends, inner_model, jnp.concatenate([model_gain, model_gain], 2)),
        [
            pltpu.VMEM((pairs, 2 * tiles + 2, depth, LANES), bf16),
            pltpu.VMEM((2, WINDOW, 2 * width + LANES), f32),
        ],
        name="outer_model",
    )
    outer_messages, (gained_same, gained_away) = outer[:pairs], outer[pairs:]
    outer_patches = [along(outer_messages[-ahead % pairs], -ahead) for ahead in range(pairs)]
    gained_away = across(gained_away)

    weight_other = across(input_weight)
    readout_weights = [output_weight]
    for index in range(1, slices):
        if index % 2:
            readout_weights.append(across(readout_weights[index - 1]))
        else:
            pattern = [(i, i ^ index) for i in range(sections)]
            readout_weights.append(lax.ppermute(output_weight, "col", pattern))
    previous = states.astype(bf16).reshape(2, block_rows // 2, tiles, 2, NODES)
    kept = lax.dynamic_index_in_dim(previous, half, 0, keepdims=False)
    got = across(lax.dynamic_index_in_dim(previous, 1 - half, 0, keepdims=False))
    chip = jnp.stack([jnp.where(first, kept, got), jnp.where(first, got, kept)])
    chip = jnp.where(first, chip[:, ::-1], chip)
    chip = chip.transpose(1, 3, 0, 2, 4).reshape(-1, NODES)
    recur = jnp.dot(
        jnp.concatenate([chip, along(chip, pairs // 2)], 0), recurrent_weight, preferred_element_type=f32
    ) + bias

    total = pairs * 2 * tiles
    parts = call(
        functools.partial(drive_kernel, pairs),
        [((8 * 2 * tiles, NODES), bf16)] * pairs,
        (place, *inner_patches, *outer_patches, input_weight, weight_other),
        [
            pltpu.VMEM((2 * total * depth, LANES), f32),
            pltpu.VMEM((4 * total, -(-depth // 2 * PATCH // LANES) * LANES), bf16),
        ],
        megabytes=40,
        name="drive",
    )
    parts = [along(part, ahead) for ahead, part in enumerate(parts)]

    fresh_same, fresh_away, own_same, own_away, far_same, far_away = call(
        functools.partial(readout_kernel, pairs, slices),
        [((2, 2 * tiles, NODES), f32)] * 2 + [((CORE, 2 * tiles, LANES), bf16)] * 4,
        (place, *parts, recur, *readout_weights),
        name="readout",
    )
    pattern = [(i, ((i + sections // 2) % sections) ^ 1) for i in range(sections)]
    far_same = along(far_same, pairs // 2)
    far_away = lax.ppermute(far_away, "col", pattern)
    own_away = across(own_away)
    fresh_away = across(fresh_away)
    return call(
        final_kernel,
        [((2, height, width), f32), ((block_rows, 2 * tiles, NODES), f32)],
        (place, own_same, own_away, far_same, far_away, gained_same, gained_away, fresh_same, fresh_away),
        [pltpu.VMEM((CORE * 2 * tiles, LANES), f32)],
        name="final",
    )


def solution(mesh):
    placed = (
        P(None, "row", "col"),
        P("row", "col", None),
        P("col", None),
        P(),
        P(),
        P(None, "col"),
        P(),
    )
    return jax.shard_map(
        local,
        mesh=mesh,
        in_specs=placed,
        out_specs=(P(None, "row", "col"), P("row", "col", None)),
        check_vma=False,
    )
```

time: 300 us -> 111 us (0.37)
  waiting for transfers between devices: 175 us -> 55.8 us
  local copies, waits for them, and re-layouts: 46.7 us -> 9.08 us
  Pallas kernels: 0 us -> 16.7 us
  blocking collectives: 14.3 us -> 0 us
  between operations: 14.4 us -> 0.84 us
  matrix products: 11.2 us -> 0.21 us
  other arithmetic: 12.1 us -> 3.07 us
    all_gather x1 -> x0, waiting for transfers between devices: 49.1 us -> none  [local(): lax.all_gather(input_weight, 'col', axis=0, tiled=True)]
    ppermute x20 -> x24, waiting for transfers between devices: 104 us -> 55.8 us  [the longest x13 48.4 us: along(): lax.ppermute(values, 'col', [(i, (i + 2 * ahead) % sections) for i in ran...]
    another operation x33 -> x0, local copies, waits for them, and re-layouts: 30.3 us -> none  [local(): inputs = jnp.stack(pieces).reshape(count, -1).astype(jnp.bfloat16)]
    all_to_all x1 -> x0, waiting for transfers between devices: 21.4 us -> none  [local(): lax.all_to_all(products, 'col', split_axis=0, concat_axis=1, tiled=True)]
    pallas_call x0 -> x5, Pallas kernels: none -> 16.7 us  [call(): pl.pallas_call(kernel, out_shape=tuple((jax.ShapeDtypeStruct(*out) for ou...]
    all_gather x1 -> x0, blocking collectives: 14.3 us -> none  [local(): lax.all_gather(readin, 'col', axis=0, tiled=True)]
    dot_general x3 -> x1, matrix products: 11.2 us -> 0.21 us  [local(): jnp.dot(jnp.concatenate([chip, along(chip, pairs // 2)], 0), recurrent_we...]
    unnamed x16 -> x30, local copies, waits for them, and re-layouts: 1.57 us -> 6.33 us
  transfers between devices with their start and end apart: 22 -> 24, of which waited for: 17 -> 11; matrix products, arithmetic and copies ran while one was open for 15% -> 5% of each run, Pallas kernels for 0% -> 13%
where the time goes in v1:
time: 111 us
  waiting for transfers between devices  55.8 us (50%)
  starting transfers between devices  25 us (23%)
  Pallas kernels  16.7 us (15%)
  local copies, waits for them, and re-layouts  9.08 us (8%)
  other arithmetic  3.07 us (3%)
    ppermute x13, waiting for transfers between devices, along(): lax.ppermute(values, 'col', [(i, (i + 2 * ahead) % sections) for i in ran...  48.4 us
    pallas_call x5, Pallas kernels, call(): pl.pallas_call(kernel, out_shape=tuple((jax.ShapeDtypeStruct(*out) for ou...  16.7 us
    ppermute x13, starting transfers between devices, along(): lax.ppermute(values, 'col', [(i, (i + 2 * ahead) % sections) for i in ran...  11.5 us
    ppermute x8, starting transfers between devices, across(): return lax.ppermute(values, 'col', [(i, i ^ 1) for i in range(sections)])  7.67 us
    unnamed x30, local copies, waits for them, and re-layouts  6.33 us
    ppermute x1, waiting for transfers between devices, local(): ends = lax.ppermute(ends, ('row', 'col'), pattern)  3.3 us
    ppermute x1, waiting for transfers between devices, local(): far_away = lax.ppermute(far_away, 'col', pattern)  2.97 us
    ppermute x1, starting transfers between devices, local(): readout_weights.append(lax.ppermute(output_weight, 'col', pattern))  2.43 us
  transfers between devices with their start and end apart: 24, of which 11 were waited for; matrix products, arithmetic and copies ran while one was open for 5% of the time, Pallas kernels for 13%

profile of v1, /device:TPU:1, one launch (start us, length us, event | category | flops | bytes accessed | tf_op | source)
XLA Modules:
  0.0 110.6 jit_solution(17762288939458957881)
XLA Ops:
  0.8 2.0 %constant_dynamic-slice_fusion.3 = f32[2,136,512]{2,1,0:T(8,128)} fusion(f32[2,256,512]{2,1,0:T(8,128)} %field_ref.3, s32[]{:T(128)S(6)} %select_n.86), kind=kLoop, calls=%fused_computation.22 | loop fusion | bytes 1114116 | tf_op jit(solution)/shard_map/dynamic_slice | solution.py:345
  3.1 2.4 %collective-permute-start.17 = (bf16[512,1024]{1,0:T(8,128)(2,1)}, bf16[512,1024]{1,0:T(8,128)(2,1)S(1)}, u32[]{:S(2)}, u32[]{:S(2)}) collective-permute-start(bf16[512,1024]{1,0:T(8,128)(2,1)} %refs_5_.1), channel_id=1, source_target_pairs={{0,2},{1,3},{2,0},{3,1},{4,6},{5,7},{6,4},{7,5},{8,10},{9,11},{10,... | collective-permute-start | bytes 3145736 | tf_op jit(solution)/shard_map/ppermute | solution.py:402
  9.0 4.1 %collective-permute-start.4 = (f32[2,136,4]{2,1,0:T(8,128)S(1)}, f32[2,136,4]{2,1,0:T(8,128)S(1)}, u32[]{:S(2)}, u32[]{:S(2)}) collective-permute-start(f32[2,136,4]{2,1,0:T(8,128)S(1)} %get-tuple-element.46), channel_id=1, source_target_pairs={{0,6},{1,7},{2,0},{3,1},{4,2},{5,3},{6,4},{7,5},{8,14},{9,15},{10,... | collective-permute-start | bytes 13064 | tf_op jit(solution)/shard_map/ppermute | solution.py:342
  13.9 3.0 %inner_model.1 = (bf16[6,72,128]{2,1,0:T(8,128)(2,1)S(1)}, bf16[6,72,128]{2,1,0:T(8,128)(2,1)S(1)}, bf16[6,72,128]{2,1,0:T(8,128)(2,1)S(1)}, bf16[6,72,128]{2,1,0:T(8,128)(2,1)S(1)}, f32[2,64,1024]{2,1,0:T(8,128)S(1)}) custom-call(s32[4]{0:T(128)S(1)} %pad_add_fusion.place_ref, f32[2,256,512]{2,1,0:T(8,128)S(1)} %copy-done.1, ...), custom_call_target="tpu_custom_call" | custom-call | tf_op jit(solution)/shard_map/inner_model/pallas_call | solution.py:31
  16.9 15.1 %collective-permute-done.4 = f32[2,136,4]{2,1,0:T(8,128)S(1)} collective-permute-done((f32[2,136,4]{2,1,0:T(8,128)S(1)}, f32[2,136,4]{2,1,0:T(8,128)S(1)}, u32[]{:S(2)}, u32[]{:S(2)}) %collective-permute-start.4) | collective-permute-done | bytes 4384 | tf_op jit(solution)/shard_map/ppermute | solution.py:342
  32.9 3.9 %collective-permute-done.5 = f32[2,136,4]{2,1,0:T(8,128)S(1)} collective-permute-done((f32[2,136,4]{2,1,0:T(8,128)S(1)}, f32[2,136,4]{2,1,0:T(8,128)S(1)}, u32[]{:S(2)}, u32[]{:S(2)}) %collective-permute-start.5) | collective-permute-done | bytes 4384 | tf_op jit(solution)/shard_map/ppermute | solution.py:342
  36.9 1.3 %collective-permute-start.1 = (bf16[6,72,128]{2,1,0:T(8,128)(2,1)S(1)}, bf16[6,72,128]{2,1,0:T(8,128)(2,1)S(1)}, u32[]{:S(2)}, u32[]{:S(2)}) collective-permute-start(bf16[6,72,128]{2,1,0:T(8,128)(2,1)S(1)} %get-tuple-element.24), channel_id=1, source_target_pairs={{0,6},{1,7},{2,0},{3,1},{4,2},{5,3},{6,4},{7,5},{8,14},{9,15},{10,... | collective-permute-start | bytes 331784 | tf_op jit(solution)/shard_map/ppermute | solution.py:342
  38.3 1.5 %collective-permute-start.18 = (bf16[512,1024]{1,0:T(8,128)(2,1)S(1)}, bf16[512,1024]{1,0:T(8,128)(2,1)}, u32[]{:S(2)}, u32[]{:S(2)}) collective-permute-start(bf16[512,1024]{1,0:T(8,128)(2,1)S(1)} %collective-permute-done.17.refs_7_), channel_id=1, source_target_pairs={{0,1},{1,0},{2,3},{3,2},{4,5},{5,4},{6,7},{7,6},{8,9},{9,8},{10,11... | collective-permute-start | bytes 3145736 | tf_op jit(solution)/shard_map/ppermute | solution.py:337
  41.0 3.3 %collective-permute-done.6.ends_ref = f32[2,8,1152]{2,1,0:T(8,128)S(1)} collective-permute-done((f32[2,8,1152]{2,1,0:T(8,128)S(1)}, f32[2,8,1152]{2,1,0:T(8,128)S(1)}, u32[]{:S(2)}, u32[]{:S(2)}) %collective-permute-start.6) | collective-permute-done | bytes 73760 | tf_op jit(solution)/shard_map/ppermute | solution.py:379
  45.0 5.5 %outer_model.1 = (bf16[10,72,128]{2,1,0:T(8,128)(2,1)S(1)}, bf16[10,72,128]{2,1,0:T(8,128)(2,1)}, bf16[10,72,128]{2,1,0:T(8,128)(2,1)S(1)}, bf16[10,72,128]{2,1,...) custom-call(s32[4]{0:T(128)S(1)} %pad_add_fusion.place_ref, f32[2,256,512]{2,1,0:T(8,128)S(1)} %copy-done.1, ...), custom_call_target="tpu_custom_call" | custom-call | tf_op jit(solution)/shard_map/outer_model/pallas_call | solution.py:31
  51.3 3.6 %collective-permute-done.2.refs_2_ = bf16[6,72,128]{2,1,0:T(8,128)(2,1)S(1)} collective-permute-done((bf16[6,72,128]{2,1,0:T(8,128)(2,1)S(1)}, bf16[6,72,128]{2,1,0:T(8,128)(2,1)S(1)}, u32[]{:S(2)}, u32[]{:S(2)}) %collective-permute-start.2) | collective-permute-done | bytes 110624 | tf_op jit(solution)/shard_map/ppermute | solution.py:342
  55.6 5.8 %collective-permute-done.7.refs_5_ = bf16[10,72,128]{2,1,0:T(8,128)(2,1)S(1)} collective-permute-done((bf16[10,72,128]{2,1,0:T(8,128)(2,1)S(1)}, bf16[10,72,128]{2,1,0:T(8,128)(2,1)S(1)}, u32[]{:S(2)}, u32[]{:S(2)}) %collective-permute-start.7) | collective-permute-done | bytes 184352 | tf_op jit(solution)/shard_map/ppermute | solution.py:342
  61.4 9.7 %collective-permute-done.8.refs_6_ = bf16[10,72,128]{2,1,0:T(8,128)(2,1)S(1)} collective-permute-done((bf16[10,72,128]{2,1,0:T(8,128)(2,1)S(1)}, bf16[10,72,128]{2,1,0:T(8,128)(2,1)S(1)}, u32[]{:S(2)}, u32[]{:S(2)}) %collective-permute-start.8) | collective-permute-done | bytes 184352 | tf_op jit(solution)/shard_map/ppermute | solution.py:342
  72.1 2.1 %collective-permute-start.15 = (bf16[32,512]{1,0:T(8,128)(2,1)S(1)}, bf16[32,512]{1,0:T(8,128)(2,1)S(1)}, u32[]{:S(2)}, u32[]{:S(2)}) collective-permute-start(bf16[32,512]{1,0:T(8,128)(2,1)S(1)} %reshape.12), channel_id=1, source_target_pairs={{0,4},{1,5},{2,6},{3,7},{4,0},{5,1},{6,2},{7,3},{8,12},{9,13},{10,... | collective-permute-start | bytes 98312 | tf_op jit(solution)/shard_map/ppermute | solution.py:342
  74.2 1.7 %copy-done.2 = bf16[2592,512]{1,0:T(8,128)(2,1)S(1)} copy-done((bf16[2592,512]{1,0:T(8,128)(2,1)S(1)}, bf16[2592,512]{1,0:T(8,128)(2,1)}, u32[]{:S(2)}) %copy-start.2) | copy-done | bytes 2654232
  78.7 3.9 %drive.1 = (bf16[64,512]{1,0:T(8,128)(2,1)S(1)}, bf16[64,512]{1,0:T(8,128)(2,1)S(1)}, bf16[64,512]{1,0:T(8,128)(2,1)S(1)}, bf16[64,512]{1,0:T(8,128)(2,1)S(1)}) custom-call(s32[4]{0:T(128)S(1)} %pad_add_fusion.place_ref, bf16[6,72,128]{2,1,0:T(8,128)(2,1)S(1)} %get-tuple-element.23.refs_0_, bf16[6,72,128]{2,1,0:T(8,128)(2,1)S(1)} %copy-done.7, ...), custom_call_target="tpu_custom_call" | custom-call | tf_op jit(solution)/shard_map/drive/pallas_call | solution.py:31
  83.2 2.8 %collective-permute-start.13 = (bf16[64,512]{1,0:T(8,128)(2,1)S(1)}, bf16[64,512]{1,0:T(8,128)(2,1)S(1)}, u32[]{:S(2)}, u32[]{:S(2)}) collective-permute-start(bf16[64,512]{1,0:T(8,128)(2,1)S(1)} %get-tuple-element.35), channel_id=1, source_target_pairs={{0,6},{1,7},{2,0},{3,1},{4,2},{5,3},{6,4},{7,5},{8,14},{9,15},{10,... | collective-permute-start | bytes 196616 | tf_op jit(solution)/shard_map/ppermute | solution.py:342
  86.2 1.4 %collective-permute-done.11.refs_1_ = bf16[64,512]{1,0:T(8,128)(2,1)S(1)} collective-permute-done((bf16[64,512]{1,0:T(8,128)(2,1)S(1)}, bf16[64,512]{1,0:T(8,128)(2,1)S(1)}, u32[]{:S(2)}, u32[]{:S(2)}) %collective-permute-start.11) | collective-permute-done | bytes 65568 | tf_op jit(solution)/shard_map/ppermute | solution.py:342
  88.7 2.5 %readout.1 = (f32[2,8,512]{2,1,0:T(8,128)S(1)}, f32[2,8,512]{2,1,0:T(8,128)S(1)}, bf16[64,8,128]{2,1,0:T(8,128)(2,1)S(1)}, bf16[64,8,128]{2,1,0:T(8,128)(2,1)S(1...) custom-call(s32[4]{0:T(128)S(1)} %pad_add_fusion.place_ref, ...), custom_call_target="tpu_custom_call" | custom-call | tf_op jit(solution)/shard_map/readout/pallas_call | solution.py:31
  91.3 3.0 %collective-permute-start.19 = (bf16[64,8,128]{2,1,0:T(8,128)(2,1)S(1)}, bf16[64,8,128]{2,1,0:T(8,128)(2,1)S(1)}, u32[]{:S(2)}, u32[]{:S(2)}) collective-permute-start(bf16[64,8,128]{2,1,0:T(8,128)(2,1)S(1)} %get-tuple-element.37), channel_id=1, source_target_pairs={{0,1},{1,0},{2,3},{3,2},{4,5},{5,4},{6,7},{7,6},{8,9},{9,8},{10,11... | collective-permute-start | bytes 393224 | tf_op jit(solution)/shard_map/ppermute | solution.py:337
  94.6 2.2 %collective-permute-start.21 = (bf16[64,8,128]{2,1,0:T(8,128)(2,1)S(1)}, bf16[64,8,128]{2,1,0:T(8,128)(2,1)S(1)}, u32[]{:S(2)}, u32[]{:S(2)}) collective-permute-start(bf16[64,8,128]{2,1,0:T(8,128)(2,1)S(1)} %get-tuple-element.39), channel_id=1, source_target_pairs={{0,5},{1,4},{2,7},{3,6},{4,1},{5,0},{6,3},{7,2},{8,13},{9,12},{10,... | collective-permute-start | bytes 393224 | tf_op jit(solution)/shard_map/ppermute | solution.py:435
  98.1 7.8 %collective-permute-done.20.far_same = bf16[64,8,128]{2,1,0:T(8,128)(2,1)S(1)} collective-permute-done((bf16[64,8,128]{2,1,0:T(8,128)(2,1)S(1)}, bf16[64,8,128]{2,1,0:T(8,128)(2,1)S(1)}, u32[]{:S(2)}, u32[]{:S(2)}) %collective-permute-start.20) | collective-permute-done | bytes 131104 | tf_op jit(solution)/shard_map/ppermute | solution.py:342
  105.8 3.0 %collective-permute-done.21.far_away = bf16[64,8,128]{2,1,0:T(8,128)(2,1)S(1)} collective-permute-done((bf16[64,8,128]{2,1,0:T(8,128)(2,1)S(1)}, bf16[64,8,128]{2,1,0:T(8,128)(2,1)S(1)}, u32[]{:S(2)}, u32[]{:S(2)}) %collective-permute-start.21) | collective-permute-done | bytes 131104 | tf_op jit(solution)/shard_map/ppermute | solution.py:435
  108.8 1.8 %final.1 = (f32[2,256,512]{2,1,0:T(8,128)}, f32[4,8,512]{2,1,0:T(8,128)}) custom-call(s32[4]{0:T(128)S(1)} %pad_add_fusion.place_ref, bf16[64,8,128]{2,1,0:T(8,128)(2,1)S(1)} %get-tuple-element.36.own_same, bf16[64,8,128]{2,1,0:T(8,128)(2,1)S(1)} %collective-permute-done.19.own_away, bf16[64,8,128]{2,1,0:T(8,128)(2,1)S(1)} %collective-permute-done.20.far_same, ...), custom_call_target="tpu_custom_call" | custom-call | tf_op jit(solution)/shard_map/final/pallas_call | solution.py:31
  (78 shorter events, 16.4 us)
Async XLA Ops:
  0.7 73.6 %collective-permute-start.10 = (bf16[2592,512]{1,0:T(8,128)(2,1)}, bf16[2592,512]{1,0:T(8,128)(2,1)}, u32[]{:S(2)}, u32[]{:S(2)}) collective-permute-start(bf16[2592,512]{1,0:T(8,128)(2,1)} %refs_8_.1), channel_id=1, source_target_pairs={{0,1},{1,0},{2,3},{3,2},{4,5},{5,4},{6,7},{7,6},{8,9},{9,8},{10,11... | collective-permute-start | bytes 7962632 | tf_op jit(solution)/shard_map/ppermute | solution.py:337
  2.8 5.1 %collective-permute-start = (f32[2,136,512]{2,1,0:T(8,128)}, f32[2,136,512]{2,1,0:T(8,128)S(1)}, u32[]{:S(2)}, u32[]{:S(2)}) collective-permute-start(f32[2,136,512]{2,1,0:T(8,128)} %constant_dynamic-slice_fusion.3), channel_id=1, source_target_pairs={{0,1},{1,0},{2,3},{3,2},{4,5},{5,4},{6,7},{7,6},{8,9},{9,8},{10,11... | collective-permute-start | bytes 1671176 | tf_op jit(solution)/shard_map/ppermute | solution.py:337
  3.1 35.1 %collective-permute-start.17 = (bf16[512,1024]{1,0:T(8,128)(2,1)}, bf16[512,1024]{1,0:T(8,128)(2,1)S(1)}, u32[]{:S(2)}, u32[]{:S(2)}) collective-permute-start(bf16[512,1024]{1,0:T(8,128)(2,1)} %refs_5_.1), channel_id=1, source_target_pairs={{0,2},{1,3},{2,0},{3,1},{4,6},{5,7},{6,4},{7,5},{8,10},{9,11},{10,... | collective-permute-start | bytes 3145736 | tf_op jit(solution)/shard_map/ppermute | solution.py:402
  5.6 77.6 %collective-permute-start.16 = (bf16[512,1024]{1,0:T(8,128)(2,1)}, bf16[512,1024]{1,0:T(8,128)(2,1)}, u32[]{:S(2)}, u32[]{:S(2)}) collective-permute-start(bf16[512,1024]{1,0:T(8,128)(2,1)} %refs_5_.1), channel_id=1, source_target_pairs={{0,1},{1,0},{2,3},{3,2},{4,5},{5,4},{6,7},{7,6},{8,9},{9,8},{10,11... | collective-permute-start | bytes 3145736 | tf_op jit(solution)/shard_map/ppermute | solution.py:337
  9.0 23.0 %collective-permute-start.4 = (f32[2,136,4]{2,1,0:T(8,128)S(1)}, f32[2,136,4]{2,1,0:T(8,128)S(1)}, u32[]{:S(2)}, u32[]{:S(2)}) collective-permute-start(f32[2,136,4]{2,1,0:T(8,128)S(1)} %get-tuple-element.46), channel_id=1, source_target_pairs={{0,6},{1,7},{2,0},{3,1},{4,2},{5,3},{6,4},{7,5},{8,14},{9,15},{10,... | collective-permute-start | bytes 13064 | tf_op jit(solution)/shard_map/ppermute | solution.py:342
  13.1 23.7 %collective-permute-start.5 = (f32[2,136,4]{2,1,0:T(8,128)S(1)}, f32[2,136,4]{2,1,0:T(8,128)S(1)}, u32[]{:S(2)}, u32[]{:S(2)}) collective-permute-start(f32[2,136,4]{2,1,0:T(8,128)S(1)} %get-tuple-element.47), channel_id=1, source_target_pairs={{0,2},{1,3},{2,4},{3,5},{4,6},{5,7},{6,0},{7,1},{8,10},{9,11},{10,... | collective-permute-start | bytes 13064 | tf_op jit(solution)/shard_map/ppermute | solution.py:342
  32.0 7.8 %collective-permute-start.14 = (bf16[2,4,2,512]{3,1,2,0:T(4,128)(2,1)S(1)}, bf16[2,4,2,512]{3,1,2,0:T(4,128)(2,1)S(1)}, u32[]{:S(2)}, u32[]{:S(2)}) collective-permute-start(bf16[2,4,2,512]{3,1,2,0:T(4,128)(2,1)S(1)} %bitcast.23), channel_id=1, source_target_pairs={{0,1},{1,0},{2,3},{3,2},{4,5},{5,4},{6,7},{7,6},{8,9},{9,8},{10,11... | collective-permute-start | bytes 49160 | tf_op jit(solution)/shard_map/ppermute | solution.py:337
  36.9 7.5 %collective-permute-start.1 = (bf16[6,72,128]{2,1,0:T(8,128)(2,1)S(1)}, bf16[6,72,128]{2,1,0:T(8,128)(2,1)S(1)}, u32[]{:S(2)}, u32[]{:S(2)}) collective-permute-start(bf16[6,72,128]{2,1,0:T(8,128)(2,1)S(1)} %get-tuple-element.24), channel_id=1, source_target_pairs={{0,6},{1,7},{2,0},{3,1},{4,2},{5,3},{6,4},{7,5},{8,14},{9,15},{10,... | collective-permute-start | bytes 331784 | tf_op jit(solution)/shard_map/ppermute | solution.py:342
  38.3 47.9 %collective-permute-start.18 = (bf16[512,1024]{1,0:T(8,128)(2,1)S(1)}, bf16[512,1024]{1,0:T(8,128)(2,1)}, u32[]{:S(2)}, u32[]{:S(2)}) collective-permute-start(bf16[512,1024]{1,0:T(8,128)(2,1)S(1)} %collective-permute-done.17.refs_7_), channel_id=1, source_target_pairs={{0,1},{1,0},{2,3},{3,2},{4,5},{5,4},{6,7},{7,6},{8,9},{9,8},{10,11... | collective-permute-start | bytes 3145736 | tf_op jit(solution)/shard_map/ppermute | solution.py:337
  39.8 4.5 %collective-permute-start.6 = (f32[2,8,1152]{2,1,0:T(8,128)S(1)}, f32[2,8,1152]{2,1,0:T(8,128)S(1)}, u32[]{:S(2)}, u32[]{:S(2)}) collective-permute-start(f32[2,8,1152]{2,1,0:T(8,128)S(1)} %pad_maximum_fusion.1), channel_id=1, source_target_pairs={{0,25},{1,8},{2,27},{3,10},{4,29},{5,12},{6,31},{7,14},{8,1},{9,16... | collective-permute-start | bytes 221192 | tf_op jit(solution)/shard_map/ppermute | solution.py:379
  44.3 10.5 %collective-permute-start.2 = (bf16[6,72,128]{2,1,0:T(8,128)(2,1)S(1)}, bf16[6,72,128]{2,1,0:T(8,128)(2,1)S(1)}, u32[]{:S(2)}, u32[]{:S(2)}) collective-permute-start(bf16[6,72,128]{2,1,0:T(8,128)(2,1)S(1)} %get-tuple-element.25), channel_id=1, source_target_pairs={{0,4},{1,5},{2,6},{3,7},{4,0},{5,1},{6,2},{7,3},{8,12},{9,13},{10,... | collective-permute-start | bytes 331784 | tf_op jit(solution)/shard_map/ppermute | solution.py:342
  44.4 10.5 %collective-permute-start.3 = (bf16[6,72,128]{2,1,0:T(8,128)(2,1)S(1)}, bf16[6,72,128]{2,1,0:T(8,128)(2,1)S(1)}, u32[]{:S(2)}, u32[]{:S(2)}) collective-permute-start(bf16[6,72,128]{2,1,0:T(8,128)(2,1)S(1)} %get-tuple-element.26), channel_id=1, source_target_pairs={{0,2},{1,3},{2,4},{3,5},{4,6},{5,7},{6,0},{7,1},{8,10},{9,11},{10,... | collective-permute-start | bytes 331784 | tf_op jit(solution)/shard_map/ppermute | solution.py:342
  54.9 6.5 %collective-permute-start.7 = (bf16[10,72,128]{2,1,0:T(8,128)(2,1)S(1)}, bf16[10,72,128]{2,1,0:T(8,128)(2,1)S(1)}, u32[]{:S(2)}, u32[]{:S(2)}) collective-permute-start(bf16[10,72,128]{2,1,0:T(8,128)(2,1)S(1)} %get-tuple-element.29), channel_id=1, source_target_pairs={{0,6},{1,7},{2,0},{3,1},{4,2},{5,3},{6,4},{7,5},{8,14},{9,15},{10,... | collective-permute-start | bytes 552968 | tf_op jit(solution)/shard_map/ppermute | solution.py:342
  55.6 15.5 %collective-permute-start.8 = (bf16[10,72,128]{2,1,0:T(8,128)(2,1)S(1)}, bf16[10,72,128]{2,1,0:T(8,128)(2,1)S(1)}, u32[]{:S(2)}, u32[]{:S(2)}) collective-permute-start(bf16[10,72,128]{2,1,0:T(8,128)(2,1)S(1)} %get-tuple-element.30), channel_id=1, source_target_pairs={{0,4},{1,5},{2,6},{3,7},{4,0},{5,1},{6,2},{7,3},{8,12},{9,13},{10,... | collective-permute-start | bytes 552968 | tf_op jit(solution)/shard_map/ppermute | solution.py:342
  61.4 10.7 %collective-permute-start.9 = (bf16[10,72,128]{2,1,0:T(8,128)(2,1)}, bf16[10,72,128]{2,1,0:T(8,128)(2,1)S(1)}, u32[]{:S(2)}, u32[]{:S(2)}) collective-permute-start(bf16[10,72,128]{2,1,0:T(8,128)(2,1)} %get-tuple-element.31), channel_id=1, source_target_pairs={{0,2},{1,3},{2,4},{3,5},{4,6},{5,7},{6,0},{7,1},{8,10},{9,11},{10,... | collective-permute-start | bytes 552968 | tf_op jit(solution)/shard_map/ppermute | solution.py:342
  71.1 25.9 %collective-permute-start.22 = (f32[2,2,64,512]{3,2,1,0:T(8,128)}, f32[2,2,64,512]{3,2,1,0:T(8,128)S(1)}, u32[]{:S(2)}, u32[]{:S(2)}) collective-permute-start(f32[2,2,64,512]{3,2,1,0:T(8,128)} %get-tuple-element.41), channel_id=1, source_target_pairs={{0,1},{1,0},{2,3},{3,2},{4,5},{5,4},{6,7},{7,6},{8,9},{9,8},{10,11... | collective-permute-start | bytes 1572872 | tf_op jit(solution)/shard_map/ppermute | solution.py:337
  72.1 10.5 %collective-permute-start.15 = (bf16[32,512]{1,0:T(8,128)(2,1)S(1)}, bf16[32,512]{1,0:T(8,128)(2,1)S(1)}, u32[]{:S(2)}, u32[]{:S(2)}) collective-permute-start(bf16[32,512]{1,0:T(8,128)(2,1)S(1)} %reshape.12), channel_id=1, source_target_pairs={{0,4},{1,5},{2,6},{3,7},{4,0},{5,1},{6,2},{7,3},{8,12},{9,13},{10,... | collective-permute-start | bytes 98312 | tf_op jit(solution)/shard_map/ppermute | solution.py:342
  82.6 5.0 %collective-permute-start.11 = (bf16[64,512]{1,0:T(8,128)(2,1)S(1)}, bf16[64,512]{1,0:T(8,128)(2,1)S(1)}, u32[]{:S(2)}, u32[]{:S(2)}) collective-permute-start(bf16[64,512]{1,0:T(8,128)(2,1)S(1)} %get-tuple-element.33), channel_id=1, source_target_pairs={{0,2},{1,3},{2,4},{3,5},{4,6},{5,7},{6,0},{7,1},{8,10},{9,11},{10,... | collective-permute-start | bytes 196616 | tf_op jit(solution)/shard_map/ppermute | solution.py:342
  82.6 5.0 %collective-permute-start.12 = (bf16[64,512]{1,0:T(8,128)(2,1)S(1)}, bf16[64,512]{1,0:T(8,128)(2,1)S(1)}, u32[]{:S(2)}, u32[]{:S(2)}) collective-permute-start(bf16[64,512]{1,0:T(8,128)(2,1)S(1)} %get-tuple-element.34), channel_id=1, source_target_pairs={{0,4},{1,5},{2,6},{3,7},{4,0},{5,1},{6,2},{7,3},{8,12},{9,13},{10,... | collective-permute-start | bytes 196616 | tf_op jit(solution)/shard_map/ppermute | solution.py:342
  83.2 5.6 %collective-permute-start.13 = (bf16[64,512]{1,0:T(8,128)(2,1)S(1)}, bf16[64,512]{1,0:T(8,128)(2,1)S(1)}, u32[]{:S(2)}, u32[]{:S(2)}) collective-permute-start(bf16[64,512]{1,0:T(8,128)(2,1)S(1)} %get-tuple-element.35), channel_id=1, source_target_pairs={{0,6},{1,7},{2,0},{3,1},{4,2},{5,3},{6,4},{7,5},{8,14},{9,15},{10,... | collective-permute-start | bytes 196616 | tf_op jit(solution)/shard_map/ppermute | solution.py:342
  91.3 6.8 %collective-permute-start.19 = (bf16[64,8,128]{2,1,0:T(8,128)(2,1)S(1)}, bf16[64,8,128]{2,1,0:T(8,128)(2,1)S(1)}, u32[]{:S(2)}, u32[]{:S(2)}) collective-permute-start(bf16[64,8,128]{2,1,0:T(8,128)(2,1)S(1)} %get-tuple-element.37), channel_id=1, source_target_pairs={{0,1},{1,0},{2,3},{3,2},{4,5},{5,4},{6,7},{7,6},{8,9},{9,8},{10,11... | collective-permute-start | bytes 393224 | tf_op jit(solution)/shard_map/ppermute | solution.py:337
  94.2 11.6 %collective-permute-start.20 = (bf16[64,8,128]{2,1,0:T(8,128)(2,1)S(1)}, bf16[64,8,128]{2,1,0:T(8,128)(2,1)S(1)}, u32[]{:S(2)}, u32[]{:S(2)}) collective-permute-start(bf16[64,8,128]{2,1,0:T(8,128)(2,1)S(1)} %get-tuple-element.38), channel_id=1, source_target_pairs={{0,4},{1,5},{2,6},{3,7},{4,0},{5,1},{6,2},{7,3},{8,12},{9,13},{10,... | collective-permute-start | bytes 393224 | tf_op jit(solution)/shard_map/ppermute | solution.py:342
  94.6 14.2 %collective-permute-start.21 = (bf16[64,8,128]{2,1,0:T(8,128)(2,1)S(1)}, bf16[64,8,128]{2,1,0:T(8,128)(2,1)S(1)}, u32[]{:S(2)}, u32[]{:S(2)}) collective-permute-start(bf16[64,8,128]{2,1,0:T(8,128)(2,1)S(1)} %get-tuple-element.39), channel_id=1, source_target_pairs={{0,5},{1,4},{2,7},{3,6},{4,1},{5,0},{6,3},{7,2},{8,13},{9,12},{10,... | collective-permute-start | bytes 393224 | tf_op jit(solution)/shard_map/ppermute | solution.py:435
  96.8 1.2 %collective-permute-start.23 = (f32[2,8,512]{2,1,0:T(8,128)S(1)}, f32[2,8,512]{2,1,0:T(8,128)S(1)}, u32[]{:S(2)}, u32[]{:S(2)}) collective-permute-start(f32[2,8,512]{2,1,0:T(8,128)S(1)} %get-tuple-element.43), channel_id=1, source_target_pairs={{0,1},{1,0},{2,3},{3,2},{4,5},{5,4},{6,7},{7,6},{8,9},{9,8},{10,11... | collective-permute-start | bytes 98312 | tf_op jit(solution)/shard_map/ppermute | solution.py:337
  (15 other events, 256.0 us)

commit v2 on v1

v2 whole, which is shorter than its diff:
```python
import functools

import jax
import jax.numpy as jnp
from jax import lax
from jax.experimental import pallas as pl
from jax.experimental.pallas import tpu as pltpu
from jax.sharding import PartitionSpec as P

CORE = 64
MARGIN = 4
NODES = 512
PATCH = 72
LANES = 128
STAGES = 4
GROUP = 8
REACH = MARGIN + STAGES
WINDOW = CORE + 2 * REACH

dispersion = 2.0
nonlinear = -0.7
time_step = 0.1

bf16 = jnp.bfloat16
f32 = jnp.float32
VMEM = pl.BlockSpec(memory_space=pltpu.VMEM)
SMEM = pl.BlockSpec(memory_space=pltpu.SMEM)


def call(kernel, outs, operands, scratch=(), megabytes=4, micros=1.0, name=None):
    return pl.pallas_call(
        kernel,
        out_shape=tuple(jax.ShapeDtypeStruct(*out) for out in outs),
        in_specs=[SMEM] + [VMEM] * (len(operands) - 1),
        out_specs=tuple(VMEM for _ in outs),
        scratch_shapes=list(scratch),
        compiler_params=pltpu.CompilerParams(vmem_limit_bytes=megabytes * 2**20),
        cost_estimate=pl.CostEstimate(flops=0, bytes_accessed=int(micros * 3.69e6), transcendentals=0),
        name=name,
    )(*operands)


def tendency(real_part, imag_part):
    def spread(values):
        rows, cols = values.shape
        return (
            pltpu.roll(values, 1, 0)
            + pltpu.roll(values, rows - 1, 0)
            + pltpu.roll(values, 1, 1)
            + pltpu.roll(values, cols - 1, 1)
            - 4.0 * values
        )

    real_spread = spread(real_part)
    imag_spread = spread(imag_part)
    modulus = real_part * real_part + imag_part * imag_part
    first = (
        real_part
        + real_spread
        - dispersion * imag_spread
        - modulus * (real_part - nonlinear * imag_part)
    )
    second = (
        imag_part
        + imag_spread
        + dispersion * real_spread
        - modulus * (imag_part + nonlinear * real_part)
    )
    return first, second


def forecast(start):
    slope = tendency(*start)
    total = slope
    for ahead, weight in ((0.5, 2.0), (0.5, 2.0), (1.0, 1.0)):
        at = tuple(s + ahead * time_step * k for s, k in zip(start, slope))
        slope = tendency(*at)
        total = tuple(t + weight * k for t, k in zip(total, slope))
    return tuple(s + time_step / 6.0 * t for s, t in zip(start, total))


def aligned(value):
    return pl.multiple_of(value, GROUP)


def both_cores(half, own, other):
    low = jnp.where(half == 0, own, other)
    high = jnp.where(half == 0, other, own)
    return low, high


def tile_of(values, tile):
    return values[:, tile * LANES : (tile + 1) * LANES]


def edges_kernel(place_ref, field_ref, out_ref):
    height, width = field_ref.shape[1:]
    lane = lax.broadcasted_iota(jnp.int32, (GROUP, LANES), 1)
    for channel in range(2):
        packed = None
        for group in range(height // GROUP):
            rows = slice(group * GROUP, (group + 1) * GROUP)
            left = pltpu.roll(field_ref[channel, rows, :LANES], group * STAGES, 1)
            right = pltpu.roll(field_ref[channel, rows, width - LANES :], (group + 1) * STAGES % LANES, 1)
            values = jnp.where(place_ref[0] == 0, left, right)
            packed = values if packed is None else jnp.where(lane >= group * STAGES, values, packed)
        out_ref[channel] = packed


def ends_kernel(place_ref, field_ref, other_ref, outer_ref, outer_other_ref, side_ref, out_ref):
    half = place_ref[0]
    height, width = field_ref.shape[1:]
    lane = lax.broadcasted_iota(jnp.int32, (GROUP, LANES), 1)
    at = aligned((height - REACH) * half)
    for channel in range(2):
        left, right = both_cores(half, outer_ref[channel], outer_other_ref[channel])
        for group in range(height // GROUP):
            after = pltpu.roll(right, (LANES - group * STAGES) % LANES, 1)
            before = pltpu.roll(left, (LANES - (group + 1) * STAGES) % LANES, 1)
            side_ref[channel, group * GROUP : (group + 1) * GROUP, :] = jnp.where(lane < LANES // 2, after, before)
        low, high = both_cores(half, field_ref[channel, pl.ds(at, REACH), :], other_ref[channel, pl.ds(at, REACH), :])
        out_ref[channel, :, :width] = low
        out_ref[channel, :, width : 2 * width] = high
        out_ref[channel, :, 2 * width :] = side_ref[channel, pl.ds(at, REACH), :]


def model_kernel(outer, place_ref, field_ref, other_ref, side_ref, *refs):
    if outer:
        ends_ref, inner_ref, *message_refs, model_ref, lines_ref, window_ref = refs
    else:
        lines_ref, model_ref = refs
    half = place_ref[0]
    height, width = field_ref.shape[1:]
    tiles = 2 * width // LANES
    length = WINDOW - REACH if outer else WINDOW
    at = aligned((height - length) * half) if outer else aligned(height // 2 - CORE - REACH + CORE * half)
    start = []
    for channel in range(2):
        own = field_ref[channel, pl.ds(at, length), :]
        other = other_ref[channel, pl.ds(at, length), :]
        cells = jnp.concatenate(both_cores(half, own, other) + (side_ref[channel, pl.ds(at, length), :],), 1)
        if outer:
            window_ref[channel, pl.ds(aligned(REACH * (1 - half)), length), :] = cells
            window_ref[channel, pl.ds(aligned(length * half), REACH), :] = ends_ref[channel]
            cells = window_ref[channel]
        start.append(cells)
    model = forecast(start)
    depth = lines_ref.shape[2]
    for channel, values in enumerate(tuple(start) + model):
        for tile in range(tiles):
            for part in range(PATCH // depth):
                at = MARGIN + part * depth
                lines_ref[channel * (PATCH // depth) + part, tile] = tile_of(values, tile)[at : at + depth].astype(bf16)
    for channel in range(2):
        model_ref[channel] = model[channel][REACH : REACH + CORE, : 2 * width]
    if outer:
        pairs = len(message_refs)
        for ahead, message_ref in enumerate(message_refs):
            of = lax.rem(place_ref[1] + ahead, pairs)
            message_ref[0] = inner_ref[of]
            message_ref[1] = lines_ref[of]


def gain_kernel(place_ref, inner_ref, outer_ref, gain_ref, same_ref, away_ref):
    half = place_ref[0]
    width = same_ref.shape[3]
    for channel in range(2):
        gain = gain_ref[channel]
        for row, model_ref in enumerate((inner_ref, outer_ref)):
            for tile in range(width // LANES):
                lanes = slice(tile * LANES, (tile + 1) * LANES)
                low = model_ref[channel, :, lanes]
                high = model_ref[channel, :, width + tile * LANES : width + (tile + 1) * LANES]
                same_ref[channel, row, :, lanes] = gain * jnp.where(half == 0, low, high)
                away_ref[channel, row, :, lanes] = gain * jnp.where(half == 0, high, low)


def drive_kernel(pairs, place_ref, *refs):
    patch_refs, weight_refs = refs[:pairs], refs[pairs : pairs + 2]
    out_refs, (cells_ref, left_ref) = refs[pairs + 2 : -2], refs[-2:]
    _, tiles, depth, _ = patch_refs[0].shape
    total = pairs * tiles
    for row in range(2):
        for pair in range(pairs):
            for tile in range(tiles):
                at = (row * total + pair * tiles + tile) * depth
                cells_ref[at : at + depth, :] = patch_refs[pair][row, tile].astype(f32)
    lane = lax.broadcasted_iota(jnp.int32, (total, LANES), 1)
    half = place_ref[0]
    lines = depth // 2
    width = lines * PATCH
    sums = None
    for which in range(2):
        begin = lines * (half if which == 0 else 1 - half)
        for row in range(2):
            held = [None, None]
            for line in range(lines):
                own = cells_ref[pl.ds(row * total * depth + begin + line, total, stride=depth), :]
                before = pltpu.roll(own, 1, 0)
                after = pltpu.roll(own, total - 1, 0)
                even = jnp.where(lane >= LANES - MARGIN, before, own)
                odd = jnp.where(lane < MARGIN, after, own)
                first = line * PATCH
                offset = first % LANES
                lanes = slice(first - offset, first - offset + LANES)
                for parity, (values, shift) in enumerate(((even, MARGIN), (odd, MARGIN + CORE))):
                    at = (row * 2 + parity) * total
                    moved = pltpu.roll(values, (first + shift) % LANES, 1)
                    current = moved if offset == 0 else jnp.where(lane >= offset, moved, held[parity])
                    if offset + PATCH >= LANES or line == lines - 1:
                        left_ref[which, at : at + total, lanes] = current.astype(bf16)
                        if line == lines - 1 and offset + PATCH > LANES:
                            more = slice(lanes.stop, lanes.stop + LANES)
                            left_ref[which, at : at + total, more] = moved.astype(bf16)
                        current = moved
                    held[parity] = current
        term = jnp.dot(left_ref[which, :, :width], weight_refs[which][...], preferred_element_type=f32)
        sums = term if sums is None else sums + term
    for pair, out_ref in enumerate(out_refs):
        pieces = []
        for of in (pair, (pair + pairs // 2) % pairs):
            for part in range(4):
                at = part * total + of * tiles
                pieces.append(sums[at : at + tiles])
        out_ref[...] = jnp.concatenate(pieces, 0).astype(bf16)


def part_kernel(place_ref, weight_ref, out_ref, done):
    rows = out_ref.shape[0]
    begin = pl.multiple_of(place_ref[4] * rows, rows)
    copy = pltpu.make_async_copy(weight_ref.at[pl.ds(begin, rows), :], out_ref, done)
    copy.start()
    copy.wait()


def row_part(place, weight):
    rows, columns = weight.shape
    return pl.pallas_call(
        part_kernel,
        out_shape=jax.ShapeDtypeStruct((rows // 2, columns), weight.dtype),
        in_specs=[SMEM, pl.BlockSpec(memory_space=pl.ANY)],
        out_specs=VMEM,
        scratch_shapes=[pltpu.SemaphoreType.DMA(())],
        compiler_params=pltpu.CompilerParams(vmem_limit_bytes=4 * 2**20),
        cost_estimate=pl.CostEstimate(flops=0, bytes_accessed=2_000_000, transcendentals=0),
        name="part",
    )(place, weight)


def previous_kernel(place_ref, states_ref, same_ref, away_ref):
    half = place_ref[0]
    block_rows, block_cols = states_ref.shape[:2]
    for away, out_ref in enumerate((same_ref, away_ref)):
        of = half if away == 0 else 1 - half
        pieces = []
        for row in (block_rows // 2 - 1 + of, (block_rows - 1) * of):
            values = states_ref[row]
            for parity in range(2):
                pieces += [values[column : column + 1] for column in range(parity, block_cols, 2)]
        out_ref[...] = jnp.concatenate(pieces, 0)


def recur_kernel(place_ref, same_ref, away_ref, weight_ref, bias_ref, out_ref):
    low, high = both_cores(place_ref[0], same_ref[...], away_ref[...])
    tiles = low.shape[0] // 4
    pieces = []
    for index in range(4):
        pieces += [values[index * tiles : (index + 1) * tiles] for values in (low, high)]
    previous = jnp.concatenate(pieces, 0).astype(bf16)
    out_ref[...] = jnp.dot(previous, weight_ref[...], preferred_element_type=f32) + bias_ref[...]


def halves(half, first, second):
    rows = first.shape[0]
    row = lax.broadcasted_iota(jnp.int32, first.shape, 0)
    low = jnp.where(row < rows // 2, first, pltpu.roll(second, rows // 2, 0))
    high = jnp.where(row < rows // 2, pltpu.roll(first, rows // 2, 0), second)
    return jnp.where(half == 0, low, high), jnp.where(half == 0, high, low)


def readout_kernel(pairs, slices, place_ref, *refs):
    parts, recur_refs, weights = refs[:pairs], refs[pairs : pairs + 2], refs[pairs + 2 : -6]
    fresh_same, fresh_away, own_same, own_away, far_same, far_away = refs[-6:]
    half = place_ref[0]
    total = jnp.concatenate([recur_ref[...] for recur_ref in recur_refs], 0)
    for part in parts:
        total = total + part[...].astype(f32)
    fresh = jnp.tanh(total)
    tiles = fresh.shape[0] // 8
    for row in range(2):
        at = row * 2 * tiles
        same, away = halves(half, fresh[at : at + tiles], fresh[at + tiles : at + 2 * tiles])
        fresh_same[row] = same
        fresh_away[row] = away
    readin = fresh.astype(bf16)
    lane = lax.broadcasted_iota(jnp.int32, (tiles, LANES), 1)
    swapped = place_ref[4] == 1
    low, high = readin[:, : NODES // 2], readin[:, NODES // 2 :]
    ordered = (jnp.where(swapped, high, low), jnp.where(swapped, low, high))
    for index in range(slices):
        if index < 2:
            products = jnp.dot(readin, weights[index][...], preferred_element_type=f32)
        else:
            products = sum(
                jnp.dot(ordered[part], weights[2 * index - 2 + part][...], preferred_element_type=f32)
                for part in range(2)
            )
        lines = products.shape[1] // CORE
        begin = lax.bitwise_xor(place_ref[2], index) * lines
        for tile in range(products.shape[1] // LANES):
            values = tile_of(products, tile)
            for of, (same_ref, away_ref) in enumerate(((own_same, own_away), (far_same, far_away))):
                pair = []
                for row in range(2):
                    at = (of * 2 + row) * 2 * tiles
                    low, high = values[at : at + tiles], values[at + tiles : at + 2 * tiles]
                    pair.append(
                        (
                            jnp.where(lane < CORE, low, pltpu.roll(high, CORE, 1)),
                            jnp.where(lane < CORE, pltpu.roll(low, CORE, 1), high),
                        )
                    )
                for line in range(2):
                    same, away = halves(half, pair[0][line], pair[1][line])
                    same_ref[begin + 2 * tile + line] = same.astype(bf16)
                    away_ref[begin + 2 * tile + line] = away.astype(bf16)


def final_kernel(
    place_ref,
    own_same,
    own_away,
    far_same,
    far_away,
    gained_same,
    gained_away,
    fresh_same,
    fresh_away,
    out_ref,
    states_ref,
    cells_ref,
):
    half = place_ref[0]
    side = place_ref[3]
    tiles = out_ref.shape[2] // LANES
    block_rows = out_ref.shape[1] // CORE
    rows = 2 * tiles
    for away, (own, far, gained, fresh) in enumerate(
        ((own_same, far_same, gained_same, fresh_same), (own_away, far_away, gained_away, fresh_away))
    ):
        of = half if away == 0 else 1 - half
        places = (block_rows // 2 - 1 + of, (block_rows - 1) * of)
        for opposite, values in enumerate((own, far)):
            channel = side if opposite == 0 else 1 - side
            cells_ref[...] = values[...].astype(f32).reshape(CORE * rows, LANES)
            for row in range(2):
                for tile in range(tiles):
                    lanes = slice(tile * LANES, (tile + 1) * LANES)
                    placed = cells_ref[pl.ds(row * tiles + tile, CORE, stride=rows), :]
                    at = pl.multiple_of(places[row] * CORE, CORE)
                    out_ref[channel, pl.ds(at, CORE), lanes] = gained[channel, row, :, lanes] + placed
        for row in range(2):
            for column in range(2 * tiles):
                at = (column % 2) * tiles + column // 2
                states_ref[places[row], column : column + 1, :] = fresh[row, at : at + 1, :]


def after(values, *others):
    return lax.optimization_barrier((values,) + others)[0]


def local(field, states, input_weight, recurrent_weight, bias, output_weight, model_gain):
    height, width = field.shape[1:]
    sections = lax.axis_size("col")
    bands = lax.axis_size("row")
    pairs = sections // 2
    block_rows = height // CORE
    tiles = width // LANES
    depth = 4 * PATCH // pairs
    slices = sections // 2
    column = lax.axis_index("col")
    band = lax.axis_index("row")
    half = column % 2
    place = jnp.stack([half, column // 2, column % slices, column // slices, band % 2])

    def across(values):
        return lax.ppermute(values, "col", [(i, i ^ 1) for i in range(sections)])

    def along(values, ahead):
        if ahead % pairs == 0:
            return values
        return lax.ppermute(values, "col", [(i, (i + 2 * ahead) % sections) for i in range(sections)])

    other = across(field)
    (edges,) = call(edges_kernel, [((2, GROUP, LANES), f32)], (place, field), name="edges")
    pattern = [(i, (i + (1 if i % 2 else -1)) % sections) for i in range(sections)]
    edges = lax.ppermute(edges, "col", pattern)
    edges_other = across(after(edges, other))
    side, ends = call(
        ends_kernel,
        [((2, height, LANES), f32), ((2, REACH, 2 * width + LANES), f32)],
        (place, field, other, edges, edges_other),
        name="ends",
    )
    pattern = []
    for item in range(bands):
        for core in range(0, sections, 2):
            pattern.append((item * sections + core, (item - 1) % bands * sections + core + 1))
            pattern.append((item * sections + core + 1, (item + 1) % bands * sections + core))
    ends = lax.ppermute(ends, ("row", "col"), pattern)

    weight_other = across(after(input_weight, edges_other))
    readout_weights = [output_weight, across(after(output_weight, edges_other))]
    part = row_part(place, after(output_weight, edges))
    firsts = [lax.ppermute(part, "col", [(i, i ^ index) for i in range(sections)]) for index in range(2, slices, 2)]

    lines = ((pairs, 2 * tiles, depth, LANES), bf16)
    model = ((2, CORE, 2 * width), f32)
    inner_lines, inner_model = call(
        functools.partial(model_kernel, False),
        [lines, model],
        (place, field, other, side),
        megabytes=8,
        micros=3.3,
        name="inner_model",
    )
    *messages, outer_model = call(
        functools.partial(model_kernel, True),
        [((2, *lines[0][1:]), bf16)] * pairs + [model],
        (place, field, other, side, after(ends, inner_model, weight_other, readout_weights[1]), inner_lines),
        [pltpu.VMEM(*lines), pltpu.VMEM((2, WINDOW, 2 * width + LANES), f32)],
        12,
        3.3,
        name="outer_model",
    )
    messages = lax.optimization_barrier((*messages, *firsts))
    messages, firsts = messages[:pairs], messages[pairs:]
    patches = [along(messages[-ahead % pairs], -ahead) for ahead in range(pairs)]
    gain = jnp.concatenate([model_gain, model_gain], 2)
    gained_same, gained_away = call(
        gain_kernel,
        [((2, 2, CORE, width), f32)] * 2,
        (place, inner_model, outer_model, gain),
        micros=1.0,
        name="gain",
    )
    gained_away = across(gained_away)

    previous = call(
        previous_kernel,
        [((block_rows * tiles, NODES), f32)] * 2,
        (place, after(states, outer_model)),
        micros=0.5,
        name="previous",
    )
    (recur,) = call(
        recur_kernel,
        [((2 * block_rows * tiles, NODES), f32)],
        (place, previous[0], across(after(previous[1], gained_away)), recurrent_weight, bias[None]),
        micros=0.5,
        name="recur",
    )

    recurs = (recur, along(recur, pairs // 2))
    total = pairs * 2 * tiles
    weight_own = after(input_weight, gained_away, *recurs)
    parts = call(
        functools.partial(drive_kernel, pairs),
        [((8 * 2 * tiles, NODES), bf16)] * pairs,
        (place, *patches, weight_own, weight_other),
        [
            pltpu.VMEM((2 * total * depth, LANES), f32),
            pltpu.VMEM((2, 4 * total, -(-depth // 2 * PATCH // LANES) * LANES), bf16),
        ],
        10,
        4.0,
        name="drive",
    )
    for first in firsts:
        second = lax.ppermute(first, "row", [(i, i ^ 1) for i in range(bands)])
        readout_weights += [first, second, across(after(first, parts[0])), across(after(second, parts[0]))]
    parts = [along(part, ahead) for ahead, part in enumerate(parts)]

    fresh_same, fresh_away, own_same, own_away, far_same, far_away = call(
        functools.partial(readout_kernel, pairs, slices),
        [((2, 2 * tiles, NODES), f32)] * 2 + [((CORE, 2 * tiles, LANES), bf16)] * 4,
        (place, *parts, *recurs, *readout_weights),
        megabytes=12,
        micros=2.5,
        name="readout",
    )
    pattern = [(i, ((i + sections // 2) % sections) ^ 1) for i in range(sections)]
    far_same = along(far_same, pairs // 2)
    far_away = lax.ppermute(far_away, "col", pattern)
    own_away = across(own_away)
    fresh_away = across(fresh_away)
    return call(
        final_kernel,
        [((2, height, width), f32), ((block_rows, 2 * tiles, NODES), f32)],
        (place, own_same, own_away, far_same, far_away, gained_same, gained_away, fresh_same, fresh_away),
        [pltpu.VMEM((CORE * 2 * tiles, LANES), f32)],
        4,
        2.0,
        name="final",
    )


def solution(mesh):
    placed = (
        P(None, "row", "col"),
        P("row", "col", None),
        P("col", None),
        P(),
        P(),
        P(None, "col"),
        P(),
    )
    return jax.shard_map(
        local,
        mesh=mesh,
        in_specs=placed,
        out_specs=(P(None, "row", "col"), P("row", "col", None)),
        check_vma=False,
    )
```

time: 111 us -> 90.4 us (0.81)
  waiting for transfers between devices: 55.8 us -> 42.7 us
  local copies, waits for them, and re-layouts: 9.08 us -> 2.58 us
  other arithmetic: 3.07 us -> 0.08 us
  starting transfers between devices: 25 us -> 27.7 us
    ppermute x13 -> x8, waiting for transfers between devices: 48.4 us -> 33.2 us  [along(): lax.ppermute(values, 'col', [(i, (i + 2 * ahead) % sections) for i in ran...]
    unnamed x30 -> x18, local copies, waits for them, and re-layouts: 6.33 us -> 2.5 us
    ppermute x1 -> x3, waiting for transfers between devices: 0.01 us -> 3.76 us  [the longest x1 2.42 us: local(): lax.ppermute(part, 'col', [(i, i ^ index) for i in range(sections)])]
    ppermute x1, waiting for transfers between devices: 3.3 us -> 0.01 us  [local(): ends = lax.ppermute(ends, ('row', 'col'), pattern)]
    dynamic_slice x4 -> x0, local copies, waits for them, and re-layouts: 2.64 us -> none  [the longest x1 1.99 us: own_rows(): return lax.dynamic_slice_in_dim(field, begin, count, 1)]
    select_n x2 -> x0, other arithmetic: 1.9 us -> none  [the longest x1 1.13 us: local(): left_edge = jnp.where(first, mine[:, :, :STAGES], other[:, :, :STAGES])]
    ppermute x8 -> x10, waiting for transfers between devices: 1.06 us -> 2.75 us  [across(): return lax.ppermute(values, 'col', [(i, i ^ 1) for i in range(sections)])]
    ppermute x1 -> x3, starting transfers between devices: 2.43 us -> 4.03 us  [the longest x1 2.75 us: local(): edges = lax.ppermute(edges, 'col', pattern)]
  transfers between devices with their start and end apart: 24 -> 23, of which waited for: 11 -> 10; matrix products, arithmetic and copies ran while one was open for 5% -> 0% of each run, Pallas kernels for 13% -> 14%
where the time goes in v2:
time: 90.4 us; the launch traced here: 90.1 us
  waiting for transfers between devices  42.7 us (47%)
  starting transfers between devices  27.7 us (31%)
  Pallas kernels  16.1 us (18%)
  local copies, waits for them, and re-layouts  2.58 us (3%)
    ppermute x8, waiting for transfers between devices, along(): lax.ppermute(values, 'col', [(i, (i + 2 * ahead) % sections) for i in ran...  33.2 us
    pallas_call x10, Pallas kernels, call(): pl.pallas_call(kernel, out_shape=tuple((jax.ShapeDtypeStruct(*out) for ou...  15.5 us
    ppermute x8, starting transfers between devices, along(): lax.ppermute(values, 'col', [(i, (i + 2 * ahead) % sections) for i in ran...  10.5 us
    ppermute x10, starting transfers between devices, across(): return lax.ppermute(values, 'col', [(i, i ^ 1) for i in range(sections)])  9.13 us
    ppermute x1, waiting for transfers between devices, local(): far_away = lax.ppermute(far_away, 'col', pattern)  2.97 us
    ppermute x1, starting transfers between devices, local(): edges = lax.ppermute(edges, 'col', pattern)  2.75 us
    ppermute x10, waiting for transfers between devices, across(): return lax.ppermute(values, 'col', [(i, i ^ 1) for i in range(sections)])  2.75 us
    ppermute x1, starting transfers between devices, local(): far_away = lax.ppermute(far_away, 'col', pattern)  2.52 us
  transfers between devices with their start and end apart: 23, of which 10 were waited for; matrix products, arithmetic and copies ran while one was open for 0% of the time, Pallas kernels for 14%

profile of v2, /device:TPU:1, one launch (start us, length us, event | category | flops | bytes accessed | tf_op | source)
XLA Modules:
  0.0 90.1 jit_solution(3643078783136089502)
XLA Ops:
  0.8 1.2 %copy-done = f32[2,256,512]{2,1,0:T(8,128)S(1)} copy-done((f32[2,256,512]{2,1,0:T(8,128)S(1)}, f32[2,256,512]{2,1,0:T(8,128)}, u32[]{:S(2)}) %copy-start) | copy-done | bytes 1048600
  2.8 2.7 %collective-permute-start.1 = (f32[2,8,128]{2,1,0:T(8,128)S(1)}, f32[2,8,128]{2,1,0:T(8,128)S(1)}, u32[]{:S(2)}, u32[]{:S(2)}) collective-permute-start(f32[2,8,128]{2,1,0:T(8,128)S(1)} %edges.1), channel_id=1, source_target_pairs={{0,7},{1,2},{2,1},{3,4},{4,3},{5,6},{6,5},{7,0},{8,15},{9,10},{10,... | collective-permute-start | bytes 24584 | tf_op jit(solution)/shard_map/ppermute | solution.py:397
  5.6 1.3 %collective-permute-done.1.outer_ref = f32[2,8,128]{2,1,0:T(8,128)S(1)} collective-permute-done((f32[2,8,128]{2,1,0:T(8,128)S(1)}, f32[2,8,128]{2,1,0:T(8,128)S(1)}, u32[]{:S(2)}, u32[]{:S(2)}) %collective-permute-start.1) | collective-permute-done | bytes 8224 | tf_op jit(solution)/shard_map/ppermute | solution.py:397
  6.9 2.5 %collective-permute-start.2 = (f32[2,8,128]{2,1,0:T(8,128)S(1)}, f32[2,8,128]{2,1,0:T(8,128)S(1)}, u32[]{:S(2)}, u32[]{:S(2)}) collective-permute-start(f32[2,8,128]{2,1,0:T(8,128)S(1)} %collective-permute-done.1.outer_ref), channel_id=1, source_target_pairs={{0,1},{1,0},{2,3},{3,2},{4,5},{5,4},{6,7},{7,6},{8,9},{9,8},{10,11... | collective-permute-start | bytes 24584 | tf_op jit(solution)/shard_map/ppermute | solution.py:387
  10.8 1.2 %copy-done.2 = bf16[512,1024]{1,0:T(8,128)(2,1)S(1)} copy-done((bf16[512,1024]{1,0:T(8,128)(2,1)S(1)}, bf16[512,1024]{1,0:T(8,128)(2,1)}, u32[]{:S(2)}) %copy-start.2) | copy-done | bytes 1048600
  13.4 1.5 %collective-permute-start.3 = (f32[2,8,1152]{2,1,0:T(8,128)S(1)}, f32[2,8,1152]{2,1,0:T(8,128)S(1)}, u32[]{:S(2)}, u32[]{:S(2)}) collective-permute-start(f32[2,8,1152]{2,1,0:T(8,128)S(1)} %get-tuple-element.42), channel_id=1, source_target_pairs={{0,25},{1,8},{2,27},{3,10},{4,29},{5,12},{6,31},{7,14},{8,1},{9,16... | collective-permute-start | bytes 221192 | tf_op jit(solution)/shard_map/ppermute | solution.py:410
  15.0 3.1 %inner_model.1 = (bf16[4,8,72,128]{3,2,1,0:T(8,128)(2,1)S(1)}, f32[2,64,1024]{2,1,0:T(8,128)S(1)}) custom-call(s32[5]{0:T(128)S(1)} %stack.23.place_ref, f32[2,256,512]{2,1,0:T(8,128)S(1)} %copy-done.1, f32[2,256,512]{2,1,0:T(8,128)S(1)} %collective-permute-done.other_ref, f32[2,256,128]{2,1,0:T(8,128)S(1)} %get-tuple-element.41.side_ref), custom_call_target="tpu_custom_call" | custom-call | bytes 12177000 | tf_op jit(solution)/shard_map/inner_model/pallas_call | solution.py:31
  18.3 3.3 %outer_model.1 = (bf16[2,8,72,128]{3,2,1,0:T(8,128)(2,1)S(1)}, bf16[2,8,72,128]{3,2,1,0:T(8,128)(2,1)S(1)}, bf16[2,8,72,128]{3,2,1,0:T(8,128)(2,1)S(1)}, bf16[2,...) custom-call(s32[5]{0:T(128)S(1)} %stack.23.place_ref, f32[2,256,512]{2,1,0:T(8,128)S(1)} %copy-done.1, ...), custom_call_target="tpu_custom_call" | custom-call | bytes 12177000 | tf_op jit(solution)/shard_map/outer_model/pallas_call | solution.py:31
  23.4 2.4 %collective-permute-done.6.refs_8_ = bf16[256,1024]{1,0:T(8,128)(2,1)S(1)} collective-permute-done((bf16[256,1024]{1,0:T(8,128)(2,1)S(1)}, bf16[256,1024]{1,0:T(8,128)(2,1)S(1)}, u32[]{:S(2)}, u32[]{:S(2)}) %collective-permute-start.6) | collective-permute-done | bytes 524320 | tf_op jit(solution)/shard_map/ppermute | solution.py:415
  25.8 1.2 %collective-permute-start.16 = (bf16[256,1024]{1,0:T(8,128)(2,1)S(1)}, bf16[256,1024]{1,0:T(8,128)(2,1)S(1)}, u32[]{:S(2)}, u32[]{:S(2)}) collective-permute-start(bf16[256,1024]{1,0:T(8,128)(2,1)S(1)} %collective-permute-done.6.refs_8_), channel_id=1, source_target_pairs={{0,8},{8,0},{16,24},{24,16},{1,9},{9,1},{17,25},{25,17},{2,10},{10... | collective-permute-start | bytes 1572872 | tf_op jit(solution)/shard_map/ppermute | solution.py:480
  27.0 3.7 %collective-permute-start.7 = (bf16[2,8,72,128]{3,2,1,0:T(8,128)(2,1)S(1)}, bf16[2,8,72,128]{3,2,1,0:T(8,128)(2,1)S(1)}, u32[]{:S(2)}, u32[]{:S(2)}) collective-permute-start(bf16[2,8,72,128]{3,2,1,0:T(8,128)(2,1)S(1)} %get-tuple-element.54), channel_id=1, source_target_pairs={{0,6},{1,7},{2,0},{3,1},{4,2},{5,3},{6,4},{7,5},{8,14},{9,15},{10,... | collective-permute-start | bytes 884744 | tf_op jit(solution)/shard_map/ppermute | solution.py:392
  31.9 1.8 %collective-permute-start.11 = (f32[16,512]{1,0:T(8,128)S(1)}, f32[16,512]{1,0:T(8,128)S(1)}, u32[]{:S(2)}, u32[]{:S(2)}) collective-permute-start(f32[16,512]{1,0:T(8,128)S(1)} %get-tuple-element.62), channel_id=1, source_target_pairs={{0,1},{1,0},{2,3},{3,2},{4,5},{5,4},{6,7},{7,6},{8,9},{9,8},{10,11... | collective-permute-start | bytes 98312 | tf_op jit(solution)/shard_map/ppermute | solution.py:387
  35.3 1.9 %collective-permute-start.12 = (f32[32,512]{1,0:T(8,128)S(1)}, f32[32,512]{1,0:T(8,128)S(1)}, u32[]{:S(2)}, u32[]{:S(2)}) collective-permute-start(f32[32,512]{1,0:T(8,128)S(1)} %recur.1.refs_4_), channel_id=1, source_target_pairs={{0,4},{1,5},{2,6},{3,7},{4,0},{5,1},{6,2},{7,3},{8,12},{9,13},{10,... | collective-permute-start | bytes 196616 | tf_op jit(solution)/shard_map/ppermute | solution.py:392
  37.2 20.8 %collective-permute-done.12.refs_5_ = f32[32,512]{1,0:T(8,128)S(1)} collective-permute-done((f32[32,512]{1,0:T(8,128)S(1)}, f32[32,512]{1,0:T(8,128)S(1)}, u32[]{:S(2)}, u32[]{:S(2)}) %collective-permute-start.12) | collective-permute-done | bytes 65568 | tf_op jit(solution)/shard_map/ppermute | solution.py:392
  58.1 2.3 %drive.1 = (bf16[64,512]{1,0:T(8,128)(2,1)S(1)}, bf16[64,512]{1,0:T(8,128)(2,1)S(1)}, bf16[64,512]{1,0:T(8,128)(2,1)S(1)}, bf16[64,512]{1,0:T(8,128)(2,1)S(1)}) custom-call(s32[5]{0:T(128)S(1)} %stack.23.place_ref, bf16[2,8,72,128]{3,2,1,0:T(8,128)(2,1)S(1)} %get-tuple-element.53.refs_0_, bf16[2,8,72,128]{3,2,1,0:T(8,128)(2,1)S(1)} %collective-permute-done.7.refs_1_, ...), custom_call_target="tpu_custom_call" | custom-call | bytes 14760000 | tf_op jit(solution)/shard_map/drive/pallas_call | solution.py:31
  60.4 1.6 %collective-permute-start.18 = (bf16[256,1024]{1,0:T(8,128)(2,1)S(1)}, bf16[256,1024]{1,0:T(8,128)(2,1)S(1)}, u32[]{:S(2)}, u32[]{:S(2)}) collective-permute-start(bf16[256,1024]{1,0:T(8,128)(2,1)S(1)} %collective-permute-done.16.refs_9_), channel_id=1, source_target_pairs={{0,1},{1,0},{2,3},{3,2},{4,5},{5,4},{6,7},{7,6},{8,9},{9,8},{10,11... | collective-permute-start | bytes 1572872 | tf_op jit(solution)/shard_map/ppermute | solution.py:387
  62.8 3.1 %collective-permute-start.14 = (bf16[64,512]{1,0:T(8,128)(2,1)S(1)}, bf16[64,512]{1,0:T(8,128)(2,1)S(1)}, u32[]{:S(2)}, u32[]{:S(2)}) collective-permute-start(bf16[64,512]{1,0:T(8,128)(2,1)S(1)} %get-tuple-element.66), channel_id=1, source_target_pairs={{0,4},{1,5},{2,6},{3,7},{4,0},{5,1},{6,2},{7,3},{8,12},{9,13},{10,... | collective-permute-start | bytes 196616 | tf_op jit(solution)/shard_map/ppermute | solution.py:392
  66.4 1.4 %collective-permute-done.13.refs_1_ = bf16[64,512]{1,0:T(8,128)(2,1)S(1)} collective-permute-done((bf16[64,512]{1,0:T(8,128)(2,1)S(1)}, bf16[64,512]{1,0:T(8,128)(2,1)S(1)}, u32[]{:S(2)}, u32[]{:S(2)}) %collective-permute-start.13) | collective-permute-done | bytes 65568 | tf_op jit(solution)/shard_map/ppermute | solution.py:392
  67.7 3.3 %collective-permute-done.14.refs_2_ = bf16[64,512]{1,0:T(8,128)(2,1)S(1)} collective-permute-done((bf16[64,512]{1,0:T(8,128)(2,1)S(1)}, bf16[64,512]{1,0:T(8,128)(2,1)S(1)}, u32[]{:S(2)}, u32[]{:S(2)}) %collective-permute-start.14) | collective-permute-done | bytes 65568 | tf_op jit(solution)/shard_map/ppermute | solution.py:392
  71.0 1.5 %readout.1 = (f32[2,8,512]{2,1,0:T(8,128)S(1)}, f32[2,8,512]{2,1,0:T(8,128)S(1)}, bf16[64,8,128]{2,1,0:T(8,128)(2,1)S(1)}, bf16[64,8,128]{2,1,0:T(8,128)(2,1)S(1...) custom-call(s32[5]{0:T(128)S(1)} %stack.23.place_ref, ...), custom_call_target="tpu_custom_call" | custom-call | bytes 9225000 | tf_op jit(solution)/shard_map/readout/pallas_call | solution.py:31
  73.8 2.5 %collective-permute-start.21 = (bf16[64,8,128]{2,1,0:T(8,128)(2,1)S(1)}, bf16[64,8,128]{2,1,0:T(8,128)(2,1)S(1)}, u32[]{:S(2)}, u32[]{:S(2)}) collective-permute-start(bf16[64,8,128]{2,1,0:T(8,128)(2,1)S(1)} %get-tuple-element.74), channel_id=1, source_target_pairs={{0,5},{1,4},{2,7},{3,6},{4,1},{5,0},{6,3},{7,2},{8,13},{9,12},{10,... | collective-permute-start | bytes 393224 | tf_op jit(solution)/shard_map/ppermute | solution.py:494
  77.5 7.8 %collective-permute-done.20.far_same = bf16[64,8,128]{2,1,0:T(8,128)(2,1)S(1)} collective-permute-done((bf16[64,8,128]{2,1,0:T(8,128)(2,1)S(1)}, bf16[64,8,128]{2,1,0:T(8,128)(2,1)S(1)}, u32[]{:S(2)}, u32[]{:S(2)}) %collective-permute-start.20) | collective-permute-done | bytes 131104 | tf_op jit(solution)/shard_map/ppermute | solution.py:392
  85.3 3.0 %collective-permute-done.21.far_away = bf16[64,8,128]{2,1,0:T(8,128)(2,1)S(1)} collective-permute-done((bf16[64,8,128]{2,1,0:T(8,128)(2,1)S(1)}, bf16[64,8,128]{2,1,0:T(8,128)(2,1)S(1)}, u32[]{:S(2)}, u32[]{:S(2)}) %collective-permute-start.21) | collective-permute-done | bytes 131104 | tf_op jit(solution)/shard_map/ppermute | solution.py:494
  88.3 1.8 %final.1 = (f32[2,256,512]{2,1,0:T(8,128)}, f32[4,8,512]{2,1,0:T(8,128)}) custom-call(s32[5]{0:T(128)S(1)} %stack.23.place_ref, bf16[64,8,128]{2,1,0:T(8,128)(2,1)S(1)} %get-tuple-element.71.own_same, bf16[64,8,128]{2,1,0:T(8,128)(2,1)S(1)} %collective-permute-done.19.own_away, bf16[64,8,128]{2,1,0:T(8,128)(2,1)S(1)} %collective-permute-done.20.far_same, ...), custom_call_target="tpu_custom_call" | custom-call | bytes 7380000 | tf_op jit(solution)/shard_map/final/pallas_call | solution.py:31
  (53 shorter events, 12.2 us)
Async XLA Ops:
  0.6 6.3 %collective-permute-start = (f32[2,256,512]{2,1,0:T(8,128)}, f32[2,256,512]{2,1,0:T(8,128)S(1)}, u32[]{:S(2)}, u32[]{:S(2)}) collective-permute-start(f32[2,256,512]{2,1,0:T(8,128)} %field_ref.7), channel_id=1, source_target_pairs={{0,1},{1,0},{2,3},{3,2},{4,5},{5,4},{6,7},{7,6},{8,9},{9,8},{10,11... | collective-permute-start | bytes 3145736 | tf_op jit(solution)/shard_map/ppermute | solution.py:387
  2.8 4.1 %collective-permute-start.1 = (f32[2,8,128]{2,1,0:T(8,128)S(1)}, f32[2,8,128]{2,1,0:T(8,128)S(1)}, u32[]{:S(2)}, u32[]{:S(2)}) collective-permute-start(f32[2,8,128]{2,1,0:T(8,128)S(1)} %edges.1), channel_id=1, source_target_pairs={{0,7},{1,2},{2,1},{3,4},{4,3},{5,6},{6,5},{7,0},{8,15},{9,10},{10,... | collective-permute-start | bytes 24584 | tf_op jit(solution)/shard_map/ppermute | solution.py:397
  6.9 3.3 %collective-permute-start.2 = (f32[2,8,128]{2,1,0:T(8,128)S(1)}, f32[2,8,128]{2,1,0:T(8,128)S(1)}, u32[]{:S(2)}, u32[]{:S(2)}) collective-permute-start(f32[2,8,128]{2,1,0:T(8,128)S(1)} %collective-permute-done.1.outer_ref), channel_id=1, source_target_pairs={{0,1},{1,0},{2,3},{3,2},{4,5},{5,4},{6,7},{7,6},{8,9},{9,8},{10,11... | collective-permute-start | bytes 24584 | tf_op jit(solution)/shard_map/ppermute | solution.py:387
  10.2 8.0 %collective-permute-start.4 = (bf16[2592,512]{1,0:T(8,128)(2,1)}, bf16[2592,512]{1,0:T(8,128)(2,1)S(1)}, u32[]{:S(2)}, u32[]{:S(2)}) collective-permute-start(bf16[2592,512]{1,0:T(8,128)(2,1)} %refs_4_), channel_id=1, source_target_pairs={{0,1},{1,0},{2,3},{3,2},{4,5},{5,4},{6,7},{7,6},{8,9},{9,8},{10,11... | collective-permute-start | bytes 7962632 | tf_op jit(solution)/shard_map/ppermute | solution.py:387
  10.6 7.6 %collective-permute-start.5 = (bf16[512,1024]{1,0:T(8,128)(2,1)}, bf16[512,1024]{1,0:T(8,128)(2,1)S(1)}, u32[]{:S(2)}, u32[]{:S(2)}) collective-permute-start(bf16[512,1024]{1,0:T(8,128)(2,1)} %refs_6_.1), channel_id=1, source_target_pairs={{0,1},{1,0},{2,3},{3,2},{4,5},{5,4},{6,7},{7,6},{8,9},{9,8},{10,11... | collective-permute-start | bytes 3145736 | tf_op jit(solution)/shard_map/ppermute | solution.py:387
  12.6 13.2 %collective-permute-start.6 = (bf16[256,1024]{1,0:T(8,128)(2,1)S(1)}, bf16[256,1024]{1,0:T(8,128)(2,1)S(1)}, u32[]{:S(2)}, u32[]{:S(2)}) collective-permute-start(bf16[256,1024]{1,0:T(8,128)(2,1)S(1)} %part.1), channel_id=1, source_target_pairs={{0,2},{1,3},{2,0},{3,1},{4,6},{5,7},{6,4},{7,5},{8,10},{9,11},{10,... | collective-permute-start | bytes 1572872 | tf_op jit(solution)/shard_map/ppermute | solution.py:415
  13.4 4.8 %collective-permute-start.3 = (f32[2,8,1152]{2,1,0:T(8,128)S(1)}, f32[2,8,1152]{2,1,0:T(8,128)S(1)}, u32[]{:S(2)}, u32[]{:S(2)}) collective-permute-start(f32[2,8,1152]{2,1,0:T(8,128)S(1)} %get-tuple-element.42), channel_id=1, source_target_pairs={{0,25},{1,8},{2,27},{3,10},{4,29},{5,12},{6,31},{7,14},{8,1},{9,16... | collective-permute-start | bytes 221192 | tf_op jit(solution)/shard_map/ppermute | solution.py:410
  18.2 39.8 %copy-start.4 = (bf16[2592,512]{1,0:T(8,128)(2,1)S(1)}, bf16[2592,512]{1,0:T(8,128)(2,1)}, u32[]{:S(2)}) copy-start(bf16[2592,512]{1,0:T(8,128)(2,1)} %refs_4_) | copy-start | bytes 7962628
  22.2 9.7 %collective-permute-start.10 = (f32[2,2,64,512]{3,2,1,0:T(8,128)S(1)}, f32[2,2,64,512]{3,2,1,0:T(8,128)S(1)}, u32[]{:S(2)}, u32[]{:S(2)}) collective-permute-start(f32[2,2,64,512]{3,2,1,0:T(8,128)S(1)} %get-tuple-element.58), channel_id=1, source_target_pairs={{0,1},{1,0},{2,3},{3,2},{4,5},{5,4},{6,7},{7,6},{8,9},{9,8},{10,11... | collective-permute-start | bytes 1572872 | tf_op jit(solution)/shard_map/ppermute | solution.py:387
  25.8 34.6 %collective-permute-start.16 = (bf16[256,1024]{1,0:T(8,128)(2,1)S(1)}, bf16[256,1024]{1,0:T(8,128)(2,1)S(1)}, u32[]{:S(2)}, u32[]{:S(2)}) collective-permute-start(bf16[256,1024]{1,0:T(8,128)(2,1)S(1)} %collective-permute-done.6.refs_8_), channel_id=1, source_target_pairs={{0,8},{8,0},{16,24},{24,16},{1,9},{9,1},{17,25},{25,17},{2,10},{10... | collective-permute-start | bytes 1572872 | tf_op jit(solution)/shard_map/ppermute | solution.py:480
  27.0 31.0 %collective-permute-start.7 = (bf16[2,8,72,128]{3,2,1,0:T(8,128)(2,1)S(1)}, bf16[2,8,72,128]{3,2,1,0:T(8,128)(2,1)S(1)}, u32[]{:S(2)}, u32[]{:S(2)}) collective-permute-start(bf16[2,8,72,128]{3,2,1,0:T(8,128)(2,1)S(1)} %get-tuple-element.54), channel_id=1, source_target_pairs={{0,6},{1,7},{2,0},{3,1},{4,2},{5,3},{6,4},{7,5},{8,14},{9,15},{10,... | collective-permute-start | bytes 884744 | tf_op jit(solution)/shard_map/ppermute | solution.py:392
  30.7 27.4 %collective-permute-start.8 = (bf16[2,8,72,128]{3,2,1,0:T(8,128)(2,1)S(1)}, bf16[2,8,72,128]{3,2,1,0:T(8,128)(2,1)S(1)}, u32[]{:S(2)}, u32[]{:S(2)}) collective-permute-start(bf16[2,8,72,128]{3,2,1,0:T(8,128)(2,1)S(1)} %get-tuple-element.55), channel_id=1, source_target_pairs={{0,4},{1,5},{2,6},{3,7},{4,0},{5,1},{6,2},{7,3},{8,12},{9,13},{10,... | collective-permute-start | bytes 884744 | tf_op jit(solution)/shard_map/ppermute | solution.py:392
  30.7 27.4 %collective-permute-start.9 = (bf16[2,8,72,128]{3,2,1,0:T(8,128)(2,1)S(1)}, bf16[2,8,72,128]{3,2,1,0:T(8,128)(2,1)S(1)}, u32[]{:S(2)}, u32[]{:S(2)}) collective-permute-start(bf16[2,8,72,128]{3,2,1,0:T(8,128)(2,1)S(1)} %get-tuple-element.56), channel_id=1, source_target_pairs={{0,2},{1,3},{2,4},{3,5},{4,6},{5,7},{6,0},{7,1},{8,10},{9,11},{10,... | collective-permute-start | bytes 884744 | tf_op jit(solution)/shard_map/ppermute | solution.py:392
  31.9 2.7 %collective-permute-start.11 = (f32[16,512]{1,0:T(8,128)S(1)}, f32[16,512]{1,0:T(8,128)S(1)}, u32[]{:S(2)}, u32[]{:S(2)}) collective-permute-start(f32[16,512]{1,0:T(8,128)S(1)} %get-tuple-element.62), channel_id=1, source_target_pairs={{0,1},{1,0},{2,3},{3,2},{4,5},{5,4},{6,7},{7,6},{8,9},{9,8},{10,11... | collective-permute-start | bytes 98312 | tf_op jit(solution)/shard_map/ppermute | solution.py:387
  35.3 22.7 %collective-permute-start.12 = (f32[32,512]{1,0:T(8,128)S(1)}, f32[32,512]{1,0:T(8,128)S(1)}, u32[]{:S(2)}, u32[]{:S(2)}) collective-permute-start(f32[32,512]{1,0:T(8,128)S(1)} %recur.1.refs_4_), channel_id=1, source_target_pairs={{0,4},{1,5},{2,6},{3,7},{4,0},{5,1},{6,2},{7,3},{8,12},{9,13},{10,... | collective-permute-start | bytes 196616 | tf_op jit(solution)/shard_map/ppermute | solution.py:392
  60.4 10.6 %collective-permute-start.18 = (bf16[256,1024]{1,0:T(8,128)(2,1)S(1)}, bf16[256,1024]{1,0:T(8,128)(2,1)S(1)}, u32[]{:S(2)}, u32[]{:S(2)}) collective-permute-start(bf16[256,1024]{1,0:T(8,128)(2,1)S(1)} %collective-permute-done.16.refs_9_), channel_id=1, source_target_pairs={{0,1},{1,0},{2,3},{3,2},{4,5},{5,4},{6,7},{7,6},{8,9},{9,8},{10,11... | collective-permute-start | bytes 1572872 | tf_op jit(solution)/shard_map/ppermute | solution.py:387
  62.0 9.1 %collective-permute-start.17 = (bf16[256,1024]{1,0:T(8,128)(2,1)S(1)}, bf16[256,1024]{1,0:T(8,128)(2,1)S(1)}, u32[]{:S(2)}, u32[]{:S(2)}) collective-permute-start(bf16[256,1024]{1,0:T(8,128)(2,1)S(1)} %collective-permute-done.6.refs_8_), channel_id=1, source_target_pairs={{0,1},{1,0},{2,3},{3,2},{4,5},{5,4},{6,7},{7,6},{8,9},{9,8},{10,11... | collective-permute-start | bytes 1572872 | tf_op jit(solution)/shard_map/ppermute | solution.py:387
  62.0 5.7 %collective-permute-start.13 = (bf16[64,512]{1,0:T(8,128)(2,1)S(1)}, bf16[64,512]{1,0:T(8,128)(2,1)S(1)}, u32[]{:S(2)}, u32[]{:S(2)}) collective-permute-start(bf16[64,512]{1,0:T(8,128)(2,1)S(1)} %get-tuple-element.65), channel_id=1, source_target_pairs={{0,2},{1,3},{2,4},{3,5},{4,6},{5,7},{6,0},{7,1},{8,10},{9,11},{10,... | collective-permute-start | bytes 196616 | tf_op jit(solution)/shard_map/ppermute | solution.py:392
  62.8 8.2 %collective-permute-start.14 = (bf16[64,512]{1,0:T(8,128)(2,1)S(1)}, bf16[64,512]{1,0:T(8,128)(2,1)S(1)}, u32[]{:S(2)}, u32[]{:S(2)}) collective-permute-start(bf16[64,512]{1,0:T(8,128)(2,1)S(1)} %get-tuple-element.66), channel_id=1, source_target_pairs={{0,4},{1,5},{2,6},{3,7},{4,0},{5,1},{6,2},{7,3},{8,12},{9,13},{10,... | collective-permute-start | bytes 196616 | tf_op jit(solution)/shard_map/ppermute | solution.py:392
  65.9 5.1 %collective-permute-start.15 = (bf16[64,512]{1,0:T(8,128)(2,1)S(1)}, bf16[64,512]{1,0:T(8,128)(2,1)S(1)}, u32[]{:S(2)}, u32[]{:S(2)}) collective-permute-start(bf16[64,512]{1,0:T(8,128)(2,1)S(1)} %get-tuple-element.67), channel_id=1, source_target_pairs={{0,6},{1,7},{2,0},{3,1},{4,2},{5,3},{6,4},{7,5},{8,14},{9,15},{10,... | collective-permute-start | bytes 196616 | tf_op jit(solution)/shard_map/ppermute | solution.py:392
  72.6 5.0 %collective-permute-start.19 = (bf16[64,8,128]{2,1,0:T(8,128)(2,1)S(1)}, bf16[64,8,128]{2,1,0:T(8,128)(2,1)S(1)}, u32[]{:S(2)}, u32[]{:S(2)}) collective-permute-start(bf16[64,8,128]{2,1,0:T(8,128)(2,1)S(1)} %get-tuple-element.72), channel_id=1, source_target_pairs={{0,1},{1,0},{2,3},{3,2},{4,5},{5,4},{6,7},{7,6},{8,9},{9,8},{10,11... | collective-permute-start | bytes 393224 | tf_op jit(solution)/shard_map/ppermute | solution.py:387
  73.7 11.6 %collective-permute-start.20 = (bf16[64,8,128]{2,1,0:T(8,128)(2,1)S(1)}, bf16[64,8,128]{2,1,0:T(8,128)(2,1)S(1)}, u32[]{:S(2)}, u32[]{:S(2)}) collective-permute-start(bf16[64,8,128]{2,1,0:T(8,128)(2,1)S(1)} %get-tuple-element.73), channel_id=1, source_target_pairs={{0,4},{1,5},{2,6},{3,7},{4,0},{5,1},{6,2},{7,3},{8,12},{9,13},{10,... | collective-permute-start | bytes 393224 | tf_op jit(solution)/shard_map/ppermute | solution.py:392
  73.8 14.5 %collective-permute-start.21 = (bf16[64,8,128]{2,1,0:T(8,128)(2,1)S(1)}, bf16[64,8,128]{2,1,0:T(8,128)(2,1)S(1)}, u32[]{:S(2)}, u32[]{:S(2)}) collective-permute-start(bf16[64,8,128]{2,1,0:T(8,128)(2,1)S(1)} %get-tuple-element.74), channel_id=1, source_target_pairs={{0,5},{1,4},{2,7},{3,6},{4,1},{5,0},{6,3},{7,2},{8,13},{9,12},{10,... | collective-permute-start | bytes 393224 | tf_op jit(solution)/shard_map/ppermute | solution.py:494
  76.3 1.2 %collective-permute-start.22 = (f32[2,8,512]{2,1,0:T(8,128)S(1)}, f32[2,8,512]{2,1,0:T(8,128)S(1)}, u32[]{:S(2)}, u32[]{:S(2)}) collective-permute-start(f32[2,8,512]{2,1,0:T(8,128)S(1)} %get-tuple-element.77), channel_id=1, source_target_pairs={{0,1},{1,0},{2,3},{3,2},{4,5},{5,4},{6,7},{7,6},{8,9},{9,8},{10,11... | collective-permute-start | bytes 98312 | tf_op jit(solution)/shard_map/ppermute | solution.py:387
  (8 other events, 109.0 us)

commit v3 on v2

--- a/solution.py
+++ b/solution.py
@@ -161,7 +161,13 @@
             message_ref[1] = lines_ref[of]
 
 
-def gain_kernel(place_ref, inner_ref, outer_ref, gain_ref, same_ref, away_ref):
+def gain_kernel(place_ref, inner_ref, outer_ref, gain_ref, *refs):
+    count = len(refs) // 2 - 1
+    first_refs, (same_ref, away_ref), quarter_refs = refs[:count], refs[count : count + 2], refs[count + 2 :]
+    for first_ref, quarter_ref in zip(first_refs, quarter_refs):
+        rows = quarter_ref.shape[0]
+        begin = pl.multiple_of(place_ref[4] * (first_ref.shape[0] - rows), rows)
+        quarter_ref[...] = first_ref[pl.ds(begin, rows), :]
     half = place_ref[0]
     width = same_ref.shape[3]
     for channel in range(2):
@@ -227,7 +233,7 @@
 
 def part_kernel(place_ref, weight_ref, out_ref, done):
     rows = out_ref.shape[0]
-    begin = pl.multiple_of(place_ref[4] * rows, rows)
+    begin = pl.multiple_of(place_ref[4] * (weight_ref.shape[0] - rows), LANES)
     copy = pltpu.make_async_copy(weight_ref.at[pl.ds(begin, rows), :], out_ref, done)
     copy.start()
     copy.wait()
@@ -237,8 +243,8 @@
     rows, columns = weight.shape
     return pl.pallas_call(
         part_kernel,
-        out_shape=jax.ShapeDtypeStruct((rows // 2, columns), weight.dtype),
-        in_specs=[SMEM, pl.BlockSpec(memory_space=pl.ANY)],
+        out_shape=jax.ShapeDtypeStruct((rows - rows // 4, columns), weight.dtype),
+        in_specs=[SMEM, pl.BlockSpec(memory_space=pltpu.HBM)],
         out_specs=VMEM,
         scratch_shapes=[pltpu.SemaphoreType.DMA(())],
         compiler_params=pltpu.CompilerParams(vmem_limit_bytes=4 * 2**20),
@@ -278,7 +284,7 @@
     return jnp.where(half == 0, low, high), jnp.where(half == 0, high, low)
 
 
-def readout_kernel(pairs, slices, place_ref, *refs):
+def readout_kernel(pairs, place_ref, *refs):
     parts, recur_refs, weights = refs[:pairs], refs[pairs : pairs + 2], refs[pairs + 2 : -6]
     fresh_same, fresh_away, own_same, own_away, far_same, far_away = refs[-6:]
     half = place_ref[0]
@@ -294,17 +300,17 @@
         fresh_away[row] = away
     readin = fresh.astype(bf16)
     lane = lax.broadcasted_iota(jnp.int32, (tiles, LANES), 1)
-    swapped = place_ref[4] == 1
-    low, high = readin[:, : NODES // 2], readin[:, NODES // 2 :]
-    ordered = (jnp.where(swapped, high, low), jnp.where(swapped, low, high))
-    for index in range(slices):
+    odd = place_ref[4] == 1
+    quarter = NODES // 4
+    most = jnp.where(odd, readin[:, quarter:], readin[:, : NODES - quarter])
+    rest = jnp.where(odd, readin[:, :quarter], readin[:, NODES - quarter :])
+    for index in range(len(weights) // 2 + 1):
         if index < 2:
             products = jnp.dot(readin, weights[index][...], preferred_element_type=f32)
         else:
-            products = sum(
-                jnp.dot(ordered[part], weights[2 * index - 2 + part][...], preferred_element_type=f32)
-                for part in range(2)
-            )
+            head, tail = weights[2 * index - 2 : 2 * index]
+            products = jnp.dot(most, head[...], preferred_element_type=f32)
+            products = products + jnp.dot(rest, tail[...], preferred_element_type=f32)
         lines = products.shape[1] // CORE
         begin = lax.bitwise_xor(place_ref[2], index) * lines
         for tile in range(products.shape[1] // LANES):
@@ -411,8 +417,9 @@
 
     weight_other = across(after(input_weight, edges_other))
     readout_weights = [output_weight, across(after(output_weight, edges_other))]
-    part = row_part(place, after(output_weight, edges))
-    firsts = [lax.ppermute(part, "col", [(i, i ^ index) for i in range(sections)]) for index in range(2, slices, 2)]
+    part = row_part(place, after(output_weight, side))
+    patterns = [[(i, i ^ index) for i in range(sections)] for index in range(2, slices, 2)]
+    firsts = [lax.ppermute(part, "col", pattern) for pattern in patterns]
 
     lines = ((pairs, 2 * tiles, depth, LANES), bf16)
     model = ((2, CORE, 2 * width), f32)
@@ -433,19 +440,7 @@
         3.3,
         name="outer_model",
     )
-    messages = lax.optimization_barrier((*messages, *firsts))
-    messages, firsts = messages[:pairs], messages[pairs:]
     patches = [along(messages[-ahead % pairs], -ahead) for ahead in range(pairs)]
-    gain = jnp.concatenate([model_gain, model_gain], 2)
-    gained_same, gained_away = call(
-        gain_kernel,
-        [((2, 2, CORE, width), f32)] * 2,
-        (place, inner_model, outer_model, gain),
-        micros=1.0,
-        name="gain",
-    )
-    gained_away = across(gained_away)
-
     previous = call(
         previous_kernel,
         [((block_rows * tiles, NODES), f32)] * 2,
@@ -456,14 +451,23 @@
     (recur,) = call(
         recur_kernel,
         [((2 * block_rows * tiles, NODES), f32)],
-        (place, previous[0], across(after(previous[1], gained_away)), recurrent_weight, bias[None]),
+        (place, previous[0], across(previous[1]), recurrent_weight, bias[None]),
         micros=0.5,
         name="recur",
     )
 
+    gain = jnp.concatenate([model_gain, model_gain], 2)
+    gained_same, gained_away, *quarters = call(
+        gain_kernel,
+        [((2, 2, CORE, width), f32)] * 2 + [((NODES // 4, first.shape[1]), bf16) for first in firsts],
+        (place, inner_model, after(outer_model, recur), gain, *firsts),
+        micros=1.0,
+        name="gain",
+    )
     recurs = (recur, along(recur, pairs // 2))
     total = pairs * 2 * tiles
-    weight_own = after(input_weight, gained_away, *recurs)
+    seconds = [lax.ppermute(quarter, "row", [(i, i ^ 1) for i in range(bands)]) for quarter in quarters]
+    weight_own = after(input_weight, gained_same, *recurs, *seconds)
     parts = call(
         functools.partial(drive_kernel, pairs),
         [((8 * 2 * tiles, NODES), bf16)] * pairs,
@@ -476,13 +480,12 @@
         4.0,
         name="drive",
     )
-    for first in firsts:
-        second = lax.ppermute(first, "row", [(i, i ^ 1) for i in range(bands)])
+    parts = [along(part, ahead) for ahead, part in enumerate(parts)]
+    for first, second in zip(firsts, seconds):
         readout_weights += [first, second, across(after(first, parts[0])), across(after(second, parts[0]))]
-    parts = [along(part, ahead) for ahead, part in enumerate(parts)]
 
     fresh_same, fresh_away, own_same, own_away, far_same, far_away = call(
-        functools.partial(readout_kernel, pairs, slices),
+        functools.partial(readout_kernel, pairs),
         [((2, 2 * tiles, NODES), f32)] * 2 + [((CORE, 2 * tiles, LANES), bf16)] * 4,
         (place, *parts, *recurs, *readout_weights),
         megabytes=12,
@@ -494,6 +497,7 @@
     far_away = lax.ppermute(far_away, "col", pattern)
     own_away = across(own_away)
     fresh_away = across(fresh_away)
+    gained_away = across(after(gained_away, own_same))
     return call(
         final_kernel,
         [((2, height, width), f32), ((block_rows, 2 * tiles, NODES), f32)],

time: 90.4 us -> 85.6 us (0.947)
  waiting for transfers between devices: 42.7 us -> 30.1 us
  starting transfers between devices: 27.7 us -> 37 us
  local copies, waits for them, and re-layouts: 2.58 us -> 1.35 us
    ppermute x8, waiting for transfers between devices: 33.2 us -> 20.8 us  [along(): lax.ppermute(values, 'col', [(i, (i + 2 * ahead) % sections) for i in ran...]
    ppermute x8, starting transfers between devices: 10.5 us -> 21.1 us  [along(): lax.ppermute(values, 'col', [(i, (i + 2 * ahead) % sections) for i in ran...]
    ppermute x10, starting transfers between devices: 9.13 us -> 7.76 us  [across(): return lax.ppermute(values, 'col', [(i, i ^ 1) for i in range(sections)])]
    unnamed x18 -> x16, local copies, waits for them, and re-layouts: 2.5 us -> 1.26 us
  transfers between devices with their start and end apart: 23 -> 23, of which waited for: 10 -> 10; matrix products, arithmetic and copies ran while one was open for 0% -> 0% of each run, Pallas kernels for 14% -> 12%
where the time goes in v3:
time: 85.6 us; the launch traced here: 85.5 us
  starting transfers between devices  37 us (43%)
  waiting for transfers between devices  30.1 us (35%)
  Pallas kernels  16.2 us (19%)
  local copies, waits for them, and re-layouts  1.35 us (2%)
    ppermute x8, starting transfers between devices, along(): lax.ppermute(values, 'col', [(i, (i + 2 * ahead) % sections) for i in ran...  21.1 us
    ppermute x8, waiting for transfers between devices, along(): lax.ppermute(values, 'col', [(i, (i + 2 * ahead) % sections) for i in ran...  20.8 us
    pallas_call x10, Pallas kernels, call(): pl.pallas_call(kernel, out_shape=tuple((jax.ShapeDtypeStruct(*out) for ou...  15.5 us
    ppermute x10, starting transfers between devices, across(): return lax.ppermute(values, 'col', [(i, i ^ 1) for i in range(sections)])  7.76 us
    ppermute x1, waiting for transfers between devices, local(): far_away = lax.ppermute(far_away, 'col', pattern)  3.38 us
    ppermute x10, waiting for transfers between devices, across(): return lax.ppermute(values, 'col', [(i, i ^ 1) for i in range(sections)])  2.82 us
    ppermute x1, starting transfers between devices, local(): edges = lax.ppermute(edges, 'col', pattern)  2.75 us
    ppermute x1, starting transfers between devices, local(): far_away = lax.ppermute(far_away, 'col', pattern)  2.54 us
  transfers between devices with their start and end apart: 23, of which 10 were waited for; matrix products, arithmetic and copies ran while one was open for 0% of the time, Pallas kernels for 12%

profile of v3, /device:TPU:1, one launch (start us, length us, event | category | flops | bytes accessed | tf_op | source)
XLA Modules:
  0.0 85.5 jit_solution(8171575687881893395)
XLA Ops:
  0.8 1.2 %copy-done = f32[2,256,512]{2,1,0:T(8,128)S(1)} copy-done((f32[2,256,512]{2,1,0:T(8,128)S(1)}, f32[2,256,512]{2,1,0:T(8,128)}, u32[]{:S(2)}) %copy-start) | copy-done | bytes 1048600
  2.8 2.8 %collective-permute-start.1 = (f32[2,8,128]{2,1,0:T(8,128)S(1)}, f32[2,8,128]{2,1,0:T(8,128)S(1)}, u32[]{:S(2)}, u32[]{:S(2)}) collective-permute-start(f32[2,8,128]{2,1,0:T(8,128)S(1)} %edges.1), channel_id=1, source_target_pairs={{0,7},{1,2},{2,1},{3,4},{4,3},{5,6},{6,5},{7,0},{8,15},{9,10},{10,... | collective-permute-start | bytes 24584 | tf_op jit(solution)/shard_map/ppermute | solution.py:403
  5.6 1.3 %collective-permute-done.1.outer_ref = f32[2,8,128]{2,1,0:T(8,128)S(1)} collective-permute-done((f32[2,8,128]{2,1,0:T(8,128)S(1)}, f32[2,8,128]{2,1,0:T(8,128)S(1)}, u32[]{:S(2)}, u32[]{:S(2)}) %collective-permute-start.1) | collective-permute-done | bytes 8224 | tf_op jit(solution)/shard_map/ppermute | solution.py:403
  6.9 2.5 %collective-permute-start.2 = (f32[2,8,128]{2,1,0:T(8,128)S(1)}, f32[2,8,128]{2,1,0:T(8,128)S(1)}, u32[]{:S(2)}, u32[]{:S(2)}) collective-permute-start(f32[2,8,128]{2,1,0:T(8,128)S(1)} %collective-permute-done.1.outer_ref), channel_id=1, source_target_pairs={{0,1},{1,0},{2,3},{3,2},{4,5},{5,4},{6,7},{7,6},{8,9},{9,8},{10,11... | collective-permute-start | bytes 24584 | tf_op jit(solution)/shard_map/ppermute | solution.py:393
  12.3 1.5 %collective-permute-start.3 = (f32[2,8,1152]{2,1,0:T(8,128)S(1)}, f32[2,8,1152]{2,1,0:T(8,128)S(1)}, u32[]{:S(2)}, u32[]{:S(2)}) collective-permute-start(f32[2,8,1152]{2,1,0:T(8,128)S(1)} %get-tuple-element.39), channel_id=1, source_target_pairs={{0,25},{1,8},{2,27},{3,10},{4,29},{5,12},{6,31},{7,14},{8,1},{9,16... | collective-permute-start | bytes 221192 | tf_op jit(solution)/shard_map/ppermute | solution.py:416
  13.8 3.1 %inner_model.1 = (bf16[4,8,72,128]{3,2,1,0:T(8,128)(2,1)S(1)}, f32[2,64,1024]{2,1,0:T(8,128)S(1)}) custom-call(s32[5]{0:T(128)S(1)} %stack.23.place_ref, f32[2,256,512]{2,1,0:T(8,128)S(1)} %copy-done.1, f32[2,256,512]{2,1,0:T(8,128)S(1)} %collective-permute-done.other_ref, f32[2,256,128]{2,1,0:T(8,128)S(1)} %get-tuple-element.38.side_ref), custom_call_target="tpu_custom_call" | custom-call | bytes 12177000 | tf_op jit(solution)/shard_map/inner_model/pallas_call | solution.py:31
  17.0 3.3 %outer_model.1 = (bf16[2,8,72,128]{3,2,1,0:T(8,128)(2,1)S(1)}, bf16[2,8,72,128]{3,2,1,0:T(8,128)(2,1)S(1)}, bf16[2,8,72,128]{3,2,1,0:T(8,128)(2,1)S(1)}, bf16[2,...) custom-call(s32[5]{0:T(128)S(1)} %stack.23.place_ref, f32[2,256,512]{2,1,0:T(8,128)S(1)} %copy-done.1, ...), custom_call_target="tpu_custom_call" | custom-call | bytes 12177000 | tf_op jit(solution)/shard_map/outer_model/pallas_call | solution.py:31
  20.2 3.5 %collective-permute-start.6 = (bf16[2,8,72,128]{3,2,1,0:T(8,128)(2,1)S(1)}, bf16[2,8,72,128]{3,2,1,0:T(8,128)(2,1)S(1)}, u32[]{:S(2)}, u32[]{:S(2)}) collective-permute-start(bf16[2,8,72,128]{3,2,1,0:T(8,128)(2,1)S(1)} %get-tuple-element.46), channel_id=1, source_target_pairs={{0,6},{1,7},{2,0},{3,1},{4,2},{5,3},{6,4},{7,5},{8,14},{9,15},{10,... | collective-permute-start | bytes 884744 | tf_op jit(solution)/shard_map/ppermute | solution.py:398
  24.2 1.4 %collective-permute-start.8 = (bf16[2,8,72,128]{3,2,1,0:T(8,128)(2,1)S(1)}, bf16[2,8,72,128]{3,2,1,0:T(8,128)(2,1)S(1)}, u32[]{:S(2)}, u32[]{:S(2)}) collective-permute-start(bf16[2,8,72,128]{3,2,1,0:T(8,128)(2,1)S(1)} %get-tuple-element.48), channel_id=1, source_target_pairs={{0,2},{1,3},{2,4},{3,5},{4,6},{5,7},{6,0},{7,1},{8,10},{9,11},{10,... | collective-permute-start | bytes 884744 | tf_op jit(solution)/shard_map/ppermute | solution.py:398
  26.2 1.9 %collective-permute-start.9 = (f32[16,512]{1,0:T(8,128)S(1)}, f32[16,512]{1,0:T(8,128)S(1)}, u32[]{:S(2)}, u32[]{:S(2)}) collective-permute-start(f32[16,512]{1,0:T(8,128)S(1)} %get-tuple-element.52), channel_id=1, source_target_pairs={{0,1},{1,0},{2,3},{3,2},{4,5},{5,4},{6,7},{7,6},{8,9},{9,8},{10,11... | collective-permute-start | bytes 98312 | tf_op jit(solution)/shard_map/ppermute | solution.py:393
  29.7 1.8 %collective-permute-done.10.refs_0_.refs_8_ = bf16[384,1024]{1,0:T(8,128)(2,1)S(1)} collective-permute-done((bf16[384,1024]{1,0:T(8,128)(2,1)S(1)}, bf16[384,1024]{1,0:T(8,128)(2,1)S(1)}, u32[]{:S(2)}, u32[]{:S(2)}) %collective-permute-start.10) | collective-permute-done | bytes 786464 | tf_op jit(solution)/shard_map/ppermute | solution.py:422
  33.4 12.1 %collective-permute-start.11 = (f32[32,512]{1,0:T(8,128)S(1)}, f32[32,512]{1,0:T(8,128)S(1)}, u32[]{:S(2)}, u32[]{:S(2)}) collective-permute-start(f32[32,512]{1,0:T(8,128)S(1)} %recur.1.refs_4_), channel_id=1, source_target_pairs={{0,4},{1,5},{2,6},{3,7},{4,0},{5,1},{6,2},{7,3},{8,12},{9,13},{10,... | collective-permute-start | bytes 196616 | tf_op jit(solution)/shard_map/ppermute | solution.py:398
  45.5 9.9 %collective-permute-done.11.refs_5_ = f32[32,512]{1,0:T(8,128)S(1)} collective-permute-done((f32[32,512]{1,0:T(8,128)S(1)}, f32[32,512]{1,0:T(8,128)S(1)}, u32[]{:S(2)}, u32[]{:S(2)}) %collective-permute-start.11) | collective-permute-done | bytes 65568 | tf_op jit(solution)/shard_map/ppermute | solution.py:398
  55.5 2.3 %drive.1 = (bf16[64,512]{1,0:T(8,128)(2,1)S(1)}, bf16[64,512]{1,0:T(8,128)(2,1)S(1)}, bf16[64,512]{1,0:T(8,128)(2,1)S(1)}, bf16[64,512]{1,0:T(8,128)(2,1)S(1)}) custom-call(s32[5]{0:T(128)S(1)} %stack.23.place_ref, bf16[2,8,72,128]{3,2,1,0:T(8,128)(2,1)S(1)} %get-tuple-element.45.refs_0_, bf16[2,8,72,128]{3,2,1,0:T(8,128)(2,1)S(1)} %collective-permute-done.6.refs_1_, ...), custom_call_target="tpu_custom_call" | custom-call | bytes 14760000 | tf_op jit(solution)/shard_map/drive/pallas_call | solution.py:31
  58.4 1.8 %collective-permute-start.14 = (bf16[64,512]{1,0:T(8,128)(2,1)S(1)}, bf16[64,512]{1,0:T(8,128)(2,1)S(1)}, u32[]{:S(2)}, u32[]{:S(2)}) collective-permute-start(bf16[64,512]{1,0:T(8,128)(2,1)S(1)} %get-tuple-element.60), channel_id=1, source_target_pairs={{0,4},{1,5},{2,6},{3,7},{4,0},{5,1},{6,2},{7,3},{8,12},{9,13},{10,... | collective-permute-start | bytes 196616 | tf_op jit(solution)/shard_map/ppermute | solution.py:398
  60.2 1.5 %collective-permute-start.15 = (bf16[64,512]{1,0:T(8,128)(2,1)S(1)}, bf16[64,512]{1,0:T(8,128)(2,1)S(1)}, u32[]{:S(2)}, u32[]{:S(2)}) collective-permute-start(bf16[64,512]{1,0:T(8,128)(2,1)S(1)} %get-tuple-element.61), channel_id=1, source_target_pairs={{0,6},{1,7},{2,0},{3,1},{4,2},{5,3},{6,4},{7,5},{8,14},{9,15},{10,... | collective-permute-start | bytes 196616 | tf_op jit(solution)/shard_map/ppermute | solution.py:398
  61.7 1.8 %collective-permute-done.13.refs_1_ = bf16[64,512]{1,0:T(8,128)(2,1)S(1)} collective-permute-done((bf16[64,512]{1,0:T(8,128)(2,1)S(1)}, bf16[64,512]{1,0:T(8,128)(2,1)S(1)}, u32[]{:S(2)}, u32[]{:S(2)}) %collective-permute-start.13) | collective-permute-done | bytes 65568 | tf_op jit(solution)/shard_map/ppermute | solution.py:398
  63.5 2.0 %collective-permute-done.15.refs_3_ = bf16[64,512]{1,0:T(8,128)(2,1)S(1)} collective-permute-done((bf16[64,512]{1,0:T(8,128)(2,1)S(1)}, bf16[64,512]{1,0:T(8,128)(2,1)S(1)}, u32[]{:S(2)}, u32[]{:S(2)}) %collective-permute-start.15) | collective-permute-done | bytes 65568 | tf_op jit(solution)/shard_map/ppermute | solution.py:398
  65.5 1.5 %readout.1 = (f32[2,8,512]{2,1,0:T(8,128)S(1)}, f32[2,8,512]{2,1,0:T(8,128)S(1)}, bf16[64,8,128]{2,1,0:T(8,128)(2,1)S(1)}, bf16[64,8,128]{2,1,0:T(8,128)(2,1)S(1...) custom-call(s32[5]{0:T(128)S(1)} %stack.23.place_ref, ...), custom_call_target="tpu_custom_call" | custom-call | bytes 9225000 | tf_op jit(solution)/shard_map/readout/pallas_call | solution.py:31
  67.0 2.0 %collective-permute-start.21 = (f32[2,2,64,512]{3,2,1,0:T(8,128)S(1)}, f32[2,2,64,512]{3,2,1,0:T(8,128)S(1)}, u32[]{:S(2)}, u32[]{:S(2)}) collective-permute-start(f32[2,2,64,512]{3,2,1,0:T(8,128)S(1)} %get-tuple-element.69), channel_id=1, source_target_pairs={{0,1},{1,0},{2,3},{3,2},{4,5},{5,4},{6,7},{7,6},{8,9},{9,8},{10,11... | collective-permute-start | bytes 1572872 | tf_op jit(solution)/shard_map/ppermute | solution.py:393
  69.5 2.5 %collective-permute-start.20 = (bf16[64,8,128]{2,1,0:T(8,128)(2,1)S(1)}, bf16[64,8,128]{2,1,0:T(8,128)(2,1)S(1)}, u32[]{:S(2)}, u32[]{:S(2)}) collective-permute-start(bf16[64,8,128]{2,1,0:T(8,128)(2,1)S(1)} %get-tuple-element.67), channel_id=1, source_target_pairs={{0,5},{1,4},{2,7},{3,6},{4,1},{5,0},{6,3},{7,2},{8,13},{9,12},{10,... | collective-permute-start | bytes 393224 | tf_op jit(solution)/shard_map/ppermute | solution.py:497
  73.3 7.0 %collective-permute-done.19.far_same = bf16[64,8,128]{2,1,0:T(8,128)(2,1)S(1)} collective-permute-done((bf16[64,8,128]{2,1,0:T(8,128)(2,1)S(1)}, bf16[64,8,128]{2,1,0:T(8,128)(2,1)S(1)}, u32[]{:S(2)}, u32[]{:S(2)}) %collective-permute-start.19) | collective-permute-done | bytes 131104 | tf_op jit(solution)/shard_map/ppermute | solution.py:398
  80.3 3.4 %collective-permute-done.20.far_away = bf16[64,8,128]{2,1,0:T(8,128)(2,1)S(1)} collective-permute-done((bf16[64,8,128]{2,1,0:T(8,128)(2,1)S(1)}, bf16[64,8,128]{2,1,0:T(8,128)(2,1)S(1)}, u32[]{:S(2)}, u32[]{:S(2)}) %collective-permute-start.20) | collective-permute-done | bytes 131104 | tf_op jit(solution)/shard_map/ppermute | solution.py:497
  83.7 1.8 %final.1 = (f32[2,256,512]{2,1,0:T(8,128)}, f32[4,8,512]{2,1,0:T(8,128)}) custom-call(s32[5]{0:T(128)S(1)} %stack.23.place_ref, bf16[64,8,128]{2,1,0:T(8,128)(2,1)S(1)} %get-tuple-element.64.own_same, bf16[64,8,128]{2,1,0:T(8,128)(2,1)S(1)} %collective-permute-done.18.own_away, bf16[64,8,128]{2,1,0:T(8,128)(2,1)S(1)} %collective-permute-done.19.far_same, ...), custom_call_target="tpu_custom_call" | custom-call | bytes 7380000 | tf_op jit(solution)/shard_map/final/pallas_call | solution.py:31
  (51 shorter events, 10.6 us)
Async XLA Ops:
  0.6 6.3 %collective-permute-start = (f32[2,256,512]{2,1,0:T(8,128)}, f32[2,256,512]{2,1,0:T(8,128)S(1)}, u32[]{:S(2)}, u32[]{:S(2)}) collective-permute-start(f32[2,256,512]{2,1,0:T(8,128)} %field_ref.7), channel_id=1, source_target_pairs={{0,1},{1,0},{2,3},{3,2},{4,5},{5,4},{6,7},{7,6},{8,9},{9,8},{10,11... | collective-permute-start | bytes 3145736 | tf_op jit(solution)/shard_map/ppermute | solution.py:393
  2.8 4.1 %collective-permute-start.1 = (f32[2,8,128]{2,1,0:T(8,128)S(1)}, f32[2,8,128]{2,1,0:T(8,128)S(1)}, u32[]{:S(2)}, u32[]{:S(2)}) collective-permute-start(f32[2,8,128]{2,1,0:T(8,128)S(1)} %edges.1), channel_id=1, source_target_pairs={{0,7},{1,2},{2,1},{3,4},{4,3},{5,6},{6,5},{7,0},{8,15},{9,10},{10,... | collective-permute-start | bytes 24584 | tf_op jit(solution)/shard_map/ppermute | solution.py:403
  6.9 3.3 %collective-permute-start.2 = (f32[2,8,128]{2,1,0:T(8,128)S(1)}, f32[2,8,128]{2,1,0:T(8,128)S(1)}, u32[]{:S(2)}, u32[]{:S(2)}) collective-permute-start(f32[2,8,128]{2,1,0:T(8,128)S(1)} %collective-permute-done.1.outer_ref), channel_id=1, source_target_pairs={{0,1},{1,0},{2,3},{3,2},{4,5},{5,4},{6,7},{7,6},{8,9},{9,8},{10,11... | collective-permute-start | bytes 24584 | tf_op jit(solution)/shard_map/ppermute | solution.py:393
  10.2 6.7 %collective-permute-start.4 = (bf16[2592,512]{1,0:T(8,128)(2,1)}, bf16[2592,512]{1,0:T(8,128)(2,1)S(1)}, u32[]{:S(2)}, u32[]{:S(2)}) collective-permute-start(bf16[2592,512]{1,0:T(8,128)(2,1)} %refs_4_), channel_id=1, source_target_pairs={{0,1},{1,0},{2,3},{3,2},{4,5},{5,4},{6,7},{7,6},{8,9},{9,8},{10,11... | collective-permute-start | bytes 7962632 | tf_op jit(solution)/shard_map/ppermute | solution.py:393
  10.6 6.3 %collective-permute-start.5 = (bf16[512,1024]{1,0:T(8,128)(2,1)}, bf16[512,1024]{1,0:T(8,128)(2,1)S(1)}, u32[]{:S(2)}, u32[]{:S(2)}) collective-permute-start(bf16[512,1024]{1,0:T(8,128)(2,1)} %refs_6_.1), channel_id=1, source_target_pairs={{0,1},{1,0},{2,3},{3,2},{4,5},{5,4},{6,7},{7,6},{8,9},{9,8},{10,11... | collective-permute-start | bytes 3145736 | tf_op jit(solution)/shard_map/ppermute | solution.py:393
  12.1 19.4 %collective-permute-start.10 = (bf16[384,1024]{1,0:T(8,128)(2,1)S(1)}, bf16[384,1024]{1,0:T(8,128)(2,1)S(1)}, u32[]{:S(2)}, u32[]{:S(2)}) collective-permute-start(bf16[384,1024]{1,0:T(8,128)(2,1)S(1)} %part.1), channel_id=1, source_target_pairs={{0,2},{1,3},{2,0},{3,1},{4,6},{5,7},{6,4},{7,5},{8,10},{9,11},{10,... | collective-permute-start | bytes 2359304 | tf_op jit(solution)/shard_map/ppermute | solution.py:422
  12.3 4.7 %collective-permute-start.3 = (f32[2,8,1152]{2,1,0:T(8,128)S(1)}, f32[2,8,1152]{2,1,0:T(8,128)S(1)}, u32[]{:S(2)}, u32[]{:S(2)}) collective-permute-start(f32[2,8,1152]{2,1,0:T(8,128)S(1)} %get-tuple-element.39), channel_id=1, source_target_pairs={{0,25},{1,8},{2,27},{3,10},{4,29},{5,12},{6,31},{7,14},{8,1},{9,16... | collective-permute-start | bytes 221192 | tf_op jit(solution)/shard_map/ppermute | solution.py:416
  16.9 38.5 %copy-start.3 = (bf16[2592,512]{1,0:T(8,128)(2,1)S(1)}, bf16[2592,512]{1,0:T(8,128)(2,1)}, u32[]{:S(2)}) copy-start(bf16[2592,512]{1,0:T(8,128)(2,1)} %refs_4_) | copy-start | bytes 7962628
  20.2 35.2 %collective-permute-start.6 = (bf16[2,8,72,128]{3,2,1,0:T(8,128)(2,1)S(1)}, bf16[2,8,72,128]{3,2,1,0:T(8,128)(2,1)S(1)}, u32[]{:S(2)}, u32[]{:S(2)}) collective-permute-start(bf16[2,8,72,128]{3,2,1,0:T(8,128)(2,1)S(1)} %get-tuple-element.46), channel_id=1, source_target_pairs={{0,6},{1,7},{2,0},{3,1},{4,2},{5,3},{6,4},{7,5},{8,14},{9,15},{10,... | collective-permute-start | bytes 884744 | tf_op jit(solution)/shard_map/ppermute | solution.py:398
  23.7 31.7 %collective-permute-start.7 = (bf16[2,8,72,128]{3,2,1,0:T(8,128)(2,1)S(1)}, bf16[2,8,72,128]{3,2,1,0:T(8,128)(2,1)S(1)}, u32[]{:S(2)}, u32[]{:S(2)}) collective-permute-start(bf16[2,8,72,128]{3,2,1,0:T(8,128)(2,1)S(1)} %get-tuple-element.47), channel_id=1, source_target_pairs={{0,4},{1,5},{2,6},{3,7},{4,0},{5,1},{6,2},{7,3},{8,12},{9,13},{10,... | collective-permute-start | bytes 884744 | tf_op jit(solution)/shard_map/ppermute | solution.py:398
  24.2 31.2 %collective-permute-start.8 = (bf16[2,8,72,128]{3,2,1,0:T(8,128)(2,1)S(1)}, bf16[2,8,72,128]{3,2,1,0:T(8,128)(2,1)S(1)}, u32[]{:S(2)}, u32[]{:S(2)}) collective-permute-start(bf16[2,8,72,128]{3,2,1,0:T(8,128)(2,1)S(1)} %get-tuple-element.48), channel_id=1, source_target_pairs={{0,2},{1,3},{2,4},{3,5},{4,6},{5,7},{6,0},{7,1},{8,10},{9,11},{10,... | collective-permute-start | bytes 884744 | tf_op jit(solution)/shard_map/ppermute | solution.py:398
  26.2 2.8 %collective-permute-start.9 = (f32[16,512]{1,0:T(8,128)S(1)}, f32[16,512]{1,0:T(8,128)S(1)}, u32[]{:S(2)}, u32[]{:S(2)}) collective-permute-start(f32[16,512]{1,0:T(8,128)S(1)} %get-tuple-element.52), channel_id=1, source_target_pairs={{0,1},{1,0},{2,3},{3,2},{4,5},{5,4},{6,7},{7,6},{8,9},{9,8},{10,11... | collective-permute-start | bytes 98312 | tf_op jit(solution)/shard_map/ppermute | solution.py:393
  32.2 23.2 %collective-permute-start.12 = (bf16[128,1024]{1,0:T(8,128)(2,1)S(1)}, bf16[128,1024]{1,0:T(8,128)(2,1)S(1)}, u32[]{:S(2)}, u32[]{:S(2)}) collective-permute-start(bf16[128,1024]{1,0:T(8,128)(2,1)S(1)} %get-tuple-element.56), channel_id=1, source_target_pairs={{0,8},{8,0},{16,24},{24,16},{1,9},{9,1},{17,25},{25,17},{2,10},{10... | collective-permute-start | bytes 786440 | tf_op jit(solution)/shard_map/ppermute | solution.py:469
  33.4 22.0 %collective-permute-start.11 = (f32[32,512]{1,0:T(8,128)S(1)}, f32[32,512]{1,0:T(8,128)S(1)}, u32[]{:S(2)}, u32[]{:S(2)}) collective-permute-start(f32[32,512]{1,0:T(8,128)S(1)} %recur.1.refs_4_), channel_id=1, source_target_pairs={{0,4},{1,5},{2,6},{3,7},{4,0},{5,1},{6,2},{7,3},{8,12},{9,13},{10,... | collective-permute-start | bytes 196616 | tf_op jit(solution)/shard_map/ppermute | solution.py:398
  57.8 7.7 %collective-permute-start.16 = (bf16[384,1024]{1,0:T(8,128)(2,1)S(1)}, bf16[384,1024]{1,0:T(8,128)(2,1)S(1)}, u32[]{:S(2)}, u32[]{:S(2)}) collective-permute-start(bf16[384,1024]{1,0:T(8,128)(2,1)S(1)} %collective-permute-done.10.refs_0_.refs_8_), channel_id=1, source_target_pairs={{0,1},{1,0},{2,3},{3,2},{4,5},{5,4},{6,7},{7,6},{8,9},{9,8},{10,11... | collective-permute-start | bytes 2359304 | tf_op jit(solution)/shard_map/ppermute | solution.py:393
  58.3 7.2 %collective-permute-start.17 = (bf16[128,1024]{1,0:T(8,128)(2,1)S(1)}, bf16[128,1024]{1,0:T(8,128)(2,1)S(1)}, u32[]{:S(2)}, u32[]{:S(2)}) collective-permute-start(bf16[128,1024]{1,0:T(8,128)(2,1)S(1)} %collective-permute-done.12.refs_9_), channel_id=1, source_target_pairs={{0,1},{1,0},{2,3},{3,2},{4,5},{5,4},{6,7},{7,6},{8,9},{9,8},{10,11... | collective-permute-start | bytes 786440 | tf_op jit(solution)/shard_map/ppermute | solution.py:393
  58.4 5.1 %collective-permute-start.13 = (bf16[64,512]{1,0:T(8,128)(2,1)S(1)}, bf16[64,512]{1,0:T(8,128)(2,1)S(1)}, u32[]{:S(2)}, u32[]{:S(2)}) collective-permute-start(bf16[64,512]{1,0:T(8,128)(2,1)S(1)} %get-tuple-element.59), channel_id=1, source_target_pairs={{0,2},{1,3},{2,4},{3,5},{4,6},{5,7},{6,0},{7,1},{8,10},{9,11},{10,... | collective-permute-start | bytes 196616 | tf_op jit(solution)/shard_map/ppermute | solution.py:398
  58.4 5.1 %collective-permute-start.14 = (bf16[64,512]{1,0:T(8,128)(2,1)S(1)}, bf16[64,512]{1,0:T(8,128)(2,1)S(1)}, u32[]{:S(2)}, u32[]{:S(2)}) collective-permute-start(bf16[64,512]{1,0:T(8,128)(2,1)S(1)} %get-tuple-element.60), channel_id=1, source_target_pairs={{0,4},{1,5},{2,6},{3,7},{4,0},{5,1},{6,2},{7,3},{8,12},{9,13},{10,... | collective-permute-start | bytes 196616 | tf_op jit(solution)/shard_map/ppermute | solution.py:398
  60.2 5.3 %collective-permute-start.15 = (bf16[64,512]{1,0:T(8,128)(2,1)S(1)}, bf16[64,512]{1,0:T(8,128)(2,1)S(1)}, u32[]{:S(2)}, u32[]{:S(2)}) collective-permute-start(bf16[64,512]{1,0:T(8,128)(2,1)S(1)} %get-tuple-element.61), channel_id=1, source_target_pairs={{0,6},{1,7},{2,0},{3,1},{4,2},{5,3},{6,4},{7,5},{8,14},{9,15},{10,... | collective-permute-start | bytes 196616 | tf_op jit(solution)/shard_map/ppermute | solution.py:398
  67.0 16.6 %collective-permute-start.21 = (f32[2,2,64,512]{3,2,1,0:T(8,128)S(1)}, f32[2,2,64,512]{3,2,1,0:T(8,128)S(1)}, u32[]{:S(2)}, u32[]{:S(2)}) collective-permute-start(f32[2,2,64,512]{3,2,1,0:T(8,128)S(1)} %get-tuple-element.69), channel_id=1, source_target_pairs={{0,1},{1,0},{2,3},{3,2},{4,5},{5,4},{6,7},{7,6},{8,9},{9,8},{10,11... | collective-permute-start | bytes 1572872 | tf_op jit(solution)/shard_map/ppermute | solution.py:393
  69.0 4.3 %collective-permute-start.18 = (bf16[64,8,128]{2,1,0:T(8,128)(2,1)S(1)}, bf16[64,8,128]{2,1,0:T(8,128)(2,1)S(1)}, u32[]{:S(2)}, u32[]{:S(2)}) collective-permute-start(bf16[64,8,128]{2,1,0:T(8,128)(2,1)S(1)} %get-tuple-element.65), channel_id=1, source_target_pairs={{0,1},{1,0},{2,3},{3,2},{4,5},{5,4},{6,7},{7,6},{8,9},{9,8},{10,11... | collective-permute-start | bytes 393224 | tf_op jit(solution)/shard_map/ppermute | solution.py:393
  69.1 11.2 %collective-permute-start.19 = (bf16[64,8,128]{2,1,0:T(8,128)(2,1)S(1)}, bf16[64,8,128]{2,1,0:T(8,128)(2,1)S(1)}, u32[]{:S(2)}, u32[]{:S(2)}) collective-permute-start(bf16[64,8,128]{2,1,0:T(8,128)(2,1)S(1)} %get-tuple-element.66), channel_id=1, source_target_pairs={{0,4},{1,5},{2,6},{3,7},{4,0},{5,1},{6,2},{7,3},{8,12},{9,13},{10,... | collective-permute-start | bytes 393224 | tf_op jit(solution)/shard_map/ppermute | solution.py:398
  69.5 14.1 %collective-permute-start.20 = (bf16[64,8,128]{2,1,0:T(8,128)(2,1)S(1)}, bf16[64,8,128]{2,1,0:T(8,128)(2,1)S(1)}, u32[]{:S(2)}, u32[]{:S(2)}) collective-permute-start(bf16[64,8,128]{2,1,0:T(8,128)(2,1)S(1)} %get-tuple-element.67), channel_id=1, source_target_pairs={{0,5},{1,4},{2,7},{3,6},{4,1},{5,0},{6,3},{7,2},{8,13},{9,12},{10,... | collective-permute-start | bytes 393224 | tf_op jit(solution)/shard_map/ppermute | solution.py:497
  72.1 1.2 %collective-permute-start.22 = (f32[2,8,512]{2,1,0:T(8,128)S(1)}, f32[2,8,512]{2,1,0:T(8,128)S(1)}, u32[]{:S(2)}, u32[]{:S(2)}) collective-permute-start(f32[2,8,512]{2,1,0:T(8,128)S(1)} %get-tuple-element.71), channel_id=1, source_target_pairs={{0,1},{1,0},{2,3},{3,2},{4,5},{5,4},{6,7},{7,6},{8,9},{9,8},{10,11... | collective-permute-start | bytes 98312 | tf_op jit(solution)/shard_map/ppermute | solution.py:393
  (7 other events, 85.0 us)

commit v4 on v3

--- a/solution.py
+++ b/solution.py
@@ -122,6 +122,10 @@
         out_ref[channel, :, :width] = low
         out_ref[channel, :, width : 2 * width] = high
         out_ref[channel, :, 2 * width :] = side_ref[channel, pl.ds(at, REACH), :]
+
+
+def upper_first(half, row):
+    return half if row else 1 - half
 
 
 def model_kernel(outer, place_ref, field_ref, other_ref, side_ref, *refs):
@@ -157,8 +161,12 @@
         pairs = len(message_refs)
         for ahead, message_ref in enumerate(message_refs):
             of = lax.rem(place_ref[1] + ahead, pairs)
-            message_ref[0] = inner_ref[of]
-            message_ref[1] = lines_ref[of]
+            for row, source_ref in enumerate((inner_ref, lines_ref)):
+                if message_ref.shape[0] == 1:
+                    at = pl.multiple_of(CORE * upper_first(half, row), CORE)
+                    message_ref[0, :, pl.ds(at, PATCH), :] = source_ref[of]
+                else:
+                    message_ref[row] = source_ref[of]
 
 
 def gain_kernel(place_ref, inner_ref, outer_ref, gain_ref, *refs):
@@ -184,13 +192,14 @@
 def drive_kernel(pairs, place_ref, *refs):
     patch_refs, weight_refs = refs[:pairs], refs[pairs : pairs + 2]
     out_refs, (cells_ref, left_ref) = refs[pairs + 2 : -2], refs[-2:]
-    _, tiles, depth, _ = patch_refs[0].shape
+    kinds, tiles, stride, _ = patch_refs[0].shape
+    depth = PATCH if kinds == 1 else stride
     total = pairs * tiles
-    for row in range(2):
+    for row in range(kinds):
         for pair in range(pairs):
             for tile in range(tiles):
-                at = (row * total + pair * tiles + tile) * depth
-                cells_ref[at : at + depth, :] = patch_refs[pair][row, tile].astype(f32)
+                at = (row * total + pair * tiles + tile) * stride
+                cells_ref[at : at + stride, :] = patch_refs[pair][row, tile].astype(f32)
     lane = lax.broadcasted_iota(jnp.int32, (total, LANES), 1)
     half = place_ref[0]
     lines = depth // 2
@@ -201,7 +210,8 @@
         for row in range(2):
             held = [None, None]
             for line in range(lines):
-                own = cells_ref[pl.ds(row * total * depth + begin + line, total, stride=depth), :]
+                at = CORE * upper_first(half, row) if kinds == 1 else row * total * depth
+                own = cells_ref[pl.ds(at + begin + line, total, stride=stride), :]
                 before = pltpu.roll(own, 1, 0)
                 after = pltpu.roll(own, total - 1, 0)
                 even = jnp.where(lane >= LANES - MARGIN, before, own)
@@ -423,6 +433,7 @@
 
     lines = ((pairs, 2 * tiles, depth, LANES), bf16)
     model = ((2, CORE, 2 * width), f32)
+    message = (1, 2 * tiles, PATCH + CORE, LANES) if depth == PATCH else (2, 2 * tiles, depth, LANES)
     inner_lines, inner_model = call(
         functools.partial(model_kernel, False),
         [lines, model],
@@ -433,7 +444,7 @@
     )
     *messages, outer_model = call(
         functools.partial(model_kernel, True),
-        [((2, *lines[0][1:]), bf16)] * pairs + [model],
+        [(message, bf16)] * pairs + [model],
         (place, field, other, side, after(ends, inner_model, weight_other, readout_weights[1]), inner_lines),
         [pltpu.VMEM(*lines), pltpu.VMEM((2, WINDOW, 2 * width + LANES), f32)],
         12,
@@ -473,7 +484,7 @@
         [((8 * 2 * tiles, NODES), bf16)] * pairs,
         (place, *patches, weight_own, weight_other),
         [
-            pltpu.VMEM((2 * total * depth, LANES), f32),
+            pltpu.VMEM((message[0] * total * message[2], LANES), f32),
             pltpu.VMEM((2, 4 * total, -(-depth // 2 * PATCH // LANES) * LANES), bf16),
         ],
         10,

time: 85.6 us -> 84.6 us (0.988)
  no operation moved by 1% of the time
where the time goes in v4:
time: 84.6 us; the launch traced here: 84.4 us
  starting transfers between devices  36.3 us (43%)
  waiting for transfers between devices  29.8 us (35%)
  Pallas kernels  16.1 us (19%)
  local copies, waits for them, and re-layouts  1.35 us (2%)
    ppermute x8, starting transfers between devices, along(): lax.ppermute(values, 'col', [(i, (i + 2 * ahead) % sections) for i in ran...  20.4 us
    ppermute x8, waiting for transfers between devices, along(): lax.ppermute(values, 'col', [(i, (i + 2 * ahead) % sections) for i in ran...  20.1 us
    pallas_call x10, Pallas kernels, call(): pl.pallas_call(kernel, out_shape=tuple((jax.ShapeDtypeStruct(*out) for ou...  15.5 us
    ppermute x10, starting transfers between devices, across(): return lax.ppermute(values, 'col', [(i, i ^ 1) for i in range(sections)])  7.78 us
    ppermute x1, waiting for transfers between devices, local(): far_away = lax.ppermute(far_away, 'col', pattern)  3.38 us
    ppermute x10, waiting for transfers between devices, across(): return lax.ppermute(values, 'col', [(i, i ^ 1) for i in range(sections)])  2.82 us
    ppermute x1, starting transfers between devices, local(): edges = lax.ppermute(edges, 'col', pattern)  2.75 us
    ppermute x1, starting transfers between devices, local(): far_away = lax.ppermute(far_away, 'col', pattern)  2.54 us
  transfers between devices with their start and end apart: 23, of which 10 were waited for; matrix products, arithmetic and copies ran while one was open for 0% of the time, Pallas kernels for 12%

profile of v4, /device:TPU:1, one launch (start us, length us, event | category | flops | bytes accessed | tf_op | source)
XLA Modules:
  0.0 84.4 jit_solution(13500307580028415406)
XLA Ops:
  0.8 1.2 %copy-done = f32[2,256,512]{2,1,0:T(8,128)S(1)} copy-done((f32[2,256,512]{2,1,0:T(8,128)S(1)}, f32[2,256,512]{2,1,0:T(8,128)}, u32[]{:S(2)}) %copy-start) | copy-done | bytes 1048600
  2.8 2.8 %collective-permute-start.1 = (f32[2,8,128]{2,1,0:T(8,128)S(1)}, f32[2,8,128]{2,1,0:T(8,128)S(1)}, u32[]{:S(2)}, u32[]{:S(2)}) collective-permute-start(f32[2,8,128]{2,1,0:T(8,128)S(1)} %edges.1), channel_id=1, source_target_pairs={{0,7},{1,2},{2,1},{3,4},{4,3},{5,6},{6,5},{7,0},{8,15},{9,10},{10,... | collective-permute-start | bytes 24584 | tf_op jit(solution)/shard_map/ppermute | solution.py:413
  5.6 1.3 %collective-permute-done.1.outer_ref = f32[2,8,128]{2,1,0:T(8,128)S(1)} collective-permute-done((f32[2,8,128]{2,1,0:T(8,128)S(1)}, f32[2,8,128]{2,1,0:T(8,128)S(1)}, u32[]{:S(2)}, u32[]{:S(2)}) %collective-permute-start.1) | collective-permute-done | bytes 8224 | tf_op jit(solution)/shard_map/ppermute | solution.py:413
  6.9 2.5 %collective-permute-start.2 = (f32[2,8,128]{2,1,0:T(8,128)S(1)}, f32[2,8,128]{2,1,0:T(8,128)S(1)}, u32[]{:S(2)}, u32[]{:S(2)}) collective-permute-start(f32[2,8,128]{2,1,0:T(8,128)S(1)} %collective-permute-done.1.outer_ref), channel_id=1, source_target_pairs={{0,1},{1,0},{2,3},{3,2},{4,5},{5,4},{6,7},{7,6},{8,9},{9,8},{10,11... | collective-permute-start | bytes 24584 | tf_op jit(solution)/shard_map/ppermute | solution.py:403
  12.3 1.5 %collective-permute-start.3 = (f32[2,8,1152]{2,1,0:T(8,128)S(1)}, f32[2,8,1152]{2,1,0:T(8,128)S(1)}, u32[]{:S(2)}, u32[]{:S(2)}) collective-permute-start(f32[2,8,1152]{2,1,0:T(8,128)S(1)} %get-tuple-element.39), channel_id=1, source_target_pairs={{0,25},{1,8},{2,27},{3,10},{4,29},{5,12},{6,31},{7,14},{8,1},{9,16... | collective-permute-start | bytes 221192 | tf_op jit(solution)/shard_map/ppermute | solution.py:426
  13.8 3.1 %inner_model.1 = (bf16[4,8,72,128]{3,2,1,0:T(8,128)(2,1)S(1)}, f32[2,64,1024]{2,1,0:T(8,128)S(1)}) custom-call(s32[5]{0:T(128)S(1)} %stack.23.place_ref, f32[2,256,512]{2,1,0:T(8,128)S(1)} %copy-done.1, f32[2,256,512]{2,1,0:T(8,128)S(1)} %collective-permute-done.other_ref, f32[2,256,128]{2,1,0:T(8,128)S(1)} %get-tuple-element.38.side_ref), custom_call_target="tpu_custom_call" | custom-call | bytes 12177000 | tf_op jit(solution)/shard_map/inner_model/pallas_call | solution.py:31
  17.0 3.3 %outer_model.1 = (bf16[1,8,136,128]{3,2,1,0:T(8,128)(2,1)S(1)}, bf16[1,8,136,128]{3,2,1,0:T(8,128)(2,1)S(1)}, bf16[1,8,136,128]{3,2,1,0:T(8,128)(2,1)S(1)}, bf16...) custom-call(s32[5]{0:T(128)S(1)} %stack.23.place_ref, f32[2,256,512]{2,1,0:T(8,128)S(1)} %copy-done.1, ...), custom_call_target="tpu_custom_call" | custom-call | bytes 12177000 | tf_op jit(solution)/shard_map/outer_model/pallas_call | solution.py:31
  20.2 3.5 %collective-permute-start.6 = (bf16[1,8,136,128]{3,2,1,0:T(8,128)(2,1)S(1)}, bf16[1,8,136,128]{3,2,1,0:T(8,128)(2,1)S(1)}, u32[]{:S(2)}, u32[]{:S(2)}) collective-permute-start(bf16[1,8,136,128]{3,2,1,0:T(8,128)(2,1)S(1)} %get-tuple-element.46), channel_id=1, source_target_pairs={{0,6},{1,7},{2,0},{3,1},{4,2},{5,3},{6,4},{7,5},{8,14},{9,15},{10,... | collective-permute-start | bytes 835592 | tf_op jit(solution)/shard_map/ppermute | solution.py:408
  24.2 1.4 %collective-permute-start.8 = (bf16[1,8,136,128]{3,2,1,0:T(8,128)(2,1)S(1)}, bf16[1,8,136,128]{3,2,1,0:T(8,128)(2,1)S(1)}, u32[]{:S(2)}, u32[]{:S(2)}) collective-permute-start(bf16[1,8,136,128]{3,2,1,0:T(8,128)(2,1)S(1)} %get-tuple-element.48), channel_id=1, source_target_pairs={{0,2},{1,3},{2,4},{3,5},{4,6},{5,7},{6,0},{7,1},{8,10},{9,11},{10,... | collective-permute-start | bytes 835592 | tf_op jit(solution)/shard_map/ppermute | solution.py:408
  26.2 1.9 %collective-permute-start.9 = (f32[16,512]{1,0:T(8,128)S(1)}, f32[16,512]{1,0:T(8,128)S(1)}, u32[]{:S(2)}, u32[]{:S(2)}) collective-permute-start(f32[16,512]{1,0:T(8,128)S(1)} %get-tuple-element.52), channel_id=1, source_target_pairs={{0,1},{1,0},{2,3},{3,2},{4,5},{5,4},{6,7},{7,6},{8,9},{9,8},{10,11... | collective-permute-start | bytes 98312 | tf_op jit(solution)/shard_map/ppermute | solution.py:403
  29.7 2.1 %collective-permute-done.10.refs_0_.refs_8_ = bf16[384,1024]{1,0:T(8,128)(2,1)S(1)} collective-permute-done((bf16[384,1024]{1,0:T(8,128)(2,1)S(1)}, bf16[384,1024]{1,0:T(8,128)(2,1)S(1)}, u32[]{:S(2)}, u32[]{:S(2)}) %collective-permute-start.10) | collective-permute-done | bytes 786464 | tf_op jit(solution)/shard_map/ppermute | solution.py:432
  33.7 11.4 %collective-permute-start.11 = (f32[32,512]{1,0:T(8,128)S(1)}, f32[32,512]{1,0:T(8,128)S(1)}, u32[]{:S(2)}, u32[]{:S(2)}) collective-permute-start(f32[32,512]{1,0:T(8,128)S(1)} %recur.1.refs_4_), channel_id=1, source_target_pairs={{0,4},{1,5},{2,6},{3,7},{4,0},{5,1},{6,2},{7,3},{8,12},{9,13},{10,... | collective-permute-start | bytes 196616 | tf_op jit(solution)/shard_map/ppermute | solution.py:408
  45.1 9.2 %collective-permute-done.11.refs_5_ = f32[32,512]{1,0:T(8,128)S(1)} collective-permute-done((f32[32,512]{1,0:T(8,128)S(1)}, f32[32,512]{1,0:T(8,128)S(1)}, u32[]{:S(2)}, u32[]{:S(2)}) %collective-permute-start.11) | collective-permute-done | bytes 65568 | tf_op jit(solution)/shard_map/ppermute | solution.py:408
  54.4 2.3 %drive.1 = (bf16[64,512]{1,0:T(8,128)(2,1)S(1)}, bf16[64,512]{1,0:T(8,128)(2,1)S(1)}, bf16[64,512]{1,0:T(8,128)(2,1)S(1)}, bf16[64,512]{1,0:T(8,128)(2,1)S(1)}) custom-call(s32[5]{0:T(128)S(1)} %stack.23.place_ref, bf16[1,8,136,128]{3,2,1,0:T(8,128)(2,1)S(1)} %get-tuple-element.45.refs_0_, bf16[1,8,136,128]{3,2,1,0:T(8,128)(2,1)S(1)} %collective-permute-done.6.refs_1_, ...), custom_call_target="tpu_custom_call" | custom-call | bytes 14760000 | tf_op jit(solution)/shard_map/drive/pallas_call | solution.py:31
  57.3 1.5 %collective-permute-start.14 = (bf16[64,512]{1,0:T(8,128)(2,1)S(1)}, bf16[64,512]{1,0:T(8,128)(2,1)S(1)}, u32[]{:S(2)}, u32[]{:S(2)}) collective-permute-start(bf16[64,512]{1,0:T(8,128)(2,1)S(1)} %get-tuple-element.60), channel_id=1, source_target_pairs={{0,4},{1,5},{2,6},{3,7},{4,0},{5,1},{6,2},{7,3},{8,12},{9,13},{10,... | collective-permute-start | bytes 196616 | tf_op jit(solution)/shard_map/ppermute | solution.py:408
  58.8 1.8 %collective-permute-start.15 = (bf16[64,512]{1,0:T(8,128)(2,1)S(1)}, bf16[64,512]{1,0:T(8,128)(2,1)S(1)}, u32[]{:S(2)}, u32[]{:S(2)}) collective-permute-start(bf16[64,512]{1,0:T(8,128)(2,1)S(1)} %get-tuple-element.61), channel_id=1, source_target_pairs={{0,6},{1,7},{2,0},{3,1},{4,2},{5,3},{6,4},{7,5},{8,14},{9,15},{10,... | collective-permute-start | bytes 196616 | tf_op jit(solution)/shard_map/ppermute | solution.py:408
  60.6 1.8 %collective-permute-done.13.refs_1_ = bf16[64,512]{1,0:T(8,128)(2,1)S(1)} collective-permute-done((bf16[64,512]{1,0:T(8,128)(2,1)S(1)}, bf16[64,512]{1,0:T(8,128)(2,1)S(1)}, u32[]{:S(2)}, u32[]{:S(2)}) %collective-permute-start.13) | collective-permute-done | bytes 65568 | tf_op jit(solution)/shard_map/ppermute | solution.py:408
  62.4 2.0 %collective-permute-done.15.refs_3_ = bf16[64,512]{1,0:T(8,128)(2,1)S(1)} collective-permute-done((bf16[64,512]{1,0:T(8,128)(2,1)S(1)}, bf16[64,512]{1,0:T(8,128)(2,1)S(1)}, u32[]{:S(2)}, u32[]{:S(2)}) %collective-permute-start.15) | collective-permute-done | bytes 65568 | tf_op jit(solution)/shard_map/ppermute | solution.py:408
  64.5 1.5 %readout.1 = (f32[2,8,512]{2,1,0:T(8,128)S(1)}, f32[2,8,512]{2,1,0:T(8,128)S(1)}, bf16[64,8,128]{2,1,0:T(8,128)(2,1)S(1)}, bf16[64,8,128]{2,1,0:T(8,128)(2,1)S(1...) custom-call(s32[5]{0:T(128)S(1)} %stack.23.place_ref, ...), custom_call_target="tpu_custom_call" | custom-call | bytes 9225000 | tf_op jit(solution)/shard_map/readout/pallas_call | solution.py:31
  66.0 2.0 %collective-permute-start.21 = (f32[2,2,64,512]{3,2,1,0:T(8,128)S(1)}, f32[2,2,64,512]{3,2,1,0:T(8,128)S(1)}, u32[]{:S(2)}, u32[]{:S(2)}) collective-permute-start(f32[2,2,64,512]{3,2,1,0:T(8,128)S(1)} %get-tuple-element.69), channel_id=1, source_target_pairs={{0,1},{1,0},{2,3},{3,2},{4,5},{5,4},{6,7},{7,6},{8,9},{9,8},{10,11... | collective-permute-start | bytes 1572872 | tf_op jit(solution)/shard_map/ppermute | solution.py:403
  68.5 2.5 %collective-permute-start.20 = (bf16[64,8,128]{2,1,0:T(8,128)(2,1)S(1)}, bf16[64,8,128]{2,1,0:T(8,128)(2,1)S(1)}, u32[]{:S(2)}, u32[]{:S(2)}) collective-permute-start(bf16[64,8,128]{2,1,0:T(8,128)(2,1)S(1)} %get-tuple-element.67), channel_id=1, source_target_pairs={{0,5},{1,4},{2,7},{3,6},{4,1},{5,0},{6,3},{7,2},{8,13},{9,12},{10,... | collective-permute-start | bytes 393224 | tf_op jit(solution)/shard_map/ppermute | solution.py:508
  72.2 7.0 %collective-permute-done.19.far_same = bf16[64,8,128]{2,1,0:T(8,128)(2,1)S(1)} collective-permute-done((bf16[64,8,128]{2,1,0:T(8,128)(2,1)S(1)}, bf16[64,8,128]{2,1,0:T(8,128)(2,1)S(1)}, u32[]{:S(2)}, u32[]{:S(2)}) %collective-permute-start.19) | collective-permute-done | bytes 131104 | tf_op jit(solution)/shard_map/ppermute | solution.py:408
  79.2 3.4 %collective-permute-done.20.far_away = bf16[64,8,128]{2,1,0:T(8,128)(2,1)S(1)} collective-permute-done((bf16[64,8,128]{2,1,0:T(8,128)(2,1)S(1)}, bf16[64,8,128]{2,1,0:T(8,128)(2,1)S(1)}, u32[]{:S(2)}, u32[]{:S(2)}) %collective-permute-start.20) | collective-permute-done | bytes 131104 | tf_op jit(solution)/shard_map/ppermute | solution.py:508
  82.6 1.8 %final.1 = (f32[2,256,512]{2,1,0:T(8,128)}, f32[4,8,512]{2,1,0:T(8,128)}) custom-call(s32[5]{0:T(128)S(1)} %stack.23.place_ref, bf16[64,8,128]{2,1,0:T(8,128)(2,1)S(1)} %get-tuple-element.64.own_same, bf16[64,8,128]{2,1,0:T(8,128)(2,1)S(1)} %collective-permute-done.18.own_away, bf16[64,8,128]{2,1,0:T(8,128)(2,1)S(1)} %collective-permute-done.19.far_same, ...), custom_call_target="tpu_custom_call" | custom-call | bytes 7380000 | tf_op jit(solution)/shard_map/final/pallas_call | solution.py:31
  (51 shorter events, 10.6 us)
Async XLA Ops:
  0.6 6.3 %collective-permute-start = (f32[2,256,512]{2,1,0:T(8,128)}, f32[2,256,512]{2,1,0:T(8,128)S(1)}, u32[]{:S(2)}, u32[]{:S(2)}) collective-permute-start(f32[2,256,512]{2,1,0:T(8,128)} %field_ref.7), channel_id=1, source_target_pairs={{0,1},{1,0},{2,3},{3,2},{4,5},{5,4},{6,7},{7,6},{8,9},{9,8},{10,11... | collective-permute-start | bytes 3145736 | tf_op jit(solution)/shard_map/ppermute | solution.py:403
  2.8 4.1 %collective-permute-start.1 = (f32[2,8,128]{2,1,0:T(8,128)S(1)}, f32[2,8,128]{2,1,0:T(8,128)S(1)}, u32[]{:S(2)}, u32[]{:S(2)}) collective-permute-start(f32[2,8,128]{2,1,0:T(8,128)S(1)} %edges.1), channel_id=1, source_target_pairs={{0,7},{1,2},{2,1},{3,4},{4,3},{5,6},{6,5},{7,0},{8,15},{9,10},{10,... | collective-permute-start | bytes 24584 | tf_op jit(solution)/shard_map/ppermute | solution.py:413
  6.9 3.3 %collective-permute-start.2 = (f32[2,8,128]{2,1,0:T(8,128)S(1)}, f32[2,8,128]{2,1,0:T(8,128)S(1)}, u32[]{:S(2)}, u32[]{:S(2)}) collective-permute-start(f32[2,8,128]{2,1,0:T(8,128)S(1)} %collective-permute-done.1.outer_ref), channel_id=1, source_target_pairs={{0,1},{1,0},{2,3},{3,2},{4,5},{5,4},{6,7},{7,6},{8,9},{9,8},{10,11... | collective-permute-start | bytes 24584 | tf_op jit(solution)/shard_map/ppermute | solution.py:403
  10.2 6.7 %collective-permute-start.4 = (bf16[2592,512]{1,0:T(8,128)(2,1)}, bf16[2592,512]{1,0:T(8,128)(2,1)S(1)}, u32[]{:S(2)}, u32[]{:S(2)}) collective-permute-start(bf16[2592,512]{1,0:T(8,128)(2,1)} %refs_4_), channel_id=1, source_target_pairs={{0,1},{1,0},{2,3},{3,2},{4,5},{5,4},{6,7},{7,6},{8,9},{9,8},{10,11... | collective-permute-start | bytes 7962632 | tf_op jit(solution)/shard_map/ppermute | solution.py:403
  10.6 6.3 %collective-permute-start.5 = (bf16[512,1024]{1,0:T(8,128)(2,1)}, bf16[512,1024]{1,0:T(8,128)(2,1)S(1)}, u32[]{:S(2)}, u32[]{:S(2)}) collective-permute-start(bf16[512,1024]{1,0:T(8,128)(2,1)} %refs_6_.1), channel_id=1, source_target_pairs={{0,1},{1,0},{2,3},{3,2},{4,5},{5,4},{6,7},{7,6},{8,9},{9,8},{10,11... | collective-permute-start | bytes 3145736 | tf_op jit(solution)/shard_map/ppermute | solution.py:403
  12.1 19.7 %collective-permute-start.10 = (bf16[384,1024]{1,0:T(8,128)(2,1)S(1)}, bf16[384,1024]{1,0:T(8,128)(2,1)S(1)}, u32[]{:S(2)}, u32[]{:S(2)}) collective-permute-start(bf16[384,1024]{1,0:T(8,128)(2,1)S(1)} %part.1), channel_id=1, source_target_pairs={{0,2},{1,3},{2,0},{3,1},{4,6},{5,7},{6,4},{7,5},{8,10},{9,11},{10,... | collective-permute-start | bytes 2359304 | tf_op jit(solution)/shard_map/ppermute | solution.py:432
  12.3 4.7 %collective-permute-start.3 = (f32[2,8,1152]{2,1,0:T(8,128)S(1)}, f32[2,8,1152]{2,1,0:T(8,128)S(1)}, u32[]{:S(2)}, u32[]{:S(2)}) collective-permute-start(f32[2,8,1152]{2,1,0:T(8,128)S(1)} %get-tuple-element.39), channel_id=1, source_target_pairs={{0,25},{1,8},{2,27},{3,10},{4,29},{5,12},{6,31},{7,14},{8,1},{9,16... | collective-permute-start | bytes 221192 | tf_op jit(solution)/shard_map/ppermute | solution.py:426
  16.9 37.4 %copy-start.3 = (bf16[2592,512]{1,0:T(8,128)(2,1)S(1)}, bf16[2592,512]{1,0:T(8,128)(2,1)}, u32[]{:S(2)}) copy-start(bf16[2592,512]{1,0:T(8,128)(2,1)} %refs_4_) | copy-start | bytes 7962628
  20.2 34.1 %collective-permute-start.6 = (bf16[1,8,136,128]{3,2,1,0:T(8,128)(2,1)S(1)}, bf16[1,8,136,128]{3,2,1,0:T(8,128)(2,1)S(1)}, u32[]{:S(2)}, u32[]{:S(2)}) collective-permute-start(bf16[1,8,136,128]{3,2,1,0:T(8,128)(2,1)S(1)} %get-tuple-element.46), channel_id=1, source_target_pairs={{0,6},{1,7},{2,0},{3,1},{4,2},{5,3},{6,4},{7,5},{8,14},{9,15},{10,... | collective-permute-start | bytes 835592 | tf_op jit(solution)/shard_map/ppermute | solution.py:408
  23.8 30.6 %collective-permute-start.7 = (bf16[1,8,136,128]{3,2,1,0:T(8,128)(2,1)S(1)}, bf16[1,8,136,128]{3,2,1,0:T(8,128)(2,1)S(1)}, u32[]{:S(2)}, u32[]{:S(2)}) collective-permute-start(bf16[1,8,136,128]{3,2,1,0:T(8,128)(2,1)S(1)} %get-tuple-element.47), channel_id=1, source_target_pairs={{0,4},{1,5},{2,6},{3,7},{4,0},{5,1},{6,2},{7,3},{8,12},{9,13},{10,... | collective-permute-start | bytes 835592 | tf_op jit(solution)/shard_map/ppermute | solution.py:408
  24.2 30.2 %collective-permute-start.8 = (bf16[1,8,136,128]{3,2,1,0:T(8,128)(2,1)S(1)}, bf16[1,8,136,128]{3,2,1,0:T(8,128)(2,1)S(1)}, u32[]{:S(2)}, u32[]{:S(2)}) collective-permute-start(bf16[1,8,136,128]{3,2,1,0:T(8,128)(2,1)S(1)} %get-tuple-element.48), channel_id=1, source_target_pairs={{0,2},{1,3},{2,4},{3,5},{4,6},{5,7},{6,0},{7,1},{8,10},{9,11},{10,... | collective-permute-start | bytes 835592 | tf_op jit(solution)/shard_map/ppermute | solution.py:408
  26.2 2.8 %collective-permute-start.9 = (f32[16,512]{1,0:T(8,128)S(1)}, f32[16,512]{1,0:T(8,128)S(1)}, u32[]{:S(2)}, u32[]{:S(2)}) collective-permute-start(f32[16,512]{1,0:T(8,128)S(1)} %get-tuple-element.52), channel_id=1, source_target_pairs={{0,1},{1,0},{2,3},{3,2},{4,5},{5,4},{6,7},{7,6},{8,9},{9,8},{10,11... | collective-permute-start | bytes 98312 | tf_op jit(solution)/shard_map/ppermute | solution.py:403
  32.5 21.8 %collective-permute-start.12 = (bf16[128,1024]{1,0:T(8,128)(2,1)S(1)}, bf16[128,1024]{1,0:T(8,128)(2,1)S(1)}, u32[]{:S(2)}, u32[]{:S(2)}) collective-permute-start(bf16[128,1024]{1,0:T(8,128)(2,1)S(1)} %get-tuple-element.56), channel_id=1, source_target_pairs={{0,8},{8,0},{16,24},{24,16},{1,9},{9,1},{17,25},{25,17},{2,10},{10... | collective-permute-start | bytes 786440 | tf_op jit(solution)/shard_map/ppermute | solution.py:480
  33.7 20.6 %collective-permute-start.11 = (f32[32,512]{1,0:T(8,128)S(1)}, f32[32,512]{1,0:T(8,128)S(1)}, u32[]{:S(2)}, u32[]{:S(2)}) collective-permute-start(f32[32,512]{1,0:T(8,128)S(1)} %recur.1.refs_4_), channel_id=1, source_target_pairs={{0,4},{1,5},{2,6},{3,7},{4,0},{5,1},{6,2},{7,3},{8,12},{9,13},{10,... | collective-permute-start | bytes 196616 | tf_op jit(solution)/shard_map/ppermute | solution.py:408
  56.7 7.8 %collective-permute-start.16 = (bf16[384,1024]{1,0:T(8,128)(2,1)S(1)}, bf16[384,1024]{1,0:T(8,128)(2,1)S(1)}, u32[]{:S(2)}, u32[]{:S(2)}) collective-permute-start(bf16[384,1024]{1,0:T(8,128)(2,1)S(1)} %collective-permute-done.10.refs_0_.refs_8_), channel_id=1, source_target_pairs={{0,1},{1,0},{2,3},{3,2},{4,5},{5,4},{6,7},{7,6},{8,9},{9,8},{10,11... | collective-permute-start | bytes 2359304 | tf_op jit(solution)/shard_map/ppermute | solution.py:403
  57.3 7.2 %collective-permute-start.17 = (bf16[128,1024]{1,0:T(8,128)(2,1)S(1)}, bf16[128,1024]{1,0:T(8,128)(2,1)S(1)}, u32[]{:S(2)}, u32[]{:S(2)}) collective-permute-start(bf16[128,1024]{1,0:T(8,128)(2,1)S(1)} %collective-permute-done.12.refs_9_), channel_id=1, source_target_pairs={{0,1},{1,0},{2,3},{3,2},{4,5},{5,4},{6,7},{7,6},{8,9},{9,8},{10,11... | collective-permute-start | bytes 786440 | tf_op jit(solution)/shard_map/ppermute | solution.py:403
  57.3 5.1 %collective-permute-start.13 = (bf16[64,512]{1,0:T(8,128)(2,1)S(1)}, bf16[64,512]{1,0:T(8,128)(2,1)S(1)}, u32[]{:S(2)}, u32[]{:S(2)}) collective-permute-start(bf16[64,512]{1,0:T(8,128)(2,1)S(1)} %get-tuple-element.59), channel_id=1, source_target_pairs={{0,2},{1,3},{2,4},{3,5},{4,6},{5,7},{6,0},{7,1},{8,10},{9,11},{10,... | collective-permute-start | bytes 196616 | tf_op jit(solution)/shard_map/ppermute | solution.py:408
  57.3 5.1 %collective-permute-start.14 = (bf16[64,512]{1,0:T(8,128)(2,1)S(1)}, bf16[64,512]{1,0:T(8,128)(2,1)S(1)}, u32[]{:S(2)}, u32[]{:S(2)}) collective-permute-start(bf16[64,512]{1,0:T(8,128)(2,1)S(1)} %get-tuple-element.60), channel_id=1, source_target_pairs={{0,4},{1,5},{2,6},{3,7},{4,0},{5,1},{6,2},{7,3},{8,12},{9,13},{10,... | collective-permute-start | bytes 196616 | tf_op jit(solution)/shard_map/ppermute | solution.py:408
  58.8 5.6 %collective-permute-start.15 = (bf16[64,512]{1,0:T(8,128)(2,1)S(1)}, bf16[64,512]{1,0:T(8,128)(2,1)S(1)}, u32[]{:S(2)}, u32[]{:S(2)}) collective-permute-start(bf16[64,512]{1,0:T(8,128)(2,1)S(1)} %get-tuple-element.61), channel_id=1, source_target_pairs={{0,6},{1,7},{2,0},{3,1},{4,2},{5,3},{6,4},{7,5},{8,14},{9,15},{10,... | collective-permute-start | bytes 196616 | tf_op jit(solution)/shard_map/ppermute | solution.py:408
  66.0 16.6 %collective-permute-start.21 = (f32[2,2,64,512]{3,2,1,0:T(8,128)S(1)}, f32[2,2,64,512]{3,2,1,0:T(8,128)S(1)}, u32[]{:S(2)}, u32[]{:S(2)}) collective-permute-start(f32[2,2,64,512]{3,2,1,0:T(8,128)S(1)} %get-tuple-element.69), channel_id=1, source_target_pairs={{0,1},{1,0},{2,3},{3,2},{4,5},{5,4},{6,7},{7,6},{8,9},{9,8},{10,11... | collective-permute-start | bytes 1572872 | tf_op jit(solution)/shard_map/ppermute | solution.py:403
  68.0 4.3 %collective-permute-start.18 = (bf16[64,8,128]{2,1,0:T(8,128)(2,1)S(1)}, bf16[64,8,128]{2,1,0:T(8,128)(2,1)S(1)}, u32[]{:S(2)}, u32[]{:S(2)}) collective-permute-start(bf16[64,8,128]{2,1,0:T(8,128)(2,1)S(1)} %get-tuple-element.65), channel_id=1, source_target_pairs={{0,1},{1,0},{2,3},{3,2},{4,5},{5,4},{6,7},{7,6},{8,9},{9,8},{10,11... | collective-permute-start | bytes 393224 | tf_op jit(solution)/shard_map/ppermute | solution.py:403
  68.1 11.2 %collective-permute-start.19 = (bf16[64,8,128]{2,1,0:T(8,128)(2,1)S(1)}, bf16[64,8,128]{2,1,0:T(8,128)(2,1)S(1)}, u32[]{:S(2)}, u32[]{:S(2)}) collective-permute-start(bf16[64,8,128]{2,1,0:T(8,128)(2,1)S(1)} %get-tuple-element.66), channel_id=1, source_target_pairs={{0,4},{1,5},{2,6},{3,7},{4,0},{5,1},{6,2},{7,3},{8,12},{9,13},{10,... | collective-permute-start | bytes 393224 | tf_op jit(solution)/shard_map/ppermute | solution.py:408
  68.5 14.1 %collective-permute-start.20 = (bf16[64,8,128]{2,1,0:T(8,128)(2,1)S(1)}, bf16[64,8,128]{2,1,0:T(8,128)(2,1)S(1)}, u32[]{:S(2)}, u32[]{:S(2)}) collective-permute-start(bf16[64,8,128]{2,1,0:T(8,128)(2,1)S(1)} %get-tuple-element.67), channel_id=1, source_target_pairs={{0,5},{1,4},{2,7},{3,6},{4,1},{5,0},{6,3},{7,2},{8,13},{9,12},{10,... | collective-permute-start | bytes 393224 | tf_op jit(solution)/shard_map/ppermute | solution.py:508
  71.0 1.2 %collective-permute-start.22 = (f32[2,8,512]{2,1,0:T(8,128)S(1)}, f32[2,8,512]{2,1,0:T(8,128)S(1)}, u32[]{:S(2)}, u32[]{:S(2)}) collective-permute-start(f32[2,8,512]{2,1,0:T(8,128)S(1)} %get-tuple-element.71), channel_id=1, source_target_pairs={{0,1},{1,0},{2,3},{3,2},{4,5},{5,4},{6,7},{7,6},{8,9},{9,8},{10,11... | collective-permute-start | bytes 98312 | tf_op jit(solution)/shard_map/ppermute | solution.py:403
  (7 other events, 85.1 us)

commit v5 on v4

--- a/solution.py
+++ b/solution.py
@@ -190,8 +190,8 @@
 
 
 def drive_kernel(pairs, place_ref, *refs):
-    patch_refs, weight_refs = refs[:pairs], refs[pairs : pairs + 2]
-    out_refs, (cells_ref, left_ref) = refs[pairs + 2 : -2], refs[-2:]
+    patch_refs, weight_refs, recur_ref = refs[:pairs], refs[pairs : pairs + 2], refs[pairs + 2]
+    out_refs, (cells_ref, left_ref) = refs[pairs + 3 : -2], refs[-2:]
     kinds, tiles, stride, _ = patch_refs[0].shape
     depth = PATCH if kinds == 1 else stride
     total = pairs * tiles
@@ -237,7 +237,10 @@
         for of in (pair, (pair + pairs // 2) % pairs):
             for part in range(4):
                 at = part * total + of * tiles
-                pieces.append(sums[at : at + tiles])
+                piece = sums[at : at + tiles]
+                if of == 0:
+                    piece = piece + recur_ref[part * tiles : (part + 1) * tiles, :]
+                pieces.append(piece)
         out_ref[...] = jnp.concatenate(pieces, 0).astype(bf16)
 
 
@@ -295,12 +298,10 @@
 
 
 def readout_kernel(pairs, place_ref, *refs):
-    parts, recur_refs, weights = refs[:pairs], refs[pairs : pairs + 2], refs[pairs + 2 : -6]
+    parts, weights = refs[:pairs], refs[pairs:-6]
     fresh_same, fresh_away, own_same, own_away, far_same, far_away = refs[-6:]
     half = place_ref[0]
-    total = jnp.concatenate([recur_ref[...] for recur_ref in recur_refs], 0)
-    for part in parts:
-        total = total + part[...].astype(f32)
+    total = sum(part[...].astype(f32) for part in parts)
     fresh = jnp.tanh(total)
     tiles = fresh.shape[0] // 8
     for row in range(2):
@@ -475,14 +476,13 @@
         micros=1.0,
         name="gain",
     )
-    recurs = (recur, along(recur, pairs // 2))
     total = pairs * 2 * tiles
     seconds = [lax.ppermute(quarter, "row", [(i, i ^ 1) for i in range(bands)]) for quarter in quarters]
-    weight_own = after(input_weight, gained_same, *recurs, *seconds)
+    weight_own = after(input_weight, gained_same, *seconds)
     parts = call(
         functools.partial(drive_kernel, pairs),
         [((8 * 2 * tiles, NODES), bf16)] * pairs,
-        (place, *patches, weight_own, weight_other),
+        (place, *patches, weight_own, weight_other, recur),
         [
             pltpu.VMEM((message[0] * total * message[2], LANES), f32),
             pltpu.VMEM((2, 4 * total, -(-depth // 2 * PATCH // LANES) * LANES), bf16),
@@ -498,7 +498,7 @@
     fresh_same, fresh_away, own_same, own_away, far_same, far_away = call(
         functools.partial(readout_kernel, pairs),
         [((2, 2 * tiles, NODES), f32)] * 2 + [((CORE, 2 * tiles, LANES), bf16)] * 4,
-        (place, *parts, *recurs, *readout_weights),
+        (place, *parts, *readout_weights),
         megabytes=12,
         micros=2.5,
         name="readout",

time: 84.6 us -> 81.9 us (0.968)
  starting transfers between devices: 36.3 us -> 24.6 us
  waiting for transfers between devices: 29.8 us -> 38.8 us
    ppermute x8 -> x7, starting transfers between devices: 20.4 us -> 8.9 us  [along(): lax.ppermute(values, 'col', [(i, (i + 2 * ahead) % sections) for i in ran...]
    ppermute x8 -> x7, waiting for transfers between devices: 20.1 us -> 24.7 us  [along(): lax.ppermute(values, 'col', [(i, (i + 2 * ahead) % sections) for i in ran...]
    ppermute x1, waiting for transfers between devices: 0.01 us -> 4.36 us  [local(): lax.ppermute(quarter, 'row', [(i, i ^ 1) for i in range(bands)])]
  transfers between devices with their start and end apart: 23 -> 22, of which waited for: 10 -> 12; matrix products, arithmetic and copies ran while one was open for 0% -> 0% of each run, Pallas kernels for 12% -> 13%
where the time goes in v5:
time: 81.9 us; the launch traced here: 81.8 us
  waiting for transfers between devices  38.8 us (47%)
  starting transfers between devices  24.6 us (30%)
  Pallas kernels  16.1 us (20%)
  local copies, waits for them, and re-layouts  1.35 us (2%)
    ppermute x7, waiting for transfers between devices, along(): lax.ppermute(values, 'col', [(i, (i + 2 * ahead) % sections) for i in ran...  24.7 us
    pallas_call x10, Pallas kernels, call(): pl.pallas_call(kernel, out_shape=tuple((jax.ShapeDtypeStruct(*out) for ou...  15.5 us
    ppermute x7, starting transfers between devices, along(): lax.ppermute(values, 'col', [(i, (i + 2 * ahead) % sections) for i in ran...  8.9 us
    ppermute x10, starting transfers between devices, across(): return lax.ppermute(values, 'col', [(i, i ^ 1) for i in range(sections)])  7.47 us
    ppermute x1, waiting for transfers between devices, local(): lax.ppermute(quarter, 'row', [(i, i ^ 1) for i in range(bands)])  4.36 us
    ppermute x1, waiting for transfers between devices, local(): far_away = lax.ppermute(far_away, 'col', pattern)  3.41 us
    ppermute x10, waiting for transfers between devices, across(): return lax.ppermute(values, 'col', [(i, i ^ 1) for i in range(sections)])  2.82 us
    ppermute x1, starting transfers between devices, local(): edges = lax.ppermute(edges, 'col', pattern)  2.75 us
  transfers between devices with their start and end apart: 22, of which 12 were waited for; matrix products, arithmetic and copies ran while one was open for 0% of the time, Pallas kernels for 13%

profile of v5, /device:TPU:1, one launch (start us, length us, event | category | flops | bytes accessed | tf_op | source)
XLA Modules:
  0.0 81.8 jit_solution(16361891129567245627)
XLA Ops:
  0.8 1.2 %copy-done = f32[2,256,512]{2,1,0:T(8,128)S(1)} copy-done((f32[2,256,512]{2,1,0:T(8,128)S(1)}, f32[2,256,512]{2,1,0:T(8,128)}, u32[]{:S(2)}) %copy-start) | copy-done | bytes 1048600
  2.8 2.8 %collective-permute-start.1 = (f32[2,8,128]{2,1,0:T(8,128)S(1)}, f32[2,8,128]{2,1,0:T(8,128)S(1)}, u32[]{:S(2)}, u32[]{:S(2)}) collective-permute-start(f32[2,8,128]{2,1,0:T(8,128)S(1)} %edges.1), channel_id=1, source_target_pairs={{0,7},{1,2},{2,1},{3,4},{4,3},{5,6},{6,5},{7,0},{8,15},{9,10},{10,... | collective-permute-start | bytes 24584 | tf_op jit(solution)/shard_map/ppermute | solution.py:414
  5.6 1.3 %collective-permute-done.1.outer_ref = f32[2,8,128]{2,1,0:T(8,128)S(1)} collective-permute-done((f32[2,8,128]{2,1,0:T(8,128)S(1)}, f32[2,8,128]{2,1,0:T(8,128)S(1)}, u32[]{:S(2)}, u32[]{:S(2)}) %collective-permute-start.1) | collective-permute-done | bytes 8224 | tf_op jit(solution)/shard_map/ppermute | solution.py:414
  6.9 2.5 %collective-permute-start.2 = (f32[2,8,128]{2,1,0:T(8,128)S(1)}, f32[2,8,128]{2,1,0:T(8,128)S(1)}, u32[]{:S(2)}, u32[]{:S(2)}) collective-permute-start(f32[2,8,128]{2,1,0:T(8,128)S(1)} %collective-permute-done.1.outer_ref), channel_id=1, source_target_pairs={{0,1},{1,0},{2,3},{3,2},{4,5},{5,4},{6,7},{7,6},{8,9},{9,8},{10,11... | collective-permute-start | bytes 24584 | tf_op jit(solution)/shard_map/ppermute | solution.py:404
  12.3 1.5 %collective-permute-start.3 = (f32[2,8,1152]{2,1,0:T(8,128)S(1)}, f32[2,8,1152]{2,1,0:T(8,128)S(1)}, u32[]{:S(2)}, u32[]{:S(2)}) collective-permute-start(f32[2,8,1152]{2,1,0:T(8,128)S(1)} %get-tuple-element.39), channel_id=1, source_target_pairs={{0,25},{1,8},{2,27},{3,10},{4,29},{5,12},{6,31},{7,14},{8,1},{9,16... | collective-permute-start | bytes 221192 | tf_op jit(solution)/shard_map/ppermute | solution.py:427
  13.8 3.1 %inner_model.1 = (bf16[4,8,72,128]{3,2,1,0:T(8,128)(2,1)S(1)}, f32[2,64,1024]{2,1,0:T(8,128)S(1)}) custom-call(s32[5]{0:T(128)S(1)} %stack.23.place_ref, f32[2,256,512]{2,1,0:T(8,128)S(1)} %copy-done.1, f32[2,256,512]{2,1,0:T(8,128)S(1)} %collective-permute-done.other_ref, f32[2,256,128]{2,1,0:T(8,128)S(1)} %get-tuple-element.38.side_ref), custom_call_target="tpu_custom_call" | custom-call | bytes 12177000 | tf_op jit(solution)/shard_map/inner_model/pallas_call | solution.py:31
  17.0 3.3 %outer_model.1 = (bf16[1,8,136,128]{3,2,1,0:T(8,128)(2,1)S(1)}, bf16[1,8,136,128]{3,2,1,0:T(8,128)(2,1)S(1)}, bf16[1,8,136,128]{3,2,1,0:T(8,128)(2,1)S(1)}, bf16...) custom-call(s32[5]{0:T(128)S(1)} %stack.23.place_ref, f32[2,256,512]{2,1,0:T(8,128)S(1)} %copy-done.1, ...), custom_call_target="tpu_custom_call" | custom-call | bytes 12177000 | tf_op jit(solution)/shard_map/outer_model/pallas_call | solution.py:31
  20.2 3.5 %collective-permute-start.6 = (bf16[1,8,136,128]{3,2,1,0:T(8,128)(2,1)S(1)}, bf16[1,8,136,128]{3,2,1,0:T(8,128)(2,1)S(1)}, u32[]{:S(2)}, u32[]{:S(2)}) collective-permute-start(bf16[1,8,136,128]{3,2,1,0:T(8,128)(2,1)S(1)} %get-tuple-element.46), channel_id=1, source_target_pairs={{0,6},{1,7},{2,0},{3,1},{4,2},{5,3},{6,4},{7,5},{8,14},{9,15},{10,... | collective-permute-start | bytes 835592 | tf_op jit(solution)/shard_map/ppermute | solution.py:409
  24.2 1.4 %collective-permute-start.8 = (bf16[1,8,136,128]{3,2,1,0:T(8,128)(2,1)S(1)}, bf16[1,8,136,128]{3,2,1,0:T(8,128)(2,1)S(1)}, u32[]{:S(2)}, u32[]{:S(2)}) collective-permute-start(bf16[1,8,136,128]{3,2,1,0:T(8,128)(2,1)S(1)} %get-tuple-element.48), channel_id=1, source_target_pairs={{0,2},{1,3},{2,4},{3,5},{4,6},{5,7},{6,0},{7,1},{8,10},{9,11},{10,... | collective-permute-start | bytes 835592 | tf_op jit(solution)/shard_map/ppermute | solution.py:409
  26.2 1.9 %collective-permute-start.9 = (f32[16,512]{1,0:T(8,128)S(1)}, f32[16,512]{1,0:T(8,128)S(1)}, u32[]{:S(2)}, u32[]{:S(2)}) collective-permute-start(f32[16,512]{1,0:T(8,128)S(1)} %get-tuple-element.52), channel_id=1, source_target_pairs={{0,1},{1,0},{2,3},{3,2},{4,5},{5,4},{6,7},{7,6},{8,9},{9,8},{10,11... | collective-permute-start | bytes 98312 | tf_op jit(solution)/shard_map/ppermute | solution.py:404
  29.7 2.1 %collective-permute-done.10.refs_0_.refs_6_ = bf16[384,1024]{1,0:T(8,128)(2,1)S(1)} collective-permute-done((bf16[384,1024]{1,0:T(8,128)(2,1)S(1)}, bf16[384,1024]{1,0:T(8,128)(2,1)S(1)}, u32[]{:S(2)}, u32[]{:S(2)}) %collective-permute-start.10) | collective-permute-done | bytes 786464 | tf_op jit(solution)/shard_map/ppermute | solution.py:433
  33.7 4.4 %collective-permute-done.11.refs_7_ = bf16[128,1024]{1,0:T(8,128)(2,1)S(1)} collective-permute-done((bf16[128,1024]{1,0:T(8,128)(2,1)S(1)}, bf16[128,1024]{1,0:T(8,128)(2,1)S(1)}, u32[]{:S(2)}, u32[]{:S(2)}) %collective-permute-start.11) | collective-permute-done | bytes 262176 | tf_op jit(solution)/shard_map/ppermute | solution.py:480
  38.1 4.8 %collective-permute-done.6.refs_1_ = bf16[1,8,136,128]{3,2,1,0:T(8,128)(2,1)S(1)} collective-permute-done((bf16[1,8,136,128]{3,2,1,0:T(8,128)(2,1)S(1)}, bf16[1,8,136,128]{3,2,1,0:T(8,128)(2,1)S(1)}, u32[]{:S(2)}, u32[]{:S(2)}) %collective-permute-start.6) | collective-permute-done | bytes 278560 | tf_op jit(solution)/shard_map/ppermute | solution.py:409
  42.9 8.4 %collective-permute-done.8.refs_3_ = bf16[1,8,136,128]{3,2,1,0:T(8,128)(2,1)S(1)} collective-permute-done((bf16[1,8,136,128]{3,2,1,0:T(8,128)(2,1)S(1)}, bf16[1,8,136,128]{3,2,1,0:T(8,128)(2,1)S(1)}, u32[]{:S(2)}, u32[]{:S(2)}) %collective-permute-start.8) | collective-permute-done | bytes 278560 | tf_op jit(solution)/shard_map/ppermute | solution.py:409
  51.3 2.3 %drive.1 = (bf16[64,512]{1,0:T(8,128)(2,1)S(1)}, bf16[64,512]{1,0:T(8,128)(2,1)S(1)}, bf16[64,512]{1,0:T(8,128)(2,1)S(1)}, bf16[64,512]{1,0:T(8,128)(2,1)S(1)}) custom-call(s32[5]{0:T(128)S(1)} %stack.23.place_ref, bf16[1,8,136,128]{3,2,1,0:T(8,128)(2,1)S(1)} %get-tuple-element.45.refs_0_, bf16[1,8,136,128]{3,2,1,0:T(8,128)(2,1)S(1)} %collective-permute-done.6.refs_1_, ...), custom_call_target="tpu_custom_call" | custom-call | bytes 14760000 | tf_op jit(solution)/shard_map/drive/pallas_call | solution.py:31
  54.5 3.0 %collective-permute-start.13 = (bf16[64,512]{1,0:T(8,128)(2,1)S(1)}, bf16[64,512]{1,0:T(8,128)(2,1)S(1)}, u32[]{:S(2)}, u32[]{:S(2)}) collective-permute-start(bf16[64,512]{1,0:T(8,128)(2,1)S(1)} %get-tuple-element.60), channel_id=1, source_target_pairs={{0,4},{1,5},{2,6},{3,7},{4,0},{5,1},{6,2},{7,3},{8,12},{9,13},{10,... | collective-permute-start | bytes 196616 | tf_op jit(solution)/shard_map/ppermute | solution.py:409
  57.8 1.8 %collective-permute-done.12.refs_1_ = bf16[64,512]{1,0:T(8,128)(2,1)S(1)} collective-permute-done((bf16[64,512]{1,0:T(8,128)(2,1)S(1)}, bf16[64,512]{1,0:T(8,128)(2,1)S(1)}, u32[]{:S(2)}, u32[]{:S(2)}) %collective-permute-start.12) | collective-permute-done | bytes 65568 | tf_op jit(solution)/shard_map/ppermute | solution.py:409
  59.5 2.8 %collective-permute-done.13.refs_2_ = bf16[64,512]{1,0:T(8,128)(2,1)S(1)} collective-permute-done((bf16[64,512]{1,0:T(8,128)(2,1)S(1)}, bf16[64,512]{1,0:T(8,128)(2,1)S(1)}, u32[]{:S(2)}, u32[]{:S(2)}) %collective-permute-start.13) | collective-permute-done | bytes 65568 | tf_op jit(solution)/shard_map/ppermute | solution.py:409
  62.3 1.5 %readout.1 = (f32[2,8,512]{2,1,0:T(8,128)S(1)}, f32[2,8,512]{2,1,0:T(8,128)S(1)}, bf16[64,8,128]{2,1,0:T(8,128)(2,1)S(1)}, bf16[64,8,128]{2,1,0:T(8,128)(2,1)S(1...) custom-call(s32[5]{0:T(128)S(1)} %stack.23.place_ref, ...), custom_call_target="tpu_custom_call" | custom-call | bytes 9225000 | tf_op jit(solution)/shard_map/readout/pallas_call | solution.py:31
  63.9 1.4 %collective-permute-start.20 = (f32[2,2,64,512]{3,2,1,0:T(8,128)S(1)}, f32[2,2,64,512]{3,2,1,0:T(8,128)S(1)}, u32[]{:S(2)}, u32[]{:S(2)}) collective-permute-start(f32[2,2,64,512]{3,2,1,0:T(8,128)S(1)} %get-tuple-element.69), channel_id=1, source_target_pairs={{0,1},{1,0},{2,3},{3,2},{4,5},{5,4},{6,7},{7,6},{8,9},{9,8},{10,11... | collective-permute-start | bytes 1572872 | tf_op jit(solution)/shard_map/ppermute | solution.py:404
  65.7 2.7 %collective-permute-start.19 = (bf16[64,8,128]{2,1,0:T(8,128)(2,1)S(1)}, bf16[64,8,128]{2,1,0:T(8,128)(2,1)S(1)}, u32[]{:S(2)}, u32[]{:S(2)}) collective-permute-start(bf16[64,8,128]{2,1,0:T(8,128)(2,1)S(1)} %get-tuple-element.67), channel_id=1, source_target_pairs={{0,5},{1,4},{2,7},{3,6},{4,1},{5,0},{6,3},{7,2},{8,13},{9,12},{10,... | collective-permute-start | bytes 393224 | tf_op jit(solution)/shard_map/ppermute | solution.py:508
  69.6 7.0 %collective-permute-done.18.far_same = bf16[64,8,128]{2,1,0:T(8,128)(2,1)S(1)} collective-permute-done((bf16[64,8,128]{2,1,0:T(8,128)(2,1)S(1)}, bf16[64,8,128]{2,1,0:T(8,128)(2,1)S(1)}, u32[]{:S(2)}, u32[]{:S(2)}) %collective-permute-start.18) | collective-permute-done | bytes 131104 | tf_op jit(solution)/shard_map/ppermute | solution.py:409
  76.5 3.4 %collective-permute-done.19.far_away = bf16[64,8,128]{2,1,0:T(8,128)(2,1)S(1)} collective-permute-done((bf16[64,8,128]{2,1,0:T(8,128)(2,1)S(1)}, bf16[64,8,128]{2,1,0:T(8,128)(2,1)S(1)}, u32[]{:S(2)}, u32[]{:S(2)}) %collective-permute-start.19) | collective-permute-done | bytes 131104 | tf_op jit(solution)/shard_map/ppermute | solution.py:508
  79.9 1.8 %final.1 = (f32[2,256,512]{2,1,0:T(8,128)}, f32[4,8,512]{2,1,0:T(8,128)}) custom-call(s32[5]{0:T(128)S(1)} %stack.23.place_ref, bf16[64,8,128]{2,1,0:T(8,128)(2,1)S(1)} %get-tuple-element.64.own_same, bf16[64,8,128]{2,1,0:T(8,128)(2,1)S(1)} %collective-permute-done.17.own_away, bf16[64,8,128]{2,1,0:T(8,128)(2,1)S(1)} %collective-permute-done.18.far_same, ...), custom_call_target="tpu_custom_call" | custom-call | bytes 7380000 | tf_op jit(solution)/shard_map/final/pallas_call | solution.py:31
  (49 shorter events, 11.0 us)
Async XLA Ops:
  0.6 6.3 %collective-permute-start = (f32[2,256,512]{2,1,0:T(8,128)}, f32[2,256,512]{2,1,0:T(8,128)S(1)}, u32[]{:S(2)}, u32[]{:S(2)}) collective-permute-start(f32[2,256,512]{2,1,0:T(8,128)} %field_ref.7), channel_id=1, source_target_pairs={{0,1},{1,0},{2,3},{3,2},{4,5},{5,4},{6,7},{7,6},{8,9},{9,8},{10,11... | collective-permute-start | bytes 3145736 | tf_op jit(solution)/shard_map/ppermute | solution.py:404
  2.8 4.1 %collective-permute-start.1 = (f32[2,8,128]{2,1,0:T(8,128)S(1)}, f32[2,8,128]{2,1,0:T(8,128)S(1)}, u32[]{:S(2)}, u32[]{:S(2)}) collective-permute-start(f32[2,8,128]{2,1,0:T(8,128)S(1)} %edges.1), channel_id=1, source_target_pairs={{0,7},{1,2},{2,1},{3,4},{4,3},{5,6},{6,5},{7,0},{8,15},{9,10},{10,... | collective-permute-start | bytes 24584 | tf_op jit(solution)/shard_map/ppermute | solution.py:414
  6.9 3.3 %collective-permute-start.2 = (f32[2,8,128]{2,1,0:T(8,128)S(1)}, f32[2,8,128]{2,1,0:T(8,128)S(1)}, u32[]{:S(2)}, u32[]{:S(2)}) collective-permute-start(f32[2,8,128]{2,1,0:T(8,128)S(1)} %collective-permute-done.1.outer_ref), channel_id=1, source_target_pairs={{0,1},{1,0},{2,3},{3,2},{4,5},{5,4},{6,7},{7,6},{8,9},{9,8},{10,11... | collective-permute-start | bytes 24584 | tf_op jit(solution)/shard_map/ppermute | solution.py:404
  10.2 6.7 %collective-permute-start.4 = (bf16[2592,512]{1,0:T(8,128)(2,1)}, bf16[2592,512]{1,0:T(8,128)(2,1)S(1)}, u32[]{:S(2)}, u32[]{:S(2)}) collective-permute-start(bf16[2592,512]{1,0:T(8,128)(2,1)} %refs_4_.1), channel_id=1, source_target_pairs={{0,1},{1,0},{2,3},{3,2},{4,5},{5,4},{6,7},{7,6},{8,9},{9,8},{10,11... | collective-permute-start | bytes 7962632 | tf_op jit(solution)/shard_map/ppermute | solution.py:404
  10.6 6.3 %collective-permute-start.5 = (bf16[512,1024]{1,0:T(8,128)(2,1)}, bf16[512,1024]{1,0:T(8,128)(2,1)S(1)}, u32[]{:S(2)}, u32[]{:S(2)}) collective-permute-start(bf16[512,1024]{1,0:T(8,128)(2,1)} %refs_4_.2), channel_id=1, source_target_pairs={{0,1},{1,0},{2,3},{3,2},{4,5},{5,4},{6,7},{7,6},{8,9},{9,8},{10,11... | collective-permute-start | bytes 3145736 | tf_op jit(solution)/shard_map/ppermute | solution.py:404
  12.1 19.7 %collective-permute-start.10 = (bf16[384,1024]{1,0:T(8,128)(2,1)S(1)}, bf16[384,1024]{1,0:T(8,128)(2,1)S(1)}, u32[]{:S(2)}, u32[]{:S(2)}) collective-permute-start(bf16[384,1024]{1,0:T(8,128)(2,1)S(1)} %part.1), channel_id=1, source_target_pairs={{0,2},{1,3},{2,0},{3,1},{4,6},{5,7},{6,4},{7,5},{8,10},{9,11},{10,... | collective-permute-start | bytes 2359304 | tf_op jit(solution)/shard_map/ppermute | solution.py:433
  12.2 16.7 %copy-start.4 = (bf16[512,512]{1,0:T(8,128)(2,1)S(1)}, bf16[512,512]{1,0:T(8,128)(2,1)}, u32[]{:S(2)}) copy-start(bf16[512,512]{1,0:T(8,128)(2,1)} %weight_ref.1) | copy-start | bytes 1572868
  12.3 4.7 %collective-permute-start.3 = (f32[2,8,1152]{2,1,0:T(8,128)S(1)}, f32[2,8,1152]{2,1,0:T(8,128)S(1)}, u32[]{:S(2)}, u32[]{:S(2)}) collective-permute-start(f32[2,8,1152]{2,1,0:T(8,128)S(1)} %get-tuple-element.39), channel_id=1, source_target_pairs={{0,25},{1,8},{2,27},{3,10},{4,29},{5,12},{6,31},{7,14},{8,1},{9,16... | collective-permute-start | bytes 221192 | tf_op jit(solution)/shard_map/ppermute | solution.py:427
  16.9 34.4 %copy-start.3 = (bf16[2592,512]{1,0:T(8,128)(2,1)S(1)}, bf16[2592,512]{1,0:T(8,128)(2,1)}, u32[]{:S(2)}) copy-start(bf16[2592,512]{1,0:T(8,128)(2,1)} %refs_4_.1) | copy-start | bytes 7962628
  20.2 22.7 %collective-permute-start.6 = (bf16[1,8,136,128]{3,2,1,0:T(8,128)(2,1)S(1)}, bf16[1,8,136,128]{3,2,1,0:T(8,128)(2,1)S(1)}, u32[]{:S(2)}, u32[]{:S(2)}) collective-permute-start(bf16[1,8,136,128]{3,2,1,0:T(8,128)(2,1)S(1)} %get-tuple-element.46), channel_id=1, source_target_pairs={{0,6},{1,7},{2,0},{3,1},{4,2},{5,3},{6,4},{7,5},{8,14},{9,15},{10,... | collective-permute-start | bytes 835592 | tf_op jit(solution)/shard_map/ppermute | solution.py:409
  23.8 19.2 %collective-permute-start.7 = (bf16[1,8,136,128]{3,2,1,0:T(8,128)(2,1)S(1)}, bf16[1,8,136,128]{3,2,1,0:T(8,128)(2,1)S(1)}, u32[]{:S(2)}, u32[]{:S(2)}) collective-permute-start(bf16[1,8,136,128]{3,2,1,0:T(8,128)(2,1)S(1)} %get-tuple-element.47), channel_id=1, source_target_pairs={{0,4},{1,5},{2,6},{3,7},{4,0},{5,1},{6,2},{7,3},{8,12},{9,13},{10,... | collective-permute-start | bytes 835592 | tf_op jit(solution)/shard_map/ppermute | solution.py:409
  24.2 27.1 %collective-permute-start.8 = (bf16[1,8,136,128]{3,2,1,0:T(8,128)(2,1)S(1)}, bf16[1,8,136,128]{3,2,1,0:T(8,128)(2,1)S(1)}, u32[]{:S(2)}, u32[]{:S(2)}) collective-permute-start(bf16[1,8,136,128]{3,2,1,0:T(8,128)(2,1)S(1)} %get-tuple-element.48), channel_id=1, source_target_pairs={{0,2},{1,3},{2,4},{3,5},{4,6},{5,7},{6,0},{7,1},{8,10},{9,11},{10,... | collective-permute-start | bytes 835592 | tf_op jit(solution)/shard_map/ppermute | solution.py:409
  26.2 2.8 %collective-permute-start.9 = (f32[16,512]{1,0:T(8,128)S(1)}, f32[16,512]{1,0:T(8,128)S(1)}, u32[]{:S(2)}, u32[]{:S(2)}) collective-permute-start(f32[16,512]{1,0:T(8,128)S(1)} %get-tuple-element.52), channel_id=1, source_target_pairs={{0,1},{1,0},{2,3},{3,2},{4,5},{5,4},{6,7},{7,6},{8,9},{9,8},{10,11... | collective-permute-start | bytes 98312 | tf_op jit(solution)/shard_map/ppermute | solution.py:404
  32.5 5.6 %collective-permute-start.11 = (bf16[128,1024]{1,0:T(8,128)(2,1)S(1)}, bf16[128,1024]{1,0:T(8,128)(2,1)S(1)}, u32[]{:S(2)}, u32[]{:S(2)}) collective-permute-start(bf16[128,1024]{1,0:T(8,128)(2,1)S(1)} %get-tuple-element.56), channel_id=1, source_target_pairs={{0,8},{8,0},{16,24},{24,16},{1,9},{9,1},{17,25},{25,17},{2,10},{10... | collective-permute-start | bytes 786440 | tf_op jit(solution)/shard_map/ppermute | solution.py:480
  53.6 8.7 %collective-permute-start.15 = (bf16[384,1024]{1,0:T(8,128)(2,1)S(1)}, bf16[384,1024]{1,0:T(8,128)(2,1)S(1)}, u32[]{:S(2)}, u32[]{:S(2)}) collective-permute-start(bf16[384,1024]{1,0:T(8,128)(2,1)S(1)} %collective-permute-done.10.refs_0_.refs_6_), channel_id=1, source_target_pairs={{0,1},{1,0},{2,3},{3,2},{4,5},{5,4},{6,7},{7,6},{8,9},{9,8},{10,11... | collective-permute-start | bytes 2359304 | tf_op jit(solution)/shard_map/ppermute | solution.py:404
  54.4 7.9 %collective-permute-start.16 = (bf16[128,1024]{1,0:T(8,128)(2,1)S(1)}, bf16[128,1024]{1,0:T(8,128)(2,1)S(1)}, u32[]{:S(2)}, u32[]{:S(2)}) collective-permute-start(bf16[128,1024]{1,0:T(8,128)(2,1)S(1)} %collective-permute-done.11.refs_7_), channel_id=1, source_target_pairs={{0,1},{1,0},{2,3},{3,2},{4,5},{5,4},{6,7},{7,6},{8,9},{9,8},{10,11... | collective-permute-start | bytes 786440 | tf_op jit(solution)/shard_map/ppermute | solution.py:404
  54.5 5.0 %collective-permute-start.12 = (bf16[64,512]{1,0:T(8,128)(2,1)S(1)}, bf16[64,512]{1,0:T(8,128)(2,1)S(1)}, u32[]{:S(2)}, u32[]{:S(2)}) collective-permute-start(bf16[64,512]{1,0:T(8,128)(2,1)S(1)} %get-tuple-element.59), channel_id=1, source_target_pairs={{0,2},{1,3},{2,4},{3,5},{4,6},{5,7},{6,0},{7,1},{8,10},{9,11},{10,... | collective-permute-start | bytes 196616 | tf_op jit(solution)/shard_map/ppermute | solution.py:409
  54.5 7.8 %collective-permute-start.13 = (bf16[64,512]{1,0:T(8,128)(2,1)S(1)}, bf16[64,512]{1,0:T(8,128)(2,1)S(1)}, u32[]{:S(2)}, u32[]{:S(2)}) collective-permute-start(bf16[64,512]{1,0:T(8,128)(2,1)S(1)} %get-tuple-element.60), channel_id=1, source_target_pairs={{0,4},{1,5},{2,6},{3,7},{4,0},{5,1},{6,2},{7,3},{8,12},{9,13},{10,... | collective-permute-start | bytes 196616 | tf_op jit(solution)/shard_map/ppermute | solution.py:409
  57.5 4.9 %collective-permute-start.14 = (bf16[64,512]{1,0:T(8,128)(2,1)S(1)}, bf16[64,512]{1,0:T(8,128)(2,1)S(1)}, u32[]{:S(2)}, u32[]{:S(2)}) collective-permute-start(bf16[64,512]{1,0:T(8,128)(2,1)S(1)} %get-tuple-element.61), channel_id=1, source_target_pairs={{0,6},{1,7},{2,0},{3,1},{4,2},{5,3},{6,4},{7,5},{8,14},{9,15},{10,... | collective-permute-start | bytes 196616 | tf_op jit(solution)/shard_map/ppermute | solution.py:409
  63.9 16.1 %collective-permute-start.20 = (f32[2,2,64,512]{3,2,1,0:T(8,128)S(1)}, f32[2,2,64,512]{3,2,1,0:T(8,128)S(1)}, u32[]{:S(2)}, u32[]{:S(2)}) collective-permute-start(f32[2,2,64,512]{3,2,1,0:T(8,128)S(1)} %get-tuple-element.69), channel_id=1, source_target_pairs={{0,1},{1,0},{2,3},{3,2},{4,5},{5,4},{6,7},{7,6},{8,9},{9,8},{10,11... | collective-permute-start | bytes 1572872 | tf_op jit(solution)/shard_map/ppermute | solution.py:404
  65.3 4.3 %collective-permute-start.17 = (bf16[64,8,128]{2,1,0:T(8,128)(2,1)S(1)}, bf16[64,8,128]{2,1,0:T(8,128)(2,1)S(1)}, u32[]{:S(2)}, u32[]{:S(2)}) collective-permute-start(bf16[64,8,128]{2,1,0:T(8,128)(2,1)S(1)} %get-tuple-element.65), channel_id=1, source_target_pairs={{0,1},{1,0},{2,3},{3,2},{4,5},{5,4},{6,7},{7,6},{8,9},{9,8},{10,11... | collective-permute-start | bytes 393224 | tf_op jit(solution)/shard_map/ppermute | solution.py:404
  65.4 11.1 %collective-permute-start.18 = (bf16[64,8,128]{2,1,0:T(8,128)(2,1)S(1)}, bf16[64,8,128]{2,1,0:T(8,128)(2,1)S(1)}, u32[]{:S(2)}, u32[]{:S(2)}) collective-permute-start(bf16[64,8,128]{2,1,0:T(8,128)(2,1)S(1)} %get-tuple-element.66), channel_id=1, source_target_pairs={{0,4},{1,5},{2,6},{3,7},{4,0},{5,1},{6,2},{7,3},{8,12},{9,13},{10,... | collective-permute-start | bytes 393224 | tf_op jit(solution)/shard_map/ppermute | solution.py:409
  65.7 14.3 %collective-permute-start.19 = (bf16[64,8,128]{2,1,0:T(8,128)(2,1)S(1)}, bf16[64,8,128]{2,1,0:T(8,128)(2,1)S(1)}, u32[]{:S(2)}, u32[]{:S(2)}) collective-permute-start(bf16[64,8,128]{2,1,0:T(8,128)(2,1)S(1)} %get-tuple-element.67), channel_id=1, source_target_pairs={{0,5},{1,4},{2,7},{3,6},{4,1},{5,0},{6,3},{7,2},{8,13},{9,12},{10,... | collective-permute-start | bytes 393224 | tf_op jit(solution)/shard_map/ppermute | solution.py:508
  68.4 1.2 %collective-permute-start.21 = (f32[2,8,512]{2,1,0:T(8,128)S(1)}, f32[2,8,512]{2,1,0:T(8,128)S(1)}, u32[]{:S(2)}, u32[]{:S(2)}) collective-permute-start(f32[2,8,512]{2,1,0:T(8,128)S(1)} %get-tuple-element.71), channel_id=1, source_target_pairs={{0,1},{1,0},{2,3},{3,2},{4,5},{5,4},{6,7},{7,6},{8,9},{9,8},{10,11... | collective-permute-start | bytes 98312 | tf_op jit(solution)/shard_map/ppermute | solution.py:404
  (6 other events, 68.4 us)

commit v6 on v5

--- a/solution.py
+++ b/solution.py
@@ -343,10 +343,22 @@
                     away_ref[begin + 2 * tile + line] = away.astype(bf16)
 
 
+def own_kernel(place_ref, own_same, own_away, gained_same, gained_away, out_ref, cells_ref):
+    side = place_ref[3]
+    tiles = out_ref.shape[2] // LANES
+    rows = 2 * tiles
+    for away, (own, gained) in enumerate(((own_same, gained_same), (own_away, gained_away))):
+        cells_ref[...] = own[...].astype(f32).reshape(CORE * rows, LANES)
+        for row in range(2):
+            for tile in range(tiles):
+                lanes = slice(tile * LANES, (tile + 1) * LANES)
+                placed = cells_ref[pl.ds(row * tiles + tile, CORE, stride=rows), :]
+                out_ref[away * 2 + row, :, lanes] = gained[side, row, :, lanes] + placed
+
+
 def final_kernel(
     place_ref,
-    own_same,
-    own_away,
+    own_sums,
     far_same,
     far_away,
     gained_same,
@@ -362,20 +374,19 @@
     tiles = out_ref.shape[2] // LANES
     block_rows = out_ref.shape[1] // CORE
     rows = 2 * tiles
-    for away, (own, far, gained, fresh) in enumerate(
-        ((own_same, far_same, gained_same, fresh_same), (own_away, far_away, gained_away, fresh_away))
+    for away, (far, gained, fresh) in enumerate(
+        ((far_same, gained_same, fresh_same), (far_away, gained_away, fresh_away))
     ):
         of = half if away == 0 else 1 - half
         places = (block_rows // 2 - 1 + of, (block_rows - 1) * of)
-        for opposite, values in enumerate((own, far)):
-            channel = side if opposite == 0 else 1 - side
-            cells_ref[...] = values[...].astype(f32).reshape(CORE * rows, LANES)
-            for row in range(2):
-                for tile in range(tiles):
-                    lanes = slice(tile * LANES, (tile + 1) * LANES)
-                    placed = cells_ref[pl.ds(row * tiles + tile, CORE, stride=rows), :]
-                    at = pl.multiple_of(places[row] * CORE, CORE)
-                    out_ref[channel, pl.ds(at, CORE), lanes] = gained[channel, row, :, lanes] + placed
+        cells_ref[...] = far[...].astype(f32).reshape(CORE * rows, LANES)
+        for row in range(2):
+            at = pl.multiple_of(places[row] * CORE, CORE)
+            out_ref[side, pl.ds(at, CORE), :] = own_sums[away * 2 + row]
+            for tile in range(tiles):
+                lanes = slice(tile * LANES, (tile + 1) * LANES)
+                placed = cells_ref[pl.ds(row * tiles + tile, CORE, stride=rows), :]
+                out_ref[1 - side, pl.ds(at, CORE), lanes] = gained[1 - side, row, :, lanes] + placed
         for row in range(2):
             for column in range(2 * tiles):
                 at = (column % 2) * tiles + column // 2
@@ -509,10 +520,17 @@
     own_away = across(own_away)
     fresh_away = across(fresh_away)
     gained_away = across(after(gained_away, own_same))
+    (own_sums,) = call(
+        own_kernel,
+        [((4, CORE, width), f32)],
+        (place, own_same, own_away, gained_same, gained_away),
+        [pltpu.VMEM((CORE * 2 * tiles, LANES), f32)],
+        name="own",
+    )
     return call(
         final_kernel,
         [((2, height, width), f32), ((block_rows, 2 * tiles, NODES), f32)],
-        (place, own_same, own_away, far_same, far_away, gained_same, gained_away, fresh_same, fresh_away),
+        (place, own_sums, far_same, far_away, gained_same, gained_away, fresh_same, fresh_away),
         [pltpu.VMEM((CORE * 2 * tiles, LANES), f32)],
         4,
         2.0,

time: 81.9 us -> 81.8 us (level)
    pallas_call x10 -> x11, Pallas kernels: 15.5 us -> 16.1 us  [call(): pl.pallas_call(kernel, out_shape=tuple((jax.ShapeDtypeStruct(*out) for ou...]
  transfers between devices with their start and end apart: 22 -> 22, of which waited for: 12 -> 12; matrix products, arithmetic and copies ran while one was open for 0% -> 0% of each run, Pallas kernels for 13% -> 14%
where the time goes in v6:
time: 81.8 us; the launch traced here: 81.7 us
  waiting for transfers between devices  38 us (46%)
  starting transfers between devices  24.7 us (30%)
  Pallas kernels  16.7 us (20%)
  local copies, waits for them, and re-layouts  1.35 us (2%)
    ppermute x7, waiting for transfers between devices, along(): lax.ppermute(values, 'col', [(i, (i + 2 * ahead) % sections) for i in ran...  24.7 us
    pallas_call x11, Pallas kernels, call(): pl.pallas_call(kernel, out_shape=tuple((jax.ShapeDtypeStruct(*out) for ou...  16.1 us
    ppermute x7, starting transfers between devices, along(): lax.ppermute(values, 'col', [(i, (i + 2 * ahead) % sections) for i in ran...  8.86 us
    ppermute x10, starting transfers between devices, across(): return lax.ppermute(values, 'col', [(i, i ^ 1) for i in range(sections)])  7.58 us
    ppermute x1, waiting for transfers between devices, local(): lax.ppermute(quarter, 'row', [(i, i ^ 1) for i in range(bands)])  4.36 us
    ppermute x1, waiting for transfers between devices, local(): far_away = lax.ppermute(far_away, 'col', pattern)  3.39 us
    ppermute x1, starting transfers between devices, local(): edges = lax.ppermute(edges, 'col', pattern)  2.75 us
    ppermute x1, starting transfers between devices, local(): far_away = lax.ppermute(far_away, 'col', pattern)  2.71 us
  transfers between devices with their start and end apart: 22, of which 12 were waited for; matrix products, arithmetic and copies ran while one was open for 0% of the time, Pallas kernels for 14%

profile of v6, /device:TPU:1, one launch (start us, length us, event | category | flops | bytes accessed | tf_op | source)
XLA Modules:
  0.0 81.7 jit_solution(12626383346079927789)
XLA Ops:
  0.8 1.2 %copy-done = f32[2,256,512]{2,1,0:T(8,128)S(1)} copy-done((f32[2,256,512]{2,1,0:T(8,128)S(1)}, f32[2,256,512]{2,1,0:T(8,128)}, u32[]{:S(2)}) %copy-start) | copy-done | bytes 1048600
  2.8 2.8 %collective-permute-start.1 = (f32[2,8,128]{2,1,0:T(8,128)S(1)}, f32[2,8,128]{2,1,0:T(8,128)S(1)}, u32[]{:S(2)}, u32[]{:S(2)}) collective-permute-start(f32[2,8,128]{2,1,0:T(8,128)S(1)} %edges.1), channel_id=1, source_target_pairs={{0,7},{1,2},{2,1},{3,4},{4,3},{5,6},{6,5},{7,0},{8,15},{9,10},{10,... | collective-permute-start | bytes 24584 | tf_op jit(solution)/shard_map/ppermute | solution.py:425
  5.6 1.3 %collective-permute-done.1.outer_ref = f32[2,8,128]{2,1,0:T(8,128)S(1)} collective-permute-done((f32[2,8,128]{2,1,0:T(8,128)S(1)}, f32[2,8,128]{2,1,0:T(8,128)S(1)}, u32[]{:S(2)}, u32[]{:S(2)}) %collective-permute-start.1) | collective-permute-done | bytes 8224 | tf_op jit(solution)/shard_map/ppermute | solution.py:425
  6.9 2.5 %collective-permute-start.2 = (f32[2,8,128]{2,1,0:T(8,128)S(1)}, f32[2,8,128]{2,1,0:T(8,128)S(1)}, u32[]{:S(2)}, u32[]{:S(2)}) collective-permute-start(f32[2,8,128]{2,1,0:T(8,128)S(1)} %collective-permute-done.1.outer_ref), channel_id=1, source_target_pairs={{0,1},{1,0},{2,3},{3,2},{4,5},{5,4},{6,7},{7,6},{8,9},{9,8},{10,11... | collective-permute-start | bytes 24584 | tf_op jit(solution)/shard_map/ppermute | solution.py:415
  12.3 1.5 %collective-permute-start.3 = (f32[2,8,1152]{2,1,0:T(8,128)S(1)}, f32[2,8,1152]{2,1,0:T(8,128)S(1)}, u32[]{:S(2)}, u32[]{:S(2)}) collective-permute-start(f32[2,8,1152]{2,1,0:T(8,128)S(1)} %get-tuple-element.39), channel_id=1, source_target_pairs={{0,25},{1,8},{2,27},{3,10},{4,29},{5,12},{6,31},{7,14},{8,1},{9,16... | collective-permute-start | bytes 221192 | tf_op jit(solution)/shard_map/ppermute | solution.py:438
  13.8 3.1 %inner_model.1 = (bf16[4,8,72,128]{3,2,1,0:T(8,128)(2,1)S(1)}, f32[2,64,1024]{2,1,0:T(8,128)S(1)}) custom-call(s32[5]{0:T(128)S(1)} %stack.23.place_ref, f32[2,256,512]{2,1,0:T(8,128)S(1)} %copy-done.1, f32[2,256,512]{2,1,0:T(8,128)S(1)} %collective-permute-done.other_ref, f32[2,256,128]{2,1,0:T(8,128)S(1)} %get-tuple-element.38.side_ref), custom_call_target="tpu_custom_call" | custom-call | bytes 12177000 | tf_op jit(solution)/shard_map/inner_model/pallas_call | solution.py:31
  17.0 3.3 %outer_model.1 = (bf16[1,8,136,128]{3,2,1,0:T(8,128)(2,1)S(1)}, bf16[1,8,136,128]{3,2,1,0:T(8,128)(2,1)S(1)}, bf16[1,8,136,128]{3,2,1,0:T(8,128)(2,1)S(1)}, bf16...) custom-call(s32[5]{0:T(128)S(1)} %stack.23.place_ref, f32[2,256,512]{2,1,0:T(8,128)S(1)} %copy-done.1, ...), custom_call_target="tpu_custom_call" | custom-call | bytes 12177000 | tf_op jit(solution)/shard_map/outer_model/pallas_call | solution.py:31
  20.2 3.5 %collective-permute-start.6 = (bf16[1,8,136,128]{3,2,1,0:T(8,128)(2,1)S(1)}, bf16[1,8,136,128]{3,2,1,0:T(8,128)(2,1)S(1)}, u32[]{:S(2)}, u32[]{:S(2)}) collective-permute-start(bf16[1,8,136,128]{3,2,1,0:T(8,128)(2,1)S(1)} %get-tuple-element.46), channel_id=1, source_target_pairs={{0,6},{1,7},{2,0},{3,1},{4,2},{5,3},{6,4},{7,5},{8,14},{9,15},{10,... | collective-permute-start | bytes 835592 | tf_op jit(solution)/shard_map/ppermute | solution.py:420
  24.2 1.4 %collective-permute-start.8 = (bf16[1,8,136,128]{3,2,1,0:T(8,128)(2,1)S(1)}, bf16[1,8,136,128]{3,2,1,0:T(8,128)(2,1)S(1)}, u32[]{:S(2)}, u32[]{:S(2)}) collective-permute-start(bf16[1,8,136,128]{3,2,1,0:T(8,128)(2,1)S(1)} %get-tuple-element.48), channel_id=1, source_target_pairs={{0,2},{1,3},{2,4},{3,5},{4,6},{5,7},{6,0},{7,1},{8,10},{9,11},{10,... | collective-permute-start | bytes 835592 | tf_op jit(solution)/shard_map/ppermute | solution.py:420
  26.2 1.9 %collective-permute-start.9 = (f32[16,512]{1,0:T(8,128)S(1)}, f32[16,512]{1,0:T(8,128)S(1)}, u32[]{:S(2)}, u32[]{:S(2)}) collective-permute-start(f32[16,512]{1,0:T(8,128)S(1)} %get-tuple-element.52), channel_id=1, source_target_pairs={{0,1},{1,0},{2,3},{3,2},{4,5},{5,4},{6,7},{7,6},{8,9},{9,8},{10,11... | collective-permute-start | bytes 98312 | tf_op jit(solution)/shard_map/ppermute | solution.py:415
  29.7 2.1 %collective-permute-done.10.refs_0_.refs_6_ = bf16[384,1024]{1,0:T(8,128)(2,1)S(1)} collective-permute-done((bf16[384,1024]{1,0:T(8,128)(2,1)S(1)}, bf16[384,1024]{1,0:T(8,128)(2,1)S(1)}, u32[]{:S(2)}, u32[]{:S(2)}) %collective-permute-start.10) | collective-permute-done | bytes 786464 | tf_op jit(solution)/shard_map/ppermute | solution.py:444
  33.7 4.4 %collective-permute-done.11.refs_7_ = bf16[128,1024]{1,0:T(8,128)(2,1)S(1)} collective-permute-done((bf16[128,1024]{1,0:T(8,128)(2,1)S(1)}, bf16[128,1024]{1,0:T(8,128)(2,1)S(1)}, u32[]{:S(2)}, u32[]{:S(2)}) %collective-permute-start.11) | collective-permute-done | bytes 262176 | tf_op jit(solution)/shard_map/ppermute | solution.py:491
  38.1 4.8 %collective-permute-done.6.refs_1_ = bf16[1,8,136,128]{3,2,1,0:T(8,128)(2,1)S(1)} collective-permute-done((bf16[1,8,136,128]{3,2,1,0:T(8,128)(2,1)S(1)}, bf16[1,8,136,128]{3,2,1,0:T(8,128)(2,1)S(1)}, u32[]{:S(2)}, u32[]{:S(2)}) %collective-permute-start.6) | collective-permute-done | bytes 278560 | tf_op jit(solution)/shard_map/ppermute | solution.py:420
  42.9 8.4 %collective-permute-done.8.refs_3_ = bf16[1,8,136,128]{3,2,1,0:T(8,128)(2,1)S(1)} collective-permute-done((bf16[1,8,136,128]{3,2,1,0:T(8,128)(2,1)S(1)}, bf16[1,8,136,128]{3,2,1,0:T(8,128)(2,1)S(1)}, u32[]{:S(2)}, u32[]{:S(2)}) %collective-permute-start.8) | collective-permute-done | bytes 278560 | tf_op jit(solution)/shard_map/ppermute | solution.py:420
  51.3 2.3 %drive.1 = (bf16[64,512]{1,0:T(8,128)(2,1)S(1)}, bf16[64,512]{1,0:T(8,128)(2,1)S(1)}, bf16[64,512]{1,0:T(8,128)(2,1)S(1)}, bf16[64,512]{1,0:T(8,128)(2,1)S(1)}) custom-call(s32[5]{0:T(128)S(1)} %stack.23.place_ref, bf16[1,8,136,128]{3,2,1,0:T(8,128)(2,1)S(1)} %get-tuple-element.45.refs_0_, bf16[1,8,136,128]{3,2,1,0:T(8,128)(2,1)S(1)} %collective-permute-done.6.refs_1_, ...), custom_call_target="tpu_custom_call" | custom-call | bytes 14760000 | tf_op jit(solution)/shard_map/drive/pallas_call | solution.py:31
  54.5 2.9 %collective-permute-start.13 = (bf16[64,512]{1,0:T(8,128)(2,1)S(1)}, bf16[64,512]{1,0:T(8,128)(2,1)S(1)}, u32[]{:S(2)}, u32[]{:S(2)}) collective-permute-start(bf16[64,512]{1,0:T(8,128)(2,1)S(1)} %get-tuple-element.60), channel_id=1, source_target_pairs={{0,4},{1,5},{2,6},{3,7},{4,0},{5,1},{6,2},{7,3},{8,12},{9,13},{10,... | collective-permute-start | bytes 196616 | tf_op jit(solution)/shard_map/ppermute | solution.py:420
  57.8 1.7 %collective-permute-done.12.refs_1_ = bf16[64,512]{1,0:T(8,128)(2,1)S(1)} collective-permute-done((bf16[64,512]{1,0:T(8,128)(2,1)S(1)}, bf16[64,512]{1,0:T(8,128)(2,1)S(1)}, u32[]{:S(2)}, u32[]{:S(2)}) %collective-permute-start.12) | collective-permute-done | bytes 65568 | tf_op jit(solution)/shard_map/ppermute | solution.py:420
  59.5 2.7 %collective-permute-done.13.refs_2_ = bf16[64,512]{1,0:T(8,128)(2,1)S(1)} collective-permute-done((bf16[64,512]{1,0:T(8,128)(2,1)S(1)}, bf16[64,512]{1,0:T(8,128)(2,1)S(1)}, u32[]{:S(2)}, u32[]{:S(2)}) %collective-permute-start.13) | collective-permute-done | bytes 65568 | tf_op jit(solution)/shard_map/ppermute | solution.py:420
  62.2 1.5 %readout.1 = (f32[2,8,512]{2,1,0:T(8,128)S(1)}, f32[2,8,512]{2,1,0:T(8,128)S(1)}, bf16[64,8,128]{2,1,0:T(8,128)(2,1)S(1)}, bf16[64,8,128]{2,1,0:T(8,128)(2,1)S(1...) custom-call(s32[5]{0:T(128)S(1)} %stack.23.place_ref, ...), custom_call_target="tpu_custom_call" | custom-call | bytes 9225000 | tf_op jit(solution)/shard_map/readout/pallas_call | solution.py:31
  63.8 1.5 %collective-permute-start.18 = (f32[2,2,64,512]{3,2,1,0:T(8,128)S(1)}, f32[2,2,64,512]{3,2,1,0:T(8,128)S(1)}, u32[]{:S(2)}, u32[]{:S(2)}) collective-permute-start(f32[2,2,64,512]{3,2,1,0:T(8,128)S(1)} %get-tuple-element.67), channel_id=1, source_target_pairs={{0,1},{1,0},{2,3},{3,2},{4,5},{5,4},{6,7},{7,6},{8,9},{9,8},{10,11... | collective-permute-start | bytes 1572872 | tf_op jit(solution)/shard_map/ppermute | solution.py:415
  65.6 2.7 %collective-permute-start.20 = (bf16[64,8,128]{2,1,0:T(8,128)(2,1)S(1)}, bf16[64,8,128]{2,1,0:T(8,128)(2,1)S(1)}, u32[]{:S(2)}, u32[]{:S(2)}) collective-permute-start(bf16[64,8,128]{2,1,0:T(8,128)(2,1)S(1)} %get-tuple-element.69), channel_id=1, source_target_pairs={{0,5},{1,4},{2,7},{3,6},{4,1},{5,0},{6,3},{7,2},{8,13},{9,12},{10,... | collective-permute-start | bytes 393224 | tf_op jit(solution)/shard_map/ppermute | solution.py:519
  69.6 7.0 %collective-permute-done.19.far_same = bf16[64,8,128]{2,1,0:T(8,128)(2,1)S(1)} collective-permute-done((bf16[64,8,128]{2,1,0:T(8,128)(2,1)S(1)}, bf16[64,8,128]{2,1,0:T(8,128)(2,1)S(1)}, u32[]{:S(2)}, u32[]{:S(2)}) %collective-permute-start.19) | collective-permute-done | bytes 131104 | tf_op jit(solution)/shard_map/ppermute | solution.py:420
  76.6 3.4 %collective-permute-done.20.far_away = bf16[64,8,128]{2,1,0:T(8,128)(2,1)S(1)} collective-permute-done((bf16[64,8,128]{2,1,0:T(8,128)(2,1)S(1)}, bf16[64,8,128]{2,1,0:T(8,128)(2,1)S(1)}, u32[]{:S(2)}, u32[]{:S(2)}) %collective-permute-start.20) | collective-permute-done | bytes 131104 | tf_op jit(solution)/shard_map/ppermute | solution.py:519
  79.9 1.7 %final.1 = (f32[2,256,512]{2,1,0:T(8,128)}, f32[4,8,512]{2,1,0:T(8,128)}) custom-call(s32[5]{0:T(128)S(1)} %stack.23.place_ref, f32[4,64,512]{2,1,0:T(8,128)S(1)} %own.1.own_sums, bf16[64,8,128]{2,1,0:T(8,128)(2,1)S(1)} %collective-permute-done.19.far_same, bf16[64,8,128]{2,1,0:T(8,128)(2,1)S(1)} %collective-permute-done.20.far_away, ...), custom_call_target="tpu_custom_call" | custom-call | bytes 7380000 | tf_op jit(solution)/shard_map/final/pallas_call | solution.py:31
  (50 shorter events, 11.0 us)
Async XLA Ops:
  0.6 6.3 %collective-permute-start = (f32[2,256,512]{2,1,0:T(8,128)}, f32[2,256,512]{2,1,0:T(8,128)S(1)}, u32[]{:S(2)}, u32[]{:S(2)}) collective-permute-start(f32[2,256,512]{2,1,0:T(8,128)} %field_ref.7), channel_id=1, source_target_pairs={{0,1},{1,0},{2,3},{3,2},{4,5},{5,4},{6,7},{7,6},{8,9},{9,8},{10,11... | collective-permute-start | bytes 3145736 | tf_op jit(solution)/shard_map/ppermute | solution.py:415
  2.8 4.1 %collective-permute-start.1 = (f32[2,8,128]{2,1,0:T(8,128)S(1)}, f32[2,8,128]{2,1,0:T(8,128)S(1)}, u32[]{:S(2)}, u32[]{:S(2)}) collective-permute-start(f32[2,8,128]{2,1,0:T(8,128)S(1)} %edges.1), channel_id=1, source_target_pairs={{0,7},{1,2},{2,1},{3,4},{4,3},{5,6},{6,5},{7,0},{8,15},{9,10},{10,... | collective-permute-start | bytes 24584 | tf_op jit(solution)/shard_map/ppermute | solution.py:425
  6.9 3.3 %collective-permute-start.2 = (f32[2,8,128]{2,1,0:T(8,128)S(1)}, f32[2,8,128]{2,1,0:T(8,128)S(1)}, u32[]{:S(2)}, u32[]{:S(2)}) collective-permute-start(f32[2,8,128]{2,1,0:T(8,128)S(1)} %collective-permute-done.1.outer_ref), channel_id=1, source_target_pairs={{0,1},{1,0},{2,3},{3,2},{4,5},{5,4},{6,7},{7,6},{8,9},{9,8},{10,11... | collective-permute-start | bytes 24584 | tf_op jit(solution)/shard_map/ppermute | solution.py:415
  10.2 6.7 %collective-permute-start.4 = (bf16[2592,512]{1,0:T(8,128)(2,1)}, bf16[2592,512]{1,0:T(8,128)(2,1)S(1)}, u32[]{:S(2)}, u32[]{:S(2)}) collective-permute-start(bf16[2592,512]{1,0:T(8,128)(2,1)} %refs_4_.1), channel_id=1, source_target_pairs={{0,1},{1,0},{2,3},{3,2},{4,5},{5,4},{6,7},{7,6},{8,9},{9,8},{10,11... | collective-permute-start | bytes 7962632 | tf_op jit(solution)/shard_map/ppermute | solution.py:415
  10.6 6.3 %collective-permute-start.5 = (bf16[512,1024]{1,0:T(8,128)(2,1)}, bf16[512,1024]{1,0:T(8,128)(2,1)S(1)}, u32[]{:S(2)}, u32[]{:S(2)}) collective-permute-start(bf16[512,1024]{1,0:T(8,128)(2,1)} %refs_4_.2), channel_id=1, source_target_pairs={{0,1},{1,0},{2,3},{3,2},{4,5},{5,4},{6,7},{7,6},{8,9},{9,8},{10,11... | collective-permute-start | bytes 3145736 | tf_op jit(solution)/shard_map/ppermute | solution.py:415
  12.1 19.7 %collective-permute-start.10 = (bf16[384,1024]{1,0:T(8,128)(2,1)S(1)}, bf16[384,1024]{1,0:T(8,128)(2,1)S(1)}, u32[]{:S(2)}, u32[]{:S(2)}) collective-permute-start(bf16[384,1024]{1,0:T(8,128)(2,1)S(1)} %part.1), channel_id=1, source_target_pairs={{0,2},{1,3},{2,0},{3,1},{4,6},{5,7},{6,4},{7,5},{8,10},{9,11},{10,... | collective-permute-start | bytes 2359304 | tf_op jit(solution)/shard_map/ppermute | solution.py:444
  12.2 16.7 %copy-start.4 = (bf16[512,512]{1,0:T(8,128)(2,1)S(1)}, bf16[512,512]{1,0:T(8,128)(2,1)}, u32[]{:S(2)}) copy-start(bf16[512,512]{1,0:T(8,128)(2,1)} %weight_ref.1) | copy-start | bytes 1572868
  12.3 4.7 %collective-permute-start.3 = (f32[2,8,1152]{2,1,0:T(8,128)S(1)}, f32[2,8,1152]{2,1,0:T(8,128)S(1)}, u32[]{:S(2)}, u32[]{:S(2)}) collective-permute-start(f32[2,8,1152]{2,1,0:T(8,128)S(1)} %get-tuple-element.39), channel_id=1, source_target_pairs={{0,25},{1,8},{2,27},{3,10},{4,29},{5,12},{6,31},{7,14},{8,1},{9,16... | collective-permute-start | bytes 221192 | tf_op jit(solution)/shard_map/ppermute | solution.py:438
  16.9 34.4 %copy-start.3 = (bf16[2592,512]{1,0:T(8,128)(2,1)S(1)}, bf16[2592,512]{1,0:T(8,128)(2,1)}, u32[]{:S(2)}) copy-start(bf16[2592,512]{1,0:T(8,128)(2,1)} %refs_4_.1) | copy-start | bytes 7962628
  20.2 22.7 %collective-permute-start.6 = (bf16[1,8,136,128]{3,2,1,0:T(8,128)(2,1)S(1)}, bf16[1,8,136,128]{3,2,1,0:T(8,128)(2,1)S(1)}, u32[]{:S(2)}, u32[]{:S(2)}) collective-permute-start(bf16[1,8,136,128]{3,2,1,0:T(8,128)(2,1)S(1)} %get-tuple-element.46), channel_id=1, source_target_pairs={{0,6},{1,7},{2,0},{3,1},{4,2},{5,3},{6,4},{7,5},{8,14},{9,15},{10,... | collective-permute-start | bytes 835592 | tf_op jit(solution)/shard_map/ppermute | solution.py:420
  23.8 19.2 %collective-permute-start.7 = (bf16[1,8,136,128]{3,2,1,0:T(8,128)(2,1)S(1)}, bf16[1,8,136,128]{3,2,1,0:T(8,128)(2,1)S(1)}, u32[]{:S(2)}, u32[]{:S(2)}) collective-permute-start(bf16[1,8,136,128]{3,2,1,0:T(8,128)(2,1)S(1)} %get-tuple-element.47), channel_id=1, source_target_pairs={{0,4},{1,5},{2,6},{3,7},{4,0},{5,1},{6,2},{7,3},{8,12},{9,13},{10,... | collective-permute-start | bytes 835592 | tf_op jit(solution)/shard_map/ppermute | solution.py:420
  24.2 27.1 %collective-permute-start.8 = (bf16[1,8,136,128]{3,2,1,0:T(8,128)(2,1)S(1)}, bf16[1,8,136,128]{3,2,1,0:T(8,128)(2,1)S(1)}, u32[]{:S(2)}, u32[]{:S(2)}) collective-permute-start(bf16[1,8,136,128]{3,2,1,0:T(8,128)(2,1)S(1)} %get-tuple-element.48), channel_id=1, source_target_pairs={{0,2},{1,3},{2,4},{3,5},{4,6},{5,7},{6,0},{7,1},{8,10},{9,11},{10,... | collective-permute-start | bytes 835592 | tf_op jit(solution)/shard_map/ppermute | solution.py:420
  26.2 2.8 %collective-permute-start.9 = (f32[16,512]{1,0:T(8,128)S(1)}, f32[16,512]{1,0:T(8,128)S(1)}, u32[]{:S(2)}, u32[]{:S(2)}) collective-permute-start(f32[16,512]{1,0:T(8,128)S(1)} %get-tuple-element.52), channel_id=1, source_target_pairs={{0,1},{1,0},{2,3},{3,2},{4,5},{5,4},{6,7},{7,6},{8,9},{9,8},{10,11... | collective-permute-start | bytes 98312 | tf_op jit(solution)/shard_map/ppermute | solution.py:415
  32.5 5.6 %collective-permute-start.11 = (bf16[128,1024]{1,0:T(8,128)(2,1)S(1)}, bf16[128,1024]{1,0:T(8,128)(2,1)S(1)}, u32[]{:S(2)}, u32[]{:S(2)}) collective-permute-start(bf16[128,1024]{1,0:T(8,128)(2,1)S(1)} %get-tuple-element.56), channel_id=1, source_target_pairs={{0,8},{8,0},{16,24},{24,16},{1,9},{9,1},{17,25},{25,17},{2,10},{10... | collective-permute-start | bytes 786440 | tf_op jit(solution)/shard_map/ppermute | solution.py:491
  53.6 8.6 %collective-permute-start.15 = (bf16[384,1024]{1,0:T(8,128)(2,1)S(1)}, bf16[384,1024]{1,0:T(8,128)(2,1)S(1)}, u32[]{:S(2)}, u32[]{:S(2)}) collective-permute-start(bf16[384,1024]{1,0:T(8,128)(2,1)S(1)} %collective-permute-done.10.refs_0_.refs_6_), channel_id=1, source_target_pairs={{0,1},{1,0},{2,3},{3,2},{4,5},{5,4},{6,7},{7,6},{8,9},{9,8},{10,11... | collective-permute-start | bytes 2359304 | tf_op jit(solution)/shard_map/ppermute | solution.py:415
  54.4 7.8 %collective-permute-start.16 = (bf16[128,1024]{1,0:T(8,128)(2,1)S(1)}, bf16[128,1024]{1,0:T(8,128)(2,1)S(1)}, u32[]{:S(2)}, u32[]{:S(2)}) collective-permute-start(bf16[128,1024]{1,0:T(8,128)(2,1)S(1)} %collective-permute-done.11.refs_7_), channel_id=1, source_target_pairs={{0,1},{1,0},{2,3},{3,2},{4,5},{5,4},{6,7},{7,6},{8,9},{9,8},{10,11... | collective-permute-start | bytes 786440 | tf_op jit(solution)/shard_map/ppermute | solution.py:415
  54.5 5.0 %collective-permute-start.12 = (bf16[64,512]{1,0:T(8,128)(2,1)S(1)}, bf16[64,512]{1,0:T(8,128)(2,1)S(1)}, u32[]{:S(2)}, u32[]{:S(2)}) collective-permute-start(bf16[64,512]{1,0:T(8,128)(2,1)S(1)} %get-tuple-element.59), channel_id=1, source_target_pairs={{0,2},{1,3},{2,4},{3,5},{4,6},{5,7},{6,0},{7,1},{8,10},{9,11},{10,... | collective-permute-start | bytes 196616 | tf_op jit(solution)/shard_map/ppermute | solution.py:420
  54.5 7.7 %collective-permute-start.13 = (bf16[64,512]{1,0:T(8,128)(2,1)S(1)}, bf16[64,512]{1,0:T(8,128)(2,1)S(1)}, u32[]{:S(2)}, u32[]{:S(2)}) collective-permute-start(bf16[64,512]{1,0:T(8,128)(2,1)S(1)} %get-tuple-element.60), channel_id=1, source_target_pairs={{0,4},{1,5},{2,6},{3,7},{4,0},{5,1},{6,2},{7,3},{8,12},{9,13},{10,... | collective-permute-start | bytes 196616 | tf_op jit(solution)/shard_map/ppermute | solution.py:420
  57.4 4.8 %collective-permute-start.14 = (bf16[64,512]{1,0:T(8,128)(2,1)S(1)}, bf16[64,512]{1,0:T(8,128)(2,1)S(1)}, u32[]{:S(2)}, u32[]{:S(2)}) collective-permute-start(bf16[64,512]{1,0:T(8,128)(2,1)S(1)} %get-tuple-element.61), channel_id=1, source_target_pairs={{0,6},{1,7},{2,0},{3,1},{4,2},{5,3},{6,4},{7,5},{8,14},{9,15},{10,... | collective-permute-start | bytes 196616 | tf_op jit(solution)/shard_map/ppermute | solution.py:420
  63.8 4.6 %collective-permute-start.18 = (f32[2,2,64,512]{3,2,1,0:T(8,128)S(1)}, f32[2,2,64,512]{3,2,1,0:T(8,128)S(1)}, u32[]{:S(2)}, u32[]{:S(2)}) collective-permute-start(f32[2,2,64,512]{3,2,1,0:T(8,128)S(1)} %get-tuple-element.67), channel_id=1, source_target_pairs={{0,1},{1,0},{2,3},{3,2},{4,5},{5,4},{6,7},{7,6},{8,9},{9,8},{10,11... | collective-permute-start | bytes 1572872 | tf_op jit(solution)/shard_map/ppermute | solution.py:415
  65.3 3.0 %collective-permute-start.17 = (bf16[64,8,128]{2,1,0:T(8,128)(2,1)S(1)}, bf16[64,8,128]{2,1,0:T(8,128)(2,1)S(1)}, u32[]{:S(2)}, u32[]{:S(2)}) collective-permute-start(bf16[64,8,128]{2,1,0:T(8,128)(2,1)S(1)} %get-tuple-element.65), channel_id=1, source_target_pairs={{0,1},{1,0},{2,3},{3,2},{4,5},{5,4},{6,7},{7,6},{8,9},{9,8},{10,11... | collective-permute-start | bytes 393224 | tf_op jit(solution)/shard_map/ppermute | solution.py:415
  65.4 11.2 %collective-permute-start.19 = (bf16[64,8,128]{2,1,0:T(8,128)(2,1)S(1)}, bf16[64,8,128]{2,1,0:T(8,128)(2,1)S(1)}, u32[]{:S(2)}, u32[]{:S(2)}) collective-permute-start(bf16[64,8,128]{2,1,0:T(8,128)(2,1)S(1)} %get-tuple-element.68), channel_id=1, source_target_pairs={{0,4},{1,5},{2,6},{3,7},{4,0},{5,1},{6,2},{7,3},{8,12},{9,13},{10,... | collective-permute-start | bytes 393224 | tf_op jit(solution)/shard_map/ppermute | solution.py:420
  65.6 14.3 %collective-permute-start.20 = (bf16[64,8,128]{2,1,0:T(8,128)(2,1)S(1)}, bf16[64,8,128]{2,1,0:T(8,128)(2,1)S(1)}, u32[]{:S(2)}, u32[]{:S(2)}) collective-permute-start(bf16[64,8,128]{2,1,0:T(8,128)(2,1)S(1)} %get-tuple-element.69), channel_id=1, source_target_pairs={{0,5},{1,4},{2,7},{3,6},{4,1},{5,0},{6,3},{7,2},{8,13},{9,12},{10,... | collective-permute-start | bytes 393224 | tf_op jit(solution)/shard_map/ppermute | solution.py:519
  68.4 1.2 %collective-permute-start.21 = (f32[2,8,512]{2,1,0:T(8,128)S(1)}, f32[2,8,512]{2,1,0:T(8,128)S(1)}, u32[]{:S(2)}, u32[]{:S(2)}) collective-permute-start(f32[2,8,512]{2,1,0:T(8,128)S(1)} %get-tuple-element.71), channel_id=1, source_target_pairs={{0,1},{1,0},{2,3},{3,2},{4,5},{5,4},{6,7},{7,6},{8,9},{9,8},{10,11... | collective-permute-start | bytes 98312 | tf_op jit(solution)/shard_map/ppermute | solution.py:415
  (6 other events, 68.4 us)
